TPU v7x, 128 devices: a whole 4x4x4 slice. The times are simulated.
128 devices in a mesh: view: 4 (over x_hi, core), col: 32 (over y, z, x_lo).
Axes of the slice: x: 4 (x_hi: 2, x_lo: 2; x = x_hi * 2 + x_lo), y: 4, z: 4, core: 2. Of those that a mesh axis runs over, the one named last changes fastest.
Arguments:
- views: bfloat16 [64, 1024, 2048], P('view', 'col'), may hold values from 0.099609375 to 1
- phases: int32 [64, 64], replicated, may hold values from 0 to 255
- kernel_phase: float32 [65536], replicated, may hold values from -3.140625 to 3.140625
Outputs:
- propagated_re: float32 [2048, 65536], P(('view', 'col'))
- propagated_im: float32 [2048, 65536], P(('view', 'col'))
All inputs are finite; a program needn't handle non-finite values.
Results may differ from a plain program's by a relative error of at most 0.0057.
Values may be sent and summed in bfloat16 or wider, within the bound.
No kernel may reach another device: no remote copies, remote signals or barrier semaphores. Data moves between devices by JAX's collectives and lax.ppermute only.
A program may use at most 128 MiB of HBM per device.

v0:
```python
import functools
import math

import jax
import jax.numpy as jnp
import numpy as np
from jax import lax
from jax.experimental import pallas as pl
from jax.experimental.pallas import tpu as pltpu
from jax.sharding import Mesh
from jax.sharding import PartitionSpec as P

PHASES = 256
DIRS = 64
SIDE = 256
VIEW = ("xh", "co")
COL = ("y", "zh", "zl", "xl")
HOGEL_GROUP = ("xh", "co", "y", "zh")
SQUARE = ("zl", "xl")
VMEM_BYTES = 40 * 1024 * 1024


def direction_table(length):
    positions = jnp.arange(length, dtype=jnp.int32)
    angles = (positions[:, None] * positions[None, :] % length).astype(jnp.float32) * (
        2.0 * math.pi / length
    )
    factor = 1.0 / math.sqrt(length)
    return (
        (jnp.cos(angles) * factor).astype(jnp.bfloat16),
        (jnp.sin(angles) * factor).astype(jnp.bfloat16),
    )


def numpy_turns(first, second, modulus):
    angles = (np.outer(first, second) % modulus) * (2.0 * np.pi / modulus)
    return np.cos(angles), np.sin(angles)


def params(steps):
    return pltpu.CompilerParams(
        dimension_semantics=("arbitrary",) * steps, vmem_limit_bytes=VMEM_BYTES
    )


def regroup_kernel(views_ref, out_ref, wide_ref):
    dirs, cols, lanes = views_ref.shape
    low_half = lax.broadcasted_iota(jnp.int32, (dirs, 128), 1) < 64
    for pair in range(lanes // 128):
        block = views_ref[:, :, 128 * pair : 128 * (pair + 1)].astype(jnp.float32)
        wide_ref[pair] = block.reshape(dirs * cols, 128)
        for col in range(0, cols, 2):
            even = wide_ref[pair, pl.ds(col, dirs, stride=cols), :]
            odd = wide_ref[pair, pl.ds(col + 1, dirs, stride=cols), :]
            first = jnp.where(low_half, even, pltpu.roll(odd, 64, 1))
            second = jnp.where(low_half, pltpu.roll(even, 64, 1), odd)
            place = slice(64 * col, 64 * col + 128)
            out_ref[2 * pair, :, place] = first.astype(jnp.bfloat16)
            out_ref[2 * pair + 1, :, place] = second.astype(jnp.bfloat16)


def regroup(views, steps=4):
    dirs, cols, merged = views.shape
    lanes = merged // steps
    return pl.pallas_call(
        regroup_kernel,
        grid=(steps,),
        in_specs=[pl.BlockSpec((dirs, cols, lanes), lambda i: (0, 0, i))],
        out_specs=pl.BlockSpec((lanes // 64, dirs, cols * 64), lambda i: (i, 0, 0)),
        out_shape=jax.ShapeDtypeStruct((merged // 64, dirs, cols * 64), jnp.bfloat16),
        scratch_shapes=[pltpu.VMEM((lanes // 128, dirs * cols, 128), jnp.float32)],
        compiler_params=params(1),
        name="regroup",
    )(views)


def field_kernel(rays_ref, cos_ref, sin_ref, inner_ref, outer_ref, *rest):
    out_refs, wave_ref, wide_ref = rest[:4], rest[4], rest[5]
    rays = rays_ref[...].reshape(DIRS, 32 * DIRS)
    phase_cos = cos_ref[...]
    phase_sin = sin_ref[...]
    for tile in range(16):
        amplitude = rays[:, 128 * tile : 128 * (tile + 1)].astype(jnp.float32)
        rows = slice(DIRS * tile, DIRS * (tile + 1))
        wave_ref[rows, 0:128] = (amplitude * phase_cos).astype(jnp.bfloat16)
        wave_ref[rows, 128:256] = (amplitude * phase_sin).astype(jnp.bfloat16)
    inner = inner_ref[...]
    outer = outer_ref[...]
    for half in range(8):
        rows = slice(2 * DIRS * half, 2 * DIRS * (half + 1))
        part = jnp.dot(wave_ref[rows, :], inner, preferred_element_type=jnp.float32)
        part = part.astype(jnp.bfloat16)
        left = jnp.concatenate([part[:DIRS, :128], part[:DIRS, 128:]], axis=0)
        right = jnp.concatenate([part[DIRS:, :128], part[DIRS:, 128:]], axis=0)
        stacked = jnp.concatenate([left, right], axis=1)
        field = jnp.dot(outer, stacked, preferred_element_type=jnp.float32)
        wide_ref[0, pl.ds(half, DIRS, stride=16), :] = field[:DIRS, :128]
        wide_ref[1, pl.ds(half, DIRS, stride=16), :] = field[:DIRS, 128:]
        wide_ref[0, pl.ds(8 + half, DIRS, stride=16), :] = field[DIRS:, :128]
        wide_ref[1, pl.ds(8 + half, DIRS, stride=16), :] = field[DIRS:, 128:]
    for quarter in range(4):
        rows = slice(256 * quarter, 256 * (quarter + 1))
        for side in range(2):
            out_refs[quarter][0, :, :, 128 * side : 128 * (side + 1)] = (
                wide_ref[side, rows, :].astype(jnp.bfloat16).reshape(16, 16, 128)
            )


def fields(rays, phase_cos, phase_sin, inner, outer):
    groups = rays.shape[1]
    whole = lambda i: (0, 0)
    return pl.pallas_call(
        field_kernel,
        grid=(groups,),
        in_specs=[
            pl.BlockSpec((4, 1, 16, 2048), lambda i: (0, i, 0, 0)),
            pl.BlockSpec((DIRS, 128), whole),
            pl.BlockSpec((DIRS, 128), whole),
            pl.BlockSpec((256, 256), whole),
            pl.BlockSpec((128, 128), whole),
        ],
        out_specs=[pl.BlockSpec((1, 16, 16, 256), lambda i: (i, 0, 0, 0))] * 4,
        out_shape=[jax.ShapeDtypeStruct((groups, 16, 16, 256), jnp.bfloat16)] * 4,
        scratch_shapes=[
            pltpu.VMEM((1024, 256), jnp.bfloat16),
            pltpu.VMEM((2, 1024, 128), jnp.float32),
        ],
        compiler_params=params(1),
        name="fields",
    )(rays, phase_cos, phase_sin, inner, outer)


def spectrum_kernel(*refs):
    pieces = refs[:4]
    first_ref, twist_re_ref, twist_im_ref, second_ref, turn_re_ref, turn_im_ref = refs[4:10]
    re_ref, im_ref = refs[10:]
    row = pl.program_id(0) % 8
    signal = jnp.concatenate([p[...].reshape(128, SIDE) for p in pieces], axis=0)
    section = jnp.dot(first_ref[...], signal, preferred_element_type=jnp.float32)
    section_re, section_im = section[:SIDE], section[SIDE:]
    twist_re, twist_im = twist_re_ref[...], twist_im_ref[...]
    turned_re = (section_re * twist_re - section_im * twist_im).astype(jnp.bfloat16)
    turned_im = (section_re * twist_im + section_im * twist_re).astype(jnp.bfloat16)
    turned = jnp.concatenate([turned_re, turned_im], axis=1)
    final = lax.dot_general(
        second_ref[...],
        turned,
        (((1,), (1,)), ((), ())),
        preferred_element_type=jnp.float32,
    )
    final_re, final_im = final[:SIDE], final[SIDE:]
    turn_re, turn_im = turn_re_ref[...], turn_im_ref[...]
    out_re = final_re * turn_re - final_im * turn_im
    out_im = final_re * turn_im + final_im * turn_re
    for side in range(2):
        lanes = slice(128 * side, 128 * (side + 1))
        rows = pl.ds(8 * side + row, SIDE, stride=16)
        re_ref[rows, :] = out_re[:, lanes]
        im_ref[rows, :] = out_im[:, lanes]


def spectra(pieces, first, twist_re, twist_im, second, turn_re, turn_im):
    groups, rows = pieces[0].shape[:2]
    whole = lambda i: (0, 0)
    piece = pl.BlockSpec((groups, 1, 16, SIDE), lambda i: (0, i, 0, 0))
    square = pl.BlockSpec((SIDE, SIDE), whole)
    big = pl.BlockSpec((2 * SIDE, 2 * SIDE), whole)
    out_block = pl.BlockSpec((16 * SIDE, 128), lambda i: (i // 8, 0))
    out_shape = jax.ShapeDtypeStruct((rows // 8 * 16 * SIDE, 128), jnp.float32)
    return pl.pallas_call(
        spectrum_kernel,
        grid=(rows,),
        in_specs=[piece] * 4 + [big, square, square, big, square, square],
        out_specs=[out_block, out_block],
        out_shape=[out_shape, out_shape],
        compiler_params=params(1),
        name="spectra",
    )(*pieces, first, twist_re, twist_im, second, turn_re, turn_im)


def inner_outer_tables():
    table_re, table_im = direction_table(DIRS)
    zero = jnp.zeros_like(table_re)
    twice = lambda t: jnp.block([[t, zero], [zero, t]])
    inner = jnp.block(
        [[twice(table_re), twice(table_im)], [twice(-table_im), twice(table_re)]]
    )
    outer = jnp.block([[table_re, -table_im], [table_im, table_re]])
    return inner, outer


def first_tables():
    source = np.arange(4)[:, None, None]
    group = np.arange(8)[None, :, None]
    low = np.arange(8)[None, None, :]
    places = 32 * group + 8 * source + low
    cosine, sine = numpy_turns(np.arange(SIDE), places.reshape(-1), SIDE)
    shape = (SIDE, 4, 8, 8)
    cosine = cosine.reshape(shape) / 16.0
    sine = sine.reshape(shape) / 16.0
    upper = np.stack([cosine, sine], axis=3)
    lower = np.stack([-sine, cosine], axis=3)
    table = np.concatenate([upper, lower], axis=0).reshape(2 * SIDE, 4, 128)
    return jnp.asarray(table.transpose(1, 0, 2), dtype=jnp.bfloat16)


def second_table():
    cosine, sine = numpy_turns(np.arange(SIDE), np.arange(SIDE), SIDE)
    table = np.block([[cosine, sine], [-sine, cosine]]) / 16.0
    return jnp.asarray(table, dtype=jnp.bfloat16)


def twist_tables():
    cosine, sine = numpy_turns(np.arange(SIDE), np.arange(SIDE), SIDE * SIDE)
    return jnp.asarray(cosine, dtype=jnp.float32), jnp.asarray(-sine, dtype=jnp.float32)


def to_rows(flat):
    rows = flat.shape[0] // (16 * SIDE) * 8
    tiles = flat.reshape(rows // 8, SIDE, 2, 8, 128)
    return tiles.transpose(0, 3, 1, 2, 4).reshape(rows, SIDE * SIDE)


def per_device(views, phases, kernel_phase):
    sent = regroup(views)
    rays = lax.all_to_all(sent, HOGEL_GROUP, split_axis=0, concat_axis=0, tiled=True)
    angles = phases.astype(jnp.float32) * (2.0 * math.pi / PHASES)
    phase_cos = jnp.tile(jnp.cos(angles), (1, 2))
    phase_sin = jnp.tile(jnp.sin(angles), (1, 2))
    inner, outer = inner_outer_tables()
    quarters = fields(rays.reshape(4, 8, 16, 2048), phase_cos, phase_sin, inner, outer)
    me = lax.axis_index("zl") * 2 + lax.axis_index("xl")
    stacked = jnp.stack(quarters)
    got = lax.all_to_all(stacked, SQUARE, split_axis=0, concat_axis=0, tiled=True)
    pieces = [got[d] for d in range(4)]
    first = first_tables().transpose(1, 0, 2).reshape(2 * SIDE, 2 * SIDE)
    twist_re, twist_im = twist_tables()
    turn = kernel_phase.reshape(SIDE, SIDE)
    flat_re, flat_im = spectra(
        pieces, first, twist_re, twist_im, second_table(), jnp.cos(turn), jnp.sin(turn)
    )
    return to_rows(flat_re), to_rows(flat_im)


def solution(mesh):
    fine = Mesh(mesh.devices.reshape(2, 2, 4, 2, 2, 2), VIEW + COL)
    in_specs = (P(VIEW, COL, None), P(), P())
    out_specs = (P(VIEW + COL, None), P(VIEW + COL, None))
    return jax.shard_map(
        per_device, mesh=fine, in_specs=in_specs, out_specs=out_specs, check_vma=False
    )
```

profile of v0, /device:TPU:0, one launch (start us, length us, event | category | flops | bytes accessed | tf_op | source)
XLA Modules:
  0.0 132.5 jit_solution(7513581168046153855)
XLA Ops:
  0.6 1.6 %copy-done.1 = bf16[16,32,2048]{2,1,0:T(8,128)(2,1)S(1)} copy-done((bf16[16,32,2048]{2,1,0:T(8,128)(2,1)S(1)}, bf16[16,32,2048]{2,1,0:T(8,128)(2,1)}, u32[]{:S(2)}) %copy-start.1) | copy-done | bytes 2097176
  2.2 3.5 %regroup.1 = bf16[32,16,2048]{2,1,0:T(8,128)(2,1)S(1)} custom-call(bf16[16,32,2048]{2,1,0:T(8,128)(2,1)S(1)} %copy-done.1), custom_call_target="tpu_custom_call" | custom-call | tf_op jit(solution)/shard_map/regroup/pallas_call | solution.py:65
  5.7 1.3 copy-done
  7.0 10.7 %all-to-all-start = ((bf16[32,16,2048]{2,1,0:T(8,128)(2,1)}), bf16[32,16,2048]{2,1,0:T(8,128)(2,1)S(1)}, u32[]{:S(2)}, u32[]{:S(2)}) async-start(bf16[32,16,2048]{2,1,0:T(8,128)(2,1)} %copy-done), calls=%async_computation | async-start | bytes 4194304 | tf_op jit(solution)/shard_map/all_to_all | solution.py:226
  17.7 0.1 fusion.25
  17.9 0.1 tile.21.sin_ref
  18.0 0.1 tile.9.cos_ref
  18.2 0.1 fusion.27
  18.3 0.2 multiply_convert_fusion
  18.5 0.1 fusion.29
  18.5 0.1 maximum_maximum_fusion.outer_ref
  18.6 0.1 fusion.16.inner_ref
  18.7 28.9 %all-to-all-done = bf16[32,16,2048]{2,1,0:T(8,128)(2,1)S(1)} async-done(((bf16[32,16,2048]{2,1,0:T(8,128)(2,1)}), bf16[32,16,2048]{2,1,0:T(8,128)(2,1)S(1)}, u32[]{:S(2)}, u32[]{:S(2)}) %all-to-all-start) | async-done | bytes 2097184 | tf_op jit(solution)/shard_map/all_to_all | solution.py:226
  47.6 8.7 %fields.1 = (bf16[8,16,16,256]{3,2,1,0:T(8,128)(2,1)S(1)}, bf16[8,16,16,256]{3,2,1,0:T(8,128)(2,1)S(1)}, bf16[8,16,16,256]{3,2,1,0:T(8,128)(2,1)S(1)}, bf16[8,16,16,256]{3,2,1,0:T(8,128)(2,1)S(1)}) custom-call(bf16[4,8,16,2048]{3,2,1,0:T(8,128)(2,1)S(1)} %bitcast.23, f32[64,128]{1,0:T(8,128)S(1)} %tile.9.cos_ref, f32[64,128]{1,0:T(8,128)S(1)} %tile.21.sin_ref, ...), custom_call_target="tpu_custom_call" | custom-call | tf_op jit(solution)/shard_map/fields/pallas_call | solution.py:112
  56.3 2.3 %pad_maximum_fusion = bf16[4,8,16,16,256]{4,3,2,1,0:T(8,128)(2,1)} fusion(bf16[1,8,16,16,256]{4,3,2,1,0:T(8,128)(2,1)S(1)} %bitcast.27, bf16[1,8,16,16,256]{4,3,2,1,0:T(8,128)(2,1)S(1)} %bitcast.26, bf16[1,8,16,16,256]{4,3,2,1,0:T(8,128)(2,1)S(1)} %bitcast.25, bf16[1,8,16,16,256]{4,3,2,1,0:T(8,128)(2,1)S(1)} %bitcast.24), kind=kLoop, calls=%fused_computation | loop fusion | flops 6291456 | bytes 8388608 | tf_op jit(solution)/shard_map/stack | solution.py:233
  58.6 5.0 %all-to-all-start.1 = ((bf16[4,8,16,16,256]{4,3,2,1,0:T(8,128)(2,1)}), bf16[4,8,16,16,256]{4,3,2,1,0:T(8,128)(2,1)}, u32[]{:S(2)}, u32[]{:S(2)}) async-start(bf16[4,8,16,16,256]{4,3,2,1,0:T(8,128)(2,1)} %pad_maximum_fusion), calls=%async_computation.1 | async-start | bytes 8388608 | tf_op jit(solution)/shard_map/all_to_all | solution.py:234
  63.6 1.0 fusion.28
  64.5 0.1 sin.24.refs_9_
  64.6 0.1 cos.20.refs_8_
  64.7 0.0 copy-start.2
  64.7 0.0 copy-start.4
  64.8 46.1 %all-to-all-done.1 = bf16[4,8,16,16,256]{4,3,2,1,0:T(8,128)(2,1)} async-done(((bf16[4,8,16,16,256]{4,3,2,1,0:T(8,128)(2,1)}), bf16[4,8,16,16,256]{4,3,2,1,0:T(8,128)(2,1)}, u32[]{:S(2)}, u32[]{:S(2)}) %all-to-all-start.1) | async-done | bytes 4194336 | tf_op jit(solution)/shard_map/all_to_all | solution.py:234
  110.9 2.6 %slice_bitcast_fusion = (bf16[8,16,16,256]{3,2,1,0:T(8,128)(2,1)S(1)}, bf16[8,16,16,256]{3,2,1,0:T(8,128)(2,1)S(1)}, bf16[8,16,16,256]{3,2,1,0:T(8,128)(2,1)S(1)}, bf16[8,16,16,256]{3,2,1,0:T(8,128)(2,1)S(1)}) fusion(bf16[4,8,16,16,256]{4,3,2,1,0:T(8,128)(2,1)} %all-to-all-done.1), kind=kLoop, calls=%fused_computation.1 | loop fusion | bytes 8388608 | tf_op jit(solution)/shard_map/squeeze | solution.py:235
  113.5 19.0 %spectra.1 = (f32[8192,128]{1,0:T(8,128)}, f32[8192,128]{1,0:T(8,128)}) custom-call(bf16[8,16,16,256]{3,2,1,0:T(8,128)(2,1)S(1)} %get-tuple-element.17.refs_0_, bf16[8,16,16,256]{3,2,1,0:T(8,128)(2,1)S(1)} %get-tuple-element.16.refs_1_, bf16[8,16,16,256]{3,2,1,0:T(8,128)(2,1)S(1)} %get-tuple-element.15.refs_2_, ...), custom_call_target="tpu_custom_call" | custom-call | tf_op jit(solution)/shard_map/spectra/pallas_call | solution.py:170
  (14 shorter events, 0.1 us)
Async XLA Ops:
  0.6 1.6 %copy-start.1 = (bf16[16,32,2048]{2,1,0:T(8,128)(2,1)S(1)}, bf16[16,32,2048]{2,1,0:T(8,128)(2,1)}, u32[]{:S(2)}) copy-start(bf16[16,32,2048]{2,1,0:T(8,128)(2,1)} %views_ref.1) | copy-start | bytes 6291460
  2.2 15.5 %copy-start.7 = (s32[64,64]{1,0:T(8,128)S(1)}, s32[64,64]{1,0:T(8,128)}, u32[]{:S(2)}) copy-start(s32[64,64]{1,0:T(8,128)} %param.8) | copy-start | bytes 49156
  5.7 1.3 copy-start
  7.0 40.6 %all-to-all-start = ((bf16[32,16,2048]{2,1,0:T(8,128)(2,1)}), bf16[32,16,2048]{2,1,0:T(8,128)(2,1)S(1)}, u32[]{:S(2)}, u32[]{:S(2)}) async-start(bf16[32,16,2048]{2,1,0:T(8,128)(2,1)} %copy-done), calls=%async_computation | async-start | bytes 4194304 | tf_op jit(solution)/shard_map/all_to_all | solution.py:226
  58.6 5.0 %copy-start.6 = (f32[65536]{0:T(1024)S(1)}, f32[65536]{0:T(1024)}, u32[]{:S(2)}) copy-start(f32[65536]{0:T(1024)} %param.9) | copy-start | bytes 786436
  58.6 52.3 %all-to-all-start.1 = ((bf16[4,8,16,16,256]{4,3,2,1,0:T(8,128)(2,1)}), bf16[4,8,16,16,256]{4,3,2,1,0:T(8,128)(2,1)}, u32[]{:S(2)}, u32[]{:S(2)}) async-start(bf16[4,8,16,16,256]{4,3,2,1,0:T(8,128)(2,1)} %pad_maximum_fusion), calls=%async_computation.1 | async-start | bytes 8388608 | tf_op jit(solution)/shard_map/all_to_all | solution.py:234
  64.7 48.8 %copy-start.2 = (bf16[512,512]{1,0:T(8,128)(2,1)S(1)}, bf16[512,512]{1,0:T(8,128)(2,1)}, u32[]{:S(2)}) copy-start(bf16[512,512]{1,0:T(8,128)(2,1)} %constant.48.refs_4_) | copy-start | bytes 1572868
  64.7 48.8 %copy-start.3 = (bf16[512,512]{1,0:T(8,128)(2,1)S(1)}, bf16[512,512]{1,0:T(8,128)(2,1)}, u32[]{:S(2)}) copy-start(bf16[512,512]{1,0:T(8,128)(2,1)} %constant.34.clone.refs_7_) | copy-start | bytes 1572868
  64.7 48.8 %copy-start.4 = (f32[256,256]{1,0:T(8,128)S(1)}, f32[256,256]{1,0:T(8,128)}, u32[]{:S(2)}) copy-start(f32[256,256]{1,0:T(8,128)} %constant.33.clone.refs_6_) | copy-start | bytes 786436
  64.7 48.8 %copy-start.5 = (f32[256,256]{1,0:T(8,128)S(1)}, f32[256,256]{1,0:T(8,128)}, u32[]{:S(2)}) copy-start(f32[256,256]{1,0:T(8,128)} %constant.32.clone.refs_5_) | copy-start | bytes 786436
where the time goes:
time: 133 us
  waiting for transfers between devices  75 us (56%)
  Pallas kernels  31.1 us (23%)
  starting transfers between devices  15.7 us (12%)
  local copies, waits for them, and re-layouts  6.98 us (5%)
  other arithmetic  2.9 us (2%)
    all_to_all x1, waiting for transfers between devices, per_device(): lax.all_to_all(stacked, SQUARE, split_axis=0, concat_axis=0, tiled=True)  46.1 us
    all_to_all x1, waiting for transfers between devices, per_device(): lax.all_to_all(sent, HOGEL_GROUP, split_axis=0, concat_axis=0, tiled=True)  28.9 us
    pallas_call x1, Pallas kernels, spectra(): pl.pallas_call(spectrum_kernel, grid=(rows,), in_specs=[piece] * 4 + [big...  19 us
    all_to_all x1, starting transfers between devices, per_device(): lax.all_to_all(sent, HOGEL_GROUP, split_axis=0, concat_axis=0, tiled=True)  10.7 us
    pallas_call x1, Pallas kernels, fields(): pl.pallas_call(field_kernel, grid=(groups,), in_specs=[pl.BlockSpec((4, 1...  8.66 us
    all_to_all x1, starting transfers between devices, per_device(): lax.all_to_all(stacked, SQUARE, split_axis=0, concat_axis=0, tiled=True)  4.98 us
    pallas_call x1, Pallas kernels, regroup(): pl.pallas_call(regroup_kernel, grid=(steps,), in_specs=[pl.BlockSpec((dir...  3.46 us
    unnamed x16, local copies, waits for them, and re-layouts  2.93 us
  transfers between devices with their start and end apart: 2, of which 2 were waited for; matrix products, arithmetic and copies ran while one was open for 2% of the time, Pallas kernels for 0%

commit v1 on v0

--- a/solution.py
+++ b/solution.py
@@ -86,28 +86,31 @@
         wave_ref[rows, 128:256] = (amplitude * phase_sin).astype(jnp.bfloat16)
     inner = inner_ref[...]
     outer = outer_ref[...]
-    for half in range(8):
-        rows = slice(2 * DIRS * half, 2 * DIRS * (half + 1))
+    count = outer.shape[0] // 2
+    for low in range(8):
+        rows = slice(2 * DIRS * low, 2 * DIRS * (low + 1))
         part = jnp.dot(wave_ref[rows, :], inner, preferred_element_type=jnp.float32)
         part = part.astype(jnp.bfloat16)
         left = jnp.concatenate([part[:DIRS, :128], part[:DIRS, 128:]], axis=0)
         right = jnp.concatenate([part[DIRS:, :128], part[DIRS:, 128:]], axis=0)
         stacked = jnp.concatenate([left, right], axis=1)
         field = jnp.dot(outer, stacked, preferred_element_type=jnp.float32)
-        wide_ref[0, pl.ds(half, DIRS, stride=16), :] = field[:DIRS, :128]
-        wide_ref[1, pl.ds(half, DIRS, stride=16), :] = field[:DIRS, 128:]
-        wide_ref[0, pl.ds(8 + half, DIRS, stride=16), :] = field[DIRS:, :128]
-        wide_ref[1, pl.ds(8 + half, DIRS, stride=16), :] = field[DIRS:, 128:]
-    for quarter in range(4):
-        rows = slice(256 * quarter, 256 * (quarter + 1))
         for side in range(2):
-            out_refs[quarter][0, :, :, 128 * side : 128 * (side + 1)] = (
-                wide_ref[side, rows, :].astype(jnp.bfloat16).reshape(16, 16, 128)
+            lanes = slice(128 * side, 128 * (side + 1))
+            wide_ref[side, pl.ds(low, count, stride=16), :] = field[:count, lanes]
+            wide_ref[side, pl.ds(8 + low, count, stride=16), :] = field[count:, lanes]
+    each = count // 4
+    for partner in range(4):
+        rows = slice(16 * each * partner, 16 * each * (partner + 1))
+        for side in range(2):
+            out_refs[partner][0, :, :, 128 * side : 128 * (side + 1)] = (
+                wide_ref[side, rows, :].astype(jnp.bfloat16).reshape(each, 16, 128)
             )
 
 
 def fields(rays, phase_cos, phase_sin, inner, outer):
     groups = rays.shape[1]
+    count = outer.shape[0] // 2
     whole = lambda i: (0, 0)
     return pl.pallas_call(
         field_kernel,
@@ -117,24 +120,27 @@
             pl.BlockSpec((DIRS, 128), whole),
             pl.BlockSpec((DIRS, 128), whole),
             pl.BlockSpec((256, 256), whole),
-            pl.BlockSpec((128, 128), whole),
+            pl.BlockSpec((2 * count, 128), whole),
         ],
-        out_specs=[pl.BlockSpec((1, 16, 16, 256), lambda i: (i, 0, 0, 0))] * 4,
-        out_shape=[jax.ShapeDtypeStruct((groups, 16, 16, 256), jnp.bfloat16)] * 4,
+        out_specs=[pl.BlockSpec((1, count // 4, 16, 256), lambda i: (i, 0, 0, 0))] * 4,
+        out_shape=[jax.ShapeDtypeStruct((groups, count // 4, 16, 256), jnp.bfloat16)] * 4,
         scratch_shapes=[
             pltpu.VMEM((1024, 256), jnp.bfloat16),
-            pltpu.VMEM((2, 1024, 128), jnp.float32),
+            pltpu.VMEM((2, 16 * count, 128), jnp.float32),
         ],
         compiler_params=params(1),
+        cost_estimate=pl.CostEstimate(
+            flops=2 * 10**9, bytes_accessed=4 * 2**20, transcendentals=0
+        ),
         name="fields",
     )(rays, phase_cos, phase_sin, inner, outer)
 
 
-def spectrum_kernel(*refs):
+def spectrum_kernel(filled, *refs):
     pieces = refs[:4]
     first_ref, twist_re_ref, twist_im_ref, second_ref, turn_re_ref, turn_im_ref = refs[4:10]
-    re_ref, im_ref = refs[10:]
-    row = pl.program_id(0) % 8
+    re_ref, im_ref = refs[10 + filled :]
+    row = pl.program_id(0)
     signal = jnp.concatenate([p[...].reshape(128, SIDE) for p in pieces], axis=0)
     section = jnp.dot(first_ref[...], signal, preferred_element_type=jnp.float32)
     section_re, section_im = section[:SIDE], section[SIDE:]
@@ -159,23 +165,30 @@
         im_ref[rows, :] = out_im[:, lanes]
 
 
-def spectra(pieces, first, twist_re, twist_im, second, turn_re, turn_im):
+def spectra(pieces, tables, half, filled):
     groups, rows = pieces[0].shape[:2]
     whole = lambda i: (0, 0)
     piece = pl.BlockSpec((groups, 1, 16, SIDE), lambda i: (0, i, 0, 0))
     square = pl.BlockSpec((SIDE, SIDE), whole)
     big = pl.BlockSpec((2 * SIDE, 2 * SIDE), whole)
-    out_block = pl.BlockSpec((16 * SIDE, 128), lambda i: (i // 8, 0))
-    out_shape = jax.ShapeDtypeStruct((rows // 8 * 16 * SIDE, 128), jnp.float32)
+    out_block = pl.BlockSpec((16 * SIDE, 128), lambda i: (half, 0))
+    out_shape = jax.ShapeDtypeStruct((2 * 16 * SIDE, 128), jnp.float32)
+    aliases = {10 + i: i for i in range(len(filled))}
     return pl.pallas_call(
-        spectrum_kernel,
+        functools.partial(spectrum_kernel, len(filled)),
         grid=(rows,),
-        in_specs=[piece] * 4 + [big, square, square, big, square, square],
+        in_specs=[piece] * 4
+        + [big, square, square, big, square, square]
+        + [pl.BlockSpec(memory_space=pl.ANY)] * len(filled),
         out_specs=[out_block, out_block],
         out_shape=[out_shape, out_shape],
+        input_output_aliases=aliases,
         compiler_params=params(1),
+        cost_estimate=pl.CostEstimate(
+            flops=8 * 10**9, bytes_accessed=8 * 2**20, transcendentals=0
+        ),
         name="spectra",
-    )(*pieces, first, twist_re, twist_im, second, turn_re, turn_im)
+    )(*pieces, *tables, *filled)
 
 
 def inner_outer_tables():
@@ -185,8 +198,13 @@
     inner = jnp.block(
         [[twice(table_re), twice(table_im)], [twice(-table_im), twice(table_re)]]
     )
-    outer = jnp.block([[table_re, -table_im], [table_im, table_re]])
-    return inner, outer
+    outer = jnp.stack(
+        [
+            jnp.concatenate([table_re, -table_im], axis=1),
+            jnp.concatenate([table_im, table_re], axis=1),
+        ]
+    )
+    return inner, outer.reshape(2, 4, 2, 8, 2 * DIRS)
 
 
 def first_tables():
@@ -224,21 +242,31 @@
 def per_device(views, phases, kernel_phase):
     sent = regroup(views)
     rays = lax.all_to_all(sent, HOGEL_GROUP, split_axis=0, concat_axis=0, tiled=True)
+    rays = rays.reshape(4, 8, 16, 2048)
     angles = phases.astype(jnp.float32) * (2.0 * math.pi / PHASES)
     phase_cos = jnp.tile(jnp.cos(angles), (1, 2))
     phase_sin = jnp.tile(jnp.sin(angles), (1, 2))
     inner, outer = inner_outer_tables()
-    quarters = fields(rays.reshape(4, 8, 16, 2048), phase_cos, phase_sin, inner, outer)
     me = lax.axis_index("zl") * 2 + lax.axis_index("xl")
-    stacked = jnp.stack(quarters)
-    got = lax.all_to_all(stacked, SQUARE, split_axis=0, concat_axis=0, tiled=True)
-    pieces = [got[d] for d in range(4)]
-    first = first_tables().transpose(1, 0, 2).reshape(2 * SIDE, 2 * SIDE)
+    partners = [me ^ d for d in range(4)]
+    pick = lambda table, at, axis: lax.dynamic_index_in_dim(table, at, axis, False)
+    outer = jnp.stack([pick(outer, at, 1) for at in partners], axis=1)
+    source_tables = first_tables()
+    first = jnp.concatenate([pick(source_tables, at, 0) for at in partners], axis=1)
     twist_re, twist_im = twist_tables()
     turn = kernel_phase.reshape(SIDE, SIDE)
-    flat_re, flat_im = spectra(
-        pieces, first, twist_re, twist_im, second_table(), jnp.cos(turn), jnp.sin(turn)
-    )
+    tables = (first, twist_re, twist_im, second_table(), jnp.cos(turn), jnp.sin(turn))
+    halves = []
+    for half in range(2):
+        outer_half = outer[:, :, half].reshape(2 * 4 * 8, 2 * DIRS)
+        sending = fields(rays, phase_cos, phase_sin, inner, outer_half)
+        pieces = [sending[0], None, None, None]
+        for d in (3, 1, 2):
+            swaps = [(i, i ^ d) for i in range(4)]
+            pieces[d] = lax.ppermute(sending[d], SQUARE, swaps)
+        halves.append(pieces)
+    filled = spectra(halves[0], tables, 0, ())
+    flat_re, flat_im = spectra(halves[1], tables, 1, filled)
     return to_rows(flat_re), to_rows(flat_im)
 
 

time: 133 us -> 116 us (0.87)
  waiting for transfers between devices: 75 us -> 41.8 us
  Pallas kernels: 31.1 us -> 46.3 us
  starting transfers between devices: 15.7 us -> 17.8 us
  other arithmetic: 2.9 us -> 1.26 us
    all_to_all x1 -> x0, waiting for transfers between devices: 46.1 us -> none  [per_device(): lax.all_to_all(stacked, SQUARE, split_axis=0, concat_axis=0, tiled=True)]
    ppermute x0 -> x6, waiting for transfers between devices: none -> 13.6 us  [per_device(): pieces[d] = lax.ppermute(sending[d], SQUARE, swaps)]
    pallas_call x1 -> x2, Pallas kernels: 8.66 us -> 21.7 us  [fields(): pl.pallas_call(field_kernel, grid=(groups,), in_specs=[pl.BlockSpec((4, 1...]
    ppermute x0 -> x6, starting transfers between devices: none -> 7.06 us  [per_device(): pieces[d] = lax.ppermute(sending[d], SQUARE, swaps)]
    all_to_all x1 -> x0, starting transfers between devices: 4.98 us -> none  [per_device(): lax.all_to_all(stacked, SQUARE, split_axis=0, concat_axis=0, tiled=True)]
    sin x2, local copies, waits for them, and re-layouts: 1.04 us -> 3.58 us  [per_device(): jnp.sin(turn)]
    another operation x1 -> x2, other arithmetic: 2.29 us -> 0.1 us  [the longest x1 0.09 us: inner_outer_tables(): jnp.stack([jnp.concatenate([table_re, -table_im], axis=1), jnp.concatenat...]
    squeeze x1, local copies, waits for them, and re-layouts: 2.6 us -> 1.14 us  [per_device(): lax.dynamic_index_in_dim(table, at, axis, False)]
  transfers between devices with their start and end apart: 2 -> 7, of which waited for: 2 -> 4; matrix products, arithmetic and copies ran while one was open for 2% -> 6% of each run, Pallas kernels for 0% -> 18%
where the time goes in v1:
time: 116 us
  Pallas kernels  46.3 us (40%)
  waiting for transfers between devices  41.8 us (36%)
  starting transfers between devices  17.8 us (15%)
  local copies, waits for them, and re-layouts  7.72 us (7%)
  other arithmetic  1.26 us (1%)
    all_to_all x1, waiting for transfers between devices, per_device(): lax.all_to_all(sent, HOGEL_GROUP, split_axis=0, concat_axis=0, tiled=True)  28.2 us
    pallas_call x2, Pallas kernels, fields(): pl.pallas_call(field_kernel, grid=(groups,), in_specs=[pl.BlockSpec((4, 1...  21.7 us
    pallas_call x2, Pallas kernels, spectra(): pl.pallas_call(functools.partial(spectrum_kernel, len(filled)), grid=(row...  20.4 us
    ppermute x6, waiting for transfers between devices, per_device(): pieces[d] = lax.ppermute(sending[d], SQUARE, swaps)  13.6 us
    all_to_all x1, starting transfers between devices, per_device(): lax.all_to_all(sent, HOGEL_GROUP, split_axis=0, concat_axis=0, tiled=True)  10.7 us
    ppermute x6, starting transfers between devices, per_device(): pieces[d] = lax.ppermute(sending[d], SQUARE, swaps)  7.06 us
    pallas_call x1, Pallas kernels, regroup(): pl.pallas_call(regroup_kernel, grid=(steps,), in_specs=[pl.BlockSpec((dir...  4.24 us
    sin x2, local copies, waits for them, and re-layouts, per_device(): jnp.sin(turn)  3.58 us
  transfers between devices with their start and end apart: 7, of which 4 were waited for; matrix products, arithmetic and copies ran while one was open for 6% of the time, Pallas kernels for 18%

profile of v1, /device:TPU:0, one launch (start us, length us, event | category | flops | bytes accessed | tf_op | source)
XLA Modules:
  0.0 115.7 jit_solution(5322392995109512249)
XLA Ops:
  0.6 1.6 %copy-done = bf16[16,32,2048]{2,1,0:T(8,128)(2,1)S(1)} copy-done((bf16[16,32,2048]{2,1,0:T(8,128)(2,1)S(1)}, bf16[16,32,2048]{2,1,0:T(8,128)(2,1)}, u32[]{:S(2)}) %copy-start) | copy-done | bytes 2097176
  2.2 4.2 %regroup.1 = bf16[32,16,2048]{2,1,0:T(8,128)(2,1)} custom-call(bf16[16,32,2048]{2,1,0:T(8,128)(2,1)S(1)} %copy-done), custom_call_target="tpu_custom_call" | custom-call | tf_op jit(solution)/shard_map/regroup/pallas_call | solution.py:65
  6.5 10.7 %all-to-all-start = ((bf16[32,16,2048]{2,1,0:T(8,128)(2,1)}), bf16[32,16,2048]{2,1,0:T(8,128)(2,1)S(1)}, u32[]{:S(2)}, u32[]{:S(2)}) async-start(bf16[32,16,2048]{2,1,0:T(8,128)(2,1)} %regroup.1), calls=%async_computation | async-start | bytes 4194304 | tf_op jit(solution)/shard_map/all_to_all | solution.py:244
  17.9 0.1 multiply_convert_fusion.2
  18.1 0.2 fusion.34
  18.4 0.2 multiply_convert_fusion
  18.8 28.2 %all-to-all-done = bf16[32,16,2048]{2,1,0:T(8,128)(2,1)S(1)} async-done(((bf16[32,16,2048]{2,1,0:T(8,128)(2,1)}), bf16[32,16,2048]{2,1,0:T(8,128)(2,1)S(1)}, u32[]{:S(2)}, u32[]{:S(2)}) %all-to-all-start) | async-done | bytes 2097184 | tf_op jit(solution)/shard_map/all_to_all | solution.py:244
  47.0 11.2 %fields.3 = (bf16[8,8,16,256]{3,2,1,0:T(8,128)(2,1)S(1)}, bf16[8,8,16,256]{3,2,1,0:T(8,128)(2,1)}, bf16[8,8,16,256]{3,2,1,0:T(8,128)(2,1)}, bf16[8,8,16,256]{3,2,1,0:T(8,128)(2,1)}) custom-call(bf16[4,8,16,2048]{3,2,1,0:T(8,128)(2,1)S(1)} %bitcast.21, f32[64,128]{1,0:T(8,128)S(1)} %tile.9.cos_ref, f32[64,128]{1,0:T(8,128)S(1)} %tile.21.sin_ref, ...), custom_call_target="tpu_custom_call" | custom-call | flops 2000000000 | bytes 4194304 | tf_op jit(solution)/shard_map/fields/pallas_call | solution.py:115
  58.2 0.6 collective-permute-start.3
  58.8 1.0 collective-permute-start.4
  59.9 1.8 %collective-permute-start.5 = (bf16[8,8,16,256]{3,2,1,0:T(8,128)(2,1)}, bf16[8,8,16,256]{3,2,1,0:T(8,128)(2,1)}, u32[]{:S(2)}, u32[]{:S(2)}) collective-permute-start(bf16[8,8,16,256]{3,2,1,0:T(8,128)(2,1)} %get-tuple-element.21), channel_id=1, source_target_pairs={{0,3},{1,2},{2,1},{3,0},{4,7},{5,6},{6,5},{7,4},{8,11},{9,10},{10,... | collective-permute-start | bytes 1572872 | tf_op jit(solution)/shard_map/ppermute | solution.py:266
  61.7 2.5 %fusion.35 = (f32[65536]{0:T(1024)}, f32[65536]{0:T(1024)}) fusion(f32[65536]{0:T(1024)} %param.9), kind=kLoop, calls=%fused_computation.66 | loop fusion | bytes 786432 | tf_op jit(solution)/shard_map/sin | solution.py:258
  64.3 1.0 sin.33.refs_9_
  65.3 1.0 cos.27.refs_8_
  66.3 1.1 dynamic-slice_bitcast_fusion.3
  67.6 10.5 %fields.2 = (bf16[8,8,16,256]{3,2,1,0:T(8,128)(2,1)S(1)}, bf16[8,8,16,256]{3,2,1,0:T(8,128)(2,1)S(1)}, bf16[8,8,16,256]{3,2,1,0:T(8,128)(2,1)S(1)}, bf16[8,8,16,256]{3,2,1,0:T(8,128)(2,1)S(1)}) custom-call(bf16[4,8,16,2048]{3,2,1,0:T(8,128)(2,1)S(1)} %bitcast.22, f32[64,128]{1,0:T(8,128)S(1)} %tile.9.cos_ref, f32[64,128]{1,0:T(8,128)S(1)} %tile.21.sin_ref, ...), custom_call_target="tpu_custom_call" | custom-call | flops 2000000000 | bytes 4194304 | tf_op jit(solution)/shard_map/fields/pallas_call | solution.py:115
  78.1 0.7 collective-permute-start
  78.8 1.0 collective-permute-start.1
  79.8 1.8 %collective-permute-start.2 = (bf16[8,8,16,256]{3,2,1,0:T(8,128)(2,1)S(1)}, bf16[8,8,16,256]{3,2,1,0:T(8,128)(2,1)S(1)}, u32[]{:S(2)}, u32[]{:S(2)}) collective-permute-start(bf16[8,8,16,256]{3,2,1,0:T(8,128)(2,1)S(1)} %get-tuple-element.17), channel_id=1, source_target_pairs={{0,3},{1,2},{2,1},{3,0},{4,7},{5,6},{6,5},{7,4},{8,11},{9,10},{10,... | collective-permute-start | bytes 1572872 | tf_op jit(solution)/shard_map/ppermute | solution.py:266
  81.6 3.5 %collective-permute-done.5.refs_3_ = bf16[8,8,16,256]{3,2,1,0:T(8,128)(2,1)} collective-permute-done((bf16[8,8,16,256]{3,2,1,0:T(8,128)(2,1)}, bf16[8,8,16,256]{3,2,1,0:T(8,128)(2,1)}, u32[]{:S(2)}, u32[]{:S(2)}) %collective-permute-start.5) | collective-permute-done | bytes 524320 | tf_op jit(solution)/shard_map/ppermute | solution.py:266
  85.1 10.7 %spectra.2 = (f32[8192,128]{1,0:T(8,128)}, f32[8192,128]{1,0:T(8,128)}) custom-call(bf16[8,8,16,256]{3,2,1,0:T(8,128)(2,1)S(1)} %copy-done.5, bf16[8,8,16,256]{3,2,1,0:T(8,128)(2,1)S(1)} %collective-permute-done.3.refs_1_, bf16[8,8,16,256]{3,2,1,0:T(8,128)(2,1)} %collective-permute-done.4.refs_2_, bf16[8,8,16,256]{3,2,1,0:T(8,128)(2,1)} %collective-permute-done.5.refs_3_, ...), custom_call_target="tpu_custom_call" | custom-call | flops 8000000000 | bytes 8388608 | tf_op jit(solution)/shard_map/spectra/pallas_call | solution.py:177
  95.8 0.4 collective-permute-done.1.refs_2_
  96.2 9.8 %collective-permute-done.2.refs_3_ = bf16[8,8,16,256]{3,2,1,0:T(8,128)(2,1)S(1)} collective-permute-done((bf16[8,8,16,256]{3,2,1,0:T(8,128)(2,1)S(1)}, bf16[8,8,16,256]{3,2,1,0:T(8,128)(2,1)S(1)}, u32[]{:S(2)}, u32[]{:S(2)}) %collective-permute-start.2) | collective-permute-done | bytes 524320 | tf_op jit(solution)/shard_map/ppermute | solution.py:266
  106.0 9.8 %spectra.3 = (f32[8192,128]{1,0:T(8,128)}, f32[8192,128]{1,0:T(8,128)}) custom-call(bf16[8,8,16,256]{3,2,1,0:T(8,128)(2,1)S(1)} %get-tuple-element.14.refs_0_, bf16[8,8,16,256]{3,2,1,0:T(8,128)(2,1)S(1)} %collective-permute-done.refs_1_, bf16[8,8,16,256]{3,2,1,0:T(8,128)(2,1)S(1)} %collective-permute-done.1.refs_2_, ...), custom_call_target="tpu_custom_call", output_to_operand_aliasing={{0}: (10, {}), {1}: (11, {})} | custom-call | flops 8000000000 | bytes 8388608 | tf_op jit(solution)/shard_map/spectra/pallas_call | solution.py:177
  (31 shorter events, 1.1 us)
Async XLA Ops:
  0.6 1.6 %copy-start = (bf16[16,32,2048]{2,1,0:T(8,128)(2,1)S(1)}, bf16[16,32,2048]{2,1,0:T(8,128)(2,1)}, u32[]{:S(2)}) copy-start(bf16[16,32,2048]{2,1,0:T(8,128)(2,1)} %views_ref.1) | copy-start | bytes 6291460
  2.2 15.0 %copy-start.6 = (s32[64,64]{1,0:T(8,128)S(1)}, s32[64,64]{1,0:T(8,128)}, u32[]{:S(2)}) copy-start(s32[64,64]{1,0:T(8,128)} %param.8) | copy-start | bytes 49156
  6.5 40.6 %all-to-all-start = ((bf16[32,16,2048]{2,1,0:T(8,128)(2,1)}), bf16[32,16,2048]{2,1,0:T(8,128)(2,1)S(1)}, u32[]{:S(2)}, u32[]{:S(2)}) async-start(bf16[32,16,2048]{2,1,0:T(8,128)(2,1)} %regroup.1), calls=%async_computation | async-start | bytes 4194304 | tf_op jit(solution)/shard_map/all_to_all | solution.py:244
  58.2 6.0 %copy-start.4 = (bf16[8,8,16,256]{3,2,1,0:T(8,128)(2,1)}, bf16[8,8,16,256]{3,2,1,0:T(8,128)(2,1)S(1)}, u32[]{:S(2)}) copy-start(bf16[8,8,16,256]{3,2,1,0:T(8,128)(2,1)S(1)} %get-tuple-element.18.refs_0_) | copy-start | bytes 1572868
  58.2 21.6 %collective-permute-start.3 = (bf16[8,8,16,256]{3,2,1,0:T(8,128)(2,1)}, bf16[8,8,16,256]{3,2,1,0:T(8,128)(2,1)S(1)}, u32[]{:S(2)}, u32[]{:S(2)}) collective-permute-start(bf16[8,8,16,256]{3,2,1,0:T(8,128)(2,1)} %get-tuple-element.19), channel_id=1, source_target_pairs={{0,1},{1,0},{2,3},{3,2},{4,5},{5,4},{6,7},{7,6},{8,9},{9,8},{10,11... | collective-permute-start | bytes 1572872 | tf_op jit(solution)/shard_map/ppermute | solution.py:266
  58.8 22.8 %collective-permute-start.4 = (bf16[8,8,16,256]{3,2,1,0:T(8,128)(2,1)}, bf16[8,8,16,256]{3,2,1,0:T(8,128)(2,1)}, u32[]{:S(2)}, u32[]{:S(2)}) collective-permute-start(bf16[8,8,16,256]{3,2,1,0:T(8,128)(2,1)} %get-tuple-element.20), channel_id=1, source_target_pairs={{0,2},{1,3},{2,0},{3,1},{4,6},{5,7},{6,4},{7,5},{8,10},{9,11},{10,... | collective-permute-start | bytes 1572872 | tf_op jit(solution)/shard_map/ppermute | solution.py:266
  59.9 25.3 %collective-permute-start.5 = (bf16[8,8,16,256]{3,2,1,0:T(8,128)(2,1)}, bf16[8,8,16,256]{3,2,1,0:T(8,128)(2,1)}, u32[]{:S(2)}, u32[]{:S(2)}) collective-permute-start(bf16[8,8,16,256]{3,2,1,0:T(8,128)(2,1)} %get-tuple-element.21), channel_id=1, source_target_pairs={{0,3},{1,2},{2,1},{3,0},{4,7},{5,6},{6,5},{7,4},{8,11},{9,10},{10,... | collective-permute-start | bytes 1572872 | tf_op jit(solution)/shard_map/ppermute | solution.py:266
  67.5 17.7 %copy-start.1 = (bf16[512,512]{1,0:T(8,128)(2,1)S(1)}, bf16[512,512]{1,0:T(8,128)(2,1)}, u32[]{:S(2)}) copy-start(bf16[512,512]{1,0:T(8,128)(2,1)} %constant.77.clone.refs_7_) | copy-start | bytes 1572868
  67.5 17.7 %copy-start.2 = (f32[256,256]{1,0:T(8,128)S(1)}, f32[256,256]{1,0:T(8,128)}, u32[]{:S(2)}) copy-start(f32[256,256]{1,0:T(8,128)} %constant.76.clone.refs_6_) | copy-start | bytes 786436
  67.5 17.6 %copy-start.3 = (f32[256,256]{1,0:T(8,128)S(1)}, f32[256,256]{1,0:T(8,128)}, u32[]{:S(2)}) copy-start(f32[256,256]{1,0:T(8,128)} %constant.75.clone.refs_5_) | copy-start | bytes 786436
  67.5 17.6 %copy-start.5 = (bf16[8,8,16,256]{3,2,1,0:T(8,128)(2,1)S(1)}, bf16[8,8,16,256]{3,2,1,0:T(8,128)(2,1)}, u32[]{:S(2)}) copy-start(bf16[8,8,16,256]{3,2,1,0:T(8,128)(2,1)} %copy-done.4) | copy-start | bytes 1572868
  78.1 17.7 %collective-permute-start = (bf16[8,8,16,256]{3,2,1,0:T(8,128)(2,1)S(1)}, bf16[8,8,16,256]{3,2,1,0:T(8,128)(2,1)S(1)}, u32[]{:S(2)}, u32[]{:S(2)}) collective-permute-start(bf16[8,8,16,256]{3,2,1,0:T(8,128)(2,1)S(1)} %get-tuple-element.15), channel_id=1, source_target_pairs={{0,1},{1,0},{2,3},{3,2},{4,5},{5,4},{6,7},{7,6},{8,9},{9,8},{10,11... | collective-permute-start | bytes 1572872 | tf_op jit(solution)/shard_map/ppermute | solution.py:266
  78.8 17.4 %collective-permute-start.1 = (bf16[8,8,16,256]{3,2,1,0:T(8,128)(2,1)S(1)}, bf16[8,8,16,256]{3,2,1,0:T(8,128)(2,1)S(1)}, u32[]{:S(2)}, u32[]{:S(2)}) collective-permute-start(bf16[8,8,16,256]{3,2,1,0:T(8,128)(2,1)S(1)} %get-tuple-element.16), channel_id=1, source_target_pairs={{0,2},{1,3},{2,0},{3,1},{4,6},{5,7},{6,4},{7,5},{8,10},{9,11},{10,... | collective-permute-start | bytes 1572872 | tf_op jit(solution)/shard_map/ppermute | solution.py:266
  79.8 26.2 %collective-permute-start.2 = (bf16[8,8,16,256]{3,2,1,0:T(8,128)(2,1)S(1)}, bf16[8,8,16,256]{3,2,1,0:T(8,128)(2,1)S(1)}, u32[]{:S(2)}, u32[]{:S(2)}) collective-permute-start(bf16[8,8,16,256]{3,2,1,0:T(8,128)(2,1)S(1)} %get-tuple-element.17), channel_id=1, source_target_pairs={{0,3},{1,2},{2,1},{3,0},{4,7},{5,6},{6,5},{7,4},{8,11},{9,10},{10,... | collective-permute-start | bytes 1572872 | tf_op jit(solution)/shard_map/ppermute | solution.py:266

commit v2 on v1

v2 whole, which is shorter than its diff:
```python
import functools
import math

import jax
import jax.numpy as jnp
import numpy as np
from jax import lax
from jax.experimental import pallas as pl
from jax.experimental.pallas import tpu as pltpu
from jax.sharding import Mesh
from jax.sharding import PartitionSpec as P

PHASES = 256
DIRS = 64
SIDE = 256
VIEW = ("xh", "co")
COL = ("y", "zh", "zl", "xl")
HOGEL_GROUP = ("xh", "co", "y", "zh")
SQUARE = ("zl", "xl")
VMEM_BYTES = 40 * 1024 * 1024


def direction_table(length):
    positions = jnp.arange(length, dtype=jnp.int32)
    angles = (positions[:, None] * positions[None, :] % length).astype(jnp.float32) * (
        2.0 * math.pi / length
    )
    factor = 1.0 / math.sqrt(length)
    return (
        (jnp.cos(angles) * factor).astype(jnp.bfloat16),
        (jnp.sin(angles) * factor).astype(jnp.bfloat16),
    )


def numpy_turns(first, second, modulus):
    angles = (np.outer(first, second) % modulus) * (2.0 * np.pi / modulus)
    return np.cos(angles), np.sin(angles)


def params(limit=VMEM_BYTES):
    return pltpu.CompilerParams(
        dimension_semantics=("arbitrary",), vmem_limit_bytes=limit
    )


def regroup_kernel(views_ref, out_ref):
    dirs, cols, lanes = views_ref.shape
    low_half = lax.broadcasted_iota(jnp.int32, (dirs, 128), 1) < 64
    for pair in range(lanes // 128):
        block = views_ref[:, :, 128 * pair : 128 * (pair + 1)]
        block = jnp.swapaxes(block, 0, 1).astype(jnp.float32)
        for col in range(0, cols, 2):
            even, odd = block[col], block[col + 1]
            first = jnp.where(low_half, even, pltpu.roll(odd, 64, 1))
            second = jnp.where(low_half, pltpu.roll(even, 64, 1), odd)
            place = slice(64 * col, 64 * col + 128)
            out_ref[2 * pair, :, place] = first.astype(jnp.bfloat16)
            out_ref[2 * pair + 1, :, place] = second.astype(jnp.bfloat16)


def regroup(views, steps=2):
    dirs, cols, merged = views.shape
    lanes = merged // steps
    return pl.pallas_call(
        regroup_kernel,
        grid=(steps,),
        in_specs=[pl.BlockSpec((dirs, cols, lanes), lambda i: (0, 0, i))],
        out_specs=pl.BlockSpec((lanes // 64, dirs, cols * 64), lambda i: (i, 0, 0)),
        out_shape=jax.ShapeDtypeStruct((merged // 64, dirs, cols * 64), jnp.bfloat16),
        compiler_params=params(60 * 1024 * 1024),
        name="regroup",
    )(views)


def field_kernel(rays_ref, cos_ref, sin_ref, inner_ref, outer_ref, *out_refs):
    phase_cos = cos_ref[...]
    phase_sin = sin_ref[...]
    inner = inner_ref[...]
    outer = outer_ref[...]
    count = outer.shape[0] // 2
    each = count // 4
    groups = rays_ref.shape[1]
    stacked = []
    for group in range(groups):
        rays = rays_ref[:, group].reshape(DIRS, 32 * DIRS)

        def wave(tile):
            amplitude = rays[:, 128 * tile : 128 * (tile + 1)].astype(jnp.float32)
            wave_re = (amplitude * phase_cos).astype(jnp.bfloat16)
            wave_im = (amplitude * phase_sin).astype(jnp.bfloat16)
            return jnp.concatenate([wave_re, wave_im], axis=1)

        parts = []
        for low in range(8):
            waves = jnp.concatenate([wave(2 * low), wave(2 * low + 1)], axis=0)
            part = jnp.dot(waves, inner, preferred_element_type=jnp.float32)
            parts.append(part.astype(jnp.bfloat16))
        for part in parts:
            left = jnp.concatenate([part[:DIRS, :128], part[:DIRS, 128:]], axis=0)
            right = jnp.concatenate([part[DIRS:, :128], part[DIRS:, 128:]], axis=0)
            stacked.append(jnp.concatenate([left, right], axis=1))
    field = [jnp.dot(outer, s, preferred_element_type=jnp.float32) for s in stacked]
    for group in range(groups):
        own = field[8 * group : 8 * (group + 1)]
        sides = []
        for rows in (slice(0, count), slice(count, 2 * count)):
            sides.append(jnp.swapaxes(jnp.stack([f[rows] for f in own]), 0, 1))
        block = jnp.concatenate(sides, axis=1).astype(jnp.bfloat16)
        for partner in range(4):
            out_refs[partner][group] = block[each * partner : each * (partner + 1)]


def fields(rays, phase_cos, phase_sin, inner, outer, step=2):
    groups = rays.shape[1]
    count = outer.shape[0] // 2
    whole = lambda i: (0, 0)
    out_block = pl.BlockSpec((step, count // 4, 16, 256), lambda i: (i, 0, 0, 0))
    return pl.pallas_call(
        field_kernel,
        grid=(groups // step,),
        in_specs=[
            pl.BlockSpec((4, step, 16, 2048), lambda i: (0, i, 0, 0)),
            pl.BlockSpec((DIRS, 128), whole),
            pl.BlockSpec((DIRS, 128), whole),
            pl.BlockSpec((256, 256), whole),
            pl.BlockSpec((2 * count, 128), whole),
        ],
        out_specs=[out_block] * 4,
        out_shape=[jax.ShapeDtypeStruct((groups, count // 4, 16, 256), jnp.bfloat16)] * 4,
        compiler_params=params(),
        cost_estimate=pl.CostEstimate(
            flops=2 * 10**9, bytes_accessed=4 * 2**20, transcendentals=0
        ),
        name="fields",
    )(rays, phase_cos, phase_sin, inner, outer)


def spectrum_kernel(filled, *refs):
    pieces = refs[:4]
    first_ref, twist_re_ref, twist_im_ref, second_ref, turn_re_ref, turn_im_ref = refs[4:10]
    re_ref, im_ref, turned_ref = refs[10 + filled :]
    rows = turned_ref.shape[0]

    @pl.when(pl.program_id(0) == 0)
    def _():
        for row in range(rows):
            signal = [p[:, row].reshape(128, SIDE) for p in pieces]
            signal = jnp.concatenate(signal, axis=0)
            section = jnp.dot(first_ref[...], signal, preferred_element_type=jnp.float32)
            section_re, section_im = section[:SIDE], section[SIDE:]
            twist_re, twist_im = twist_re_ref[...], twist_im_ref[...]
            turned_re = section_re * twist_re - section_im * twist_im
            turned_im = section_re * twist_im + section_im * twist_re
            turned_ref[row, :, :SIDE] = turned_re.astype(jnp.bfloat16)
            turned_ref[row, :, SIDE:] = turned_im.astype(jnp.bfloat16)

    half = SIDE // 2
    second = second_ref[...].reshape(2 * half, 2 * SIDE)
    for row in range(rows):
        final = lax.dot_general(
            second,
            turned_ref[row],
            (((1,), (1,)), ((), ())),
            preferred_element_type=jnp.float32,
        )
        final_re, final_im = final[:half], final[half:]
        turn_re, turn_im = turn_re_ref[...], turn_im_ref[...]
        out_re = final_re * turn_re - final_im * turn_im
        out_im = final_re * turn_im + final_im * turn_re
        for side in range(2):
            lanes = slice(128 * side, 128 * (side + 1))
            place = pl.ds(8 * side + row, half, stride=16)
            re_ref[place, :] = out_re[:, lanes]
            im_ref[place, :] = out_im[:, lanes]


def spectra(pieces, tables, half, filled):
    groups, rows = pieces[0].shape[:2]
    whole = lambda i: (0, 0)
    piece = pl.BlockSpec((groups, rows, 16, SIDE), lambda i: (0, 0, 0, 0))
    square = pl.BlockSpec((SIDE, SIDE), whole)
    first = pl.BlockSpec((2 * SIDE, 2 * SIDE), whole)
    second = pl.BlockSpec((2, SIDE // 2, 2 * SIDE), lambda i: (0, i, 0))
    turn = pl.BlockSpec((SIDE // 2, SIDE), lambda i: (i, 0))
    out_block = pl.BlockSpec((8 * SIDE, 128), lambda i: (2 * half + i, 0))
    out_shape = jax.ShapeDtypeStruct((2 * 16 * SIDE, 128), jnp.float32)
    aliases = {10 + i: i for i in range(len(filled))}
    return pl.pallas_call(
        functools.partial(spectrum_kernel, len(filled)),
        grid=(2,),
        in_specs=[piece] * 4
        + [first, square, square, second, turn, turn]
        + [pl.BlockSpec(memory_space=pl.ANY)] * len(filled),
        out_specs=[out_block, out_block],
        out_shape=[out_shape, out_shape],
        scratch_shapes=[pltpu.VMEM((rows, SIDE, 2 * SIDE), jnp.bfloat16)],
        input_output_aliases=aliases,
        compiler_params=params(),
        cost_estimate=pl.CostEstimate(
            flops=8 * 10**9, bytes_accessed=8 * 2**20, transcendentals=0
        ),
        name="spectra",
    )(*pieces, *tables, *filled)


def inner_outer_tables():
    table_re, table_im = direction_table(DIRS)
    zero = jnp.zeros_like(table_re)
    twice = lambda t: jnp.block([[t, zero], [zero, t]])
    inner = jnp.block(
        [[twice(table_re), twice(table_im)], [twice(-table_im), twice(table_re)]]
    )
    outer = jnp.stack(
        [
            jnp.concatenate([table_re, -table_im], axis=1),
            jnp.concatenate([table_im, table_re], axis=1),
        ]
    )
    return inner, outer.reshape(2, 4, 2, 8, 2 * DIRS)


def first_tables():
    source = np.arange(4)[:, None, None]
    group = np.arange(8)[None, :, None]
    low = np.arange(8)[None, None, :]
    places = 32 * group + 8 * source + low
    cosine, sine = numpy_turns(np.arange(SIDE), places.reshape(-1), SIDE)
    shape = (SIDE, 4, 8, 8)
    cosine = cosine.reshape(shape) / 16.0
    sine = sine.reshape(shape) / 16.0
    upper = np.stack([cosine, sine], axis=3)
    lower = np.stack([-sine, cosine], axis=3)
    table = np.concatenate([upper, lower], axis=0).reshape(2 * SIDE, 4, 128)
    return jnp.asarray(table.transpose(1, 0, 2), dtype=jnp.bfloat16)


def second_table():
    cosine, sine = numpy_turns(np.arange(SIDE), np.arange(SIDE), SIDE)
    table = np.block([[cosine, sine], [-sine, cosine]]) / 16.0
    return jnp.asarray(table.reshape(2, SIDE, 2 * SIDE), dtype=jnp.bfloat16)


def twist_tables():
    cosine, sine = numpy_turns(np.arange(SIDE), np.arange(SIDE), SIDE * SIDE)
    return jnp.asarray(cosine, dtype=jnp.float32), jnp.asarray(-sine, dtype=jnp.float32)


def to_rows(flat):
    rows = flat.shape[0] // (16 * SIDE) * 8
    tiles = flat.reshape(rows // 8, SIDE, 2, 8, 128)
    return tiles.transpose(0, 3, 1, 2, 4).reshape(rows, SIDE * SIDE)


def per_device(views, phases, kernel_phase):
    sent = regroup(views)
    rays = lax.all_to_all(sent, HOGEL_GROUP, split_axis=0, concat_axis=0, tiled=True)
    rays = rays.reshape(4, 8, 16, 2048)
    angles = phases.astype(jnp.float32) * (2.0 * math.pi / PHASES)
    phase_cos = jnp.tile(jnp.cos(angles), (1, 2))
    phase_sin = jnp.tile(jnp.sin(angles), (1, 2))
    inner, outer = inner_outer_tables()
    me = lax.axis_index("zl") * 2 + lax.axis_index("xl")
    partners = [me ^ d for d in range(4)]
    pick = lambda table, at, axis: lax.dynamic_index_in_dim(table, at, axis, False)
    outer = jnp.stack([pick(outer, at, 1) for at in partners], axis=1)
    source_tables = first_tables()
    first = jnp.concatenate([pick(source_tables, at, 0) for at in partners], axis=1)
    twist_re, twist_im = twist_tables()
    turn = kernel_phase.reshape(SIDE, SIDE)
    tables = (first, twist_re, twist_im, second_table(), jnp.cos(turn), jnp.sin(turn))
    halves = []
    for half in range(2):
        outer_half = outer[:, :, half].reshape(2 * 4 * 8, 2 * DIRS)
        sending = fields(rays, phase_cos, phase_sin, inner, outer_half)
        pieces = [sending[0], None, None, None]
        for d in (3, 1, 2):
            swaps = [(i, i ^ d) for i in range(4)]
            pieces[d] = lax.ppermute(sending[d], SQUARE, swaps)
        halves.append(pieces)
    filled = spectra(halves[0], tables, 0, ())
    flat_re, flat_im = spectra(halves[1], tables, 1, filled)
    return to_rows(flat_re), to_rows(flat_im)


def solution(mesh):
    fine = Mesh(mesh.devices.reshape(2, 2, 4, 2, 2, 2), VIEW + COL)
    in_specs = (P(VIEW, COL, None), P(), P())
    out_specs = (P(VIEW + COL, None), P(VIEW + COL, None))
    return jax.shard_map(
        per_device, mesh=fine, in_specs=in_specs, out_specs=out_specs, check_vma=False
    )
```

time: 116 us -> 102 us (0.88)
  Pallas kernels: 46.3 us -> 22.3 us
  waiting for transfers between devices: 41.8 us -> 54.1 us
  local copies, waits for them, and re-layouts: 7.72 us -> 6.13 us
    pallas_call x4, Pallas kernels: 42.1 us -> 18.7 us  [the longest x2 12.1 us: spectra(): pl.pallas_call(functools.partial(spectrum_kernel, len(filled)), grid=(2,)...]
    ppermute x6, waiting for transfers between devices: 13.6 us -> 25.9 us  [per_device(): pieces[d] = lax.ppermute(sending[d], SQUARE, swaps)]
    unnamed x14 -> x12, local copies, waits for them, and re-layouts: 1.62 us -> 0.03 us
  transfers between devices with their start and end apart: 7 -> 7, of which waited for: 4 -> 7; matrix products, arithmetic and copies ran while one was open for 6% -> 7% of each run, Pallas kernels for 18% -> 9%
where the time goes in v2:
time: 102 us
  waiting for transfers between devices  54.1 us (53%)
  Pallas kernels  22.3 us (22%)
  starting transfers between devices  17.1 us (17%)
  local copies, waits for them, and re-layouts  6.13 us (6%)
  other arithmetic  1.26 us (1%)
    all_to_all x1, waiting for transfers between devices, per_device(): lax.all_to_all(sent, HOGEL_GROUP, split_axis=0, concat_axis=0, tiled=True)  28.2 us
    ppermute x6, waiting for transfers between devices, per_device(): pieces[d] = lax.ppermute(sending[d], SQUARE, swaps)  25.9 us
    pallas_call x2, Pallas kernels, spectra(): pl.pallas_call(functools.partial(spectrum_kernel, len(filled)), grid=(2,)...  12.1 us
    all_to_all x1, starting transfers between devices, per_device(): lax.all_to_all(sent, HOGEL_GROUP, split_axis=0, concat_axis=0, tiled=True)  10.7 us
    pallas_call x2, Pallas kernels, fields(): pl.pallas_call(field_kernel, grid=(groups // step,), in_specs=[pl.BlockSp...  6.61 us
    ppermute x6, starting transfers between devices, per_device(): pieces[d] = lax.ppermute(sending[d], SQUARE, swaps)  6.38 us
    pallas_call x1, Pallas kernels, regroup(): pl.pallas_call(regroup_kernel, grid=(steps,), in_specs=[pl.BlockSpec((dir...  3.62 us
    sin x2, local copies, waits for them, and re-layouts, per_device(): jnp.sin(turn)  3.57 us
  transfers between devices with their start and end apart: 7, of which 7 were waited for; matrix products, arithmetic and copies ran while one was open for 7% of the time, Pallas kernels for 9%

profile of v2, /device:TPU:0, one launch (start us, length us, event | category | flops | bytes accessed | tf_op | source)
XLA Modules:
  0.0 101.7 jit_solution(10019233403177347790)
XLA Ops:
  0.6 3.6 %regroup.1 = bf16[32,16,2048]{2,1,0:T(8,128)(2,1)} custom-call(bf16[16,32,2048]{2,1,0:T(8,128)(2,1)} %views_ref.1), custom_call_target="tpu_custom_call" | custom-call | tf_op jit(solution)/shard_map/regroup/pallas_call | solution.py:64
  4.3 10.7 %all-to-all-start = ((bf16[32,16,2048]{2,1,0:T(8,128)(2,1)}), bf16[32,16,2048]{2,1,0:T(8,128)(2,1)S(1)}, u32[]{:S(2)}, u32[]{:S(2)}) async-start(bf16[32,16,2048]{2,1,0:T(8,128)(2,1)} %regroup.1), calls=%async_computation | async-start | bytes 4194304 | tf_op jit(solution)/shard_map/all_to_all | solution.py:256
  15.9 0.2 fusion.34
  16.2 0.2 multiply_convert_fusion
  16.6 28.2 %all-to-all-done = bf16[32,16,2048]{2,1,0:T(8,128)(2,1)S(1)} async-done(((bf16[32,16,2048]{2,1,0:T(8,128)(2,1)}), bf16[32,16,2048]{2,1,0:T(8,128)(2,1)S(1)}, u32[]{:S(2)}, u32[]{:S(2)}) %all-to-all-start) | async-done | bytes 2097184 | tf_op jit(solution)/shard_map/all_to_all | solution.py:256
  44.8 3.7 %fields.3 = (bf16[8,8,16,256]{3,2,1,0:T(8,128)(2,1)S(1)}, bf16[8,8,16,256]{3,2,1,0:T(8,128)(2,1)}, bf16[8,8,16,256]{3,2,1,0:T(8,128)(2,1)}, bf16[8,8,16,256]{3,2,1,0:T(8,128)(2,1)}) custom-call(bf16[4,8,16,2048]{3,2,1,0:T(8,128)(2,1)S(1)} %bitcast.21, f32[64,128]{1,0:T(8,128)S(1)} %tile.9.cos_ref, f32[64,128]{1,0:T(8,128)S(1)} %tile.21.sin_ref, ...), custom_call_target="tpu_custom_call" | custom-call | flops 2000000000 | bytes 4194304 | tf_op jit(solution)/shard_map/fields/pallas_call | solution.py:118
  48.5 0.6 collective-permute-start.3
  49.1 1.1 %collective-permute-start.4 = (bf16[8,8,16,256]{3,2,1,0:T(8,128)(2,1)}, bf16[8,8,16,256]{3,2,1,0:T(8,128)(2,1)}, u32[]{:S(2)}, u32[]{:S(2)}) collective-permute-start(bf16[8,8,16,256]{3,2,1,0:T(8,128)(2,1)} %get-tuple-element.20), channel_id=1, source_target_pairs={{0,2},{1,3},{2,0},{3,1},{4,6},{5,7},{6,4},{7,5},{8,10},{9,11},{10,... | collective-permute-start | bytes 1572872 | tf_op jit(solution)/shard_map/ppermute | solution.py:278
  50.2 1.8 %collective-permute-start.5 = (bf16[8,8,16,256]{3,2,1,0:T(8,128)(2,1)}, bf16[8,8,16,256]{3,2,1,0:T(8,128)(2,1)}, u32[]{:S(2)}, u32[]{:S(2)}) collective-permute-start(bf16[8,8,16,256]{3,2,1,0:T(8,128)(2,1)} %get-tuple-element.21), channel_id=1, source_target_pairs={{0,3},{1,2},{2,1},{3,0},{4,7},{5,6},{6,5},{7,4},{8,11},{9,10},{10,... | collective-permute-start | bytes 1572872 | tf_op jit(solution)/shard_map/ppermute | solution.py:278
  52.0 2.5 %fusion.35 = (f32[65536]{0:T(1024)}, f32[65536]{0:T(1024)}) fusion(f32[65536]{0:T(1024)} %param.9), kind=kLoop, calls=%fused_computation.66 | loop fusion | bytes 786432 | tf_op jit(solution)/shard_map/sin | solution.py:270
  54.5 1.0 %sin.33.refs_9_ = f32[256,256]{1,0:T(8,128)S(1)} reshape(f32[65536]{0:T(1024)} %get-tuple-element.30) | data formatting | bytes 524288 | tf_op jit(solution)/shard_map/sin | solution.py:270
  55.6 1.0 %cos.27.refs_8_ = f32[256,256]{1,0:T(8,128)S(1)} reshape(f32[65536]{0:T(1024)} %get-tuple-element.31) | data formatting | bytes 524288 | tf_op jit(solution)/shard_map/cos | solution.py:270
  56.6 1.1 %dynamic-slice_bitcast_fusion.3 = (bf16[512,128]{1,0:T(8,128)(2,1)S(1)}, bf16[512,128]{1,0:T(8,128)(2,1)S(1)}, bf16[512,128]{1,0:T(8,128)(2,1)S(1)}, bf16[512,128]{1,0:T(8,128)(2,1)S(1)}) fusion(bf16[4,512,128]{2,1,0:T(8,128)(2,1)} %constant.74.clone, s32[]{:T(128)S(6)} %select_n.57, s32[]{:T(128)S(6)} %select_n.58, s32[]{:T(128)S(6)} %select_n.60, ...), kind=kLoop, calls=%fused_computation.31 | loop fusion | bytes 1048592 | tf_op jit(solution)/shard_map/jit(dynamic_index_in_dim)/squeeze | solution.py:264
  57.9 2.9 %fields.2 = (bf16[8,8,16,256]{3,2,1,0:T(8,128)(2,1)S(1)}, bf16[8,8,16,256]{3,2,1,0:T(8,128)(2,1)S(1)}, bf16[8,8,16,256]{3,2,1,0:T(8,128)(2,1)S(1)}, bf16[8,8,16,256]{3,2,1,0:T(8,128)(2,1)S(1)}) custom-call(bf16[4,8,16,2048]{3,2,1,0:T(8,128)(2,1)S(1)} %bitcast.22, f32[64,128]{1,0:T(8,128)S(1)} %tile.9.cos_ref, f32[64,128]{1,0:T(8,128)S(1)} %tile.21.sin_ref, ...), custom_call_target="tpu_custom_call" | custom-call | flops 2000000000 | bytes 4194304 | tf_op jit(solution)/shard_map/fields/pallas_call | solution.py:118
  60.8 0.7 collective-permute-start
  61.5 1.1 %collective-permute-start.1 = (bf16[8,8,16,256]{3,2,1,0:T(8,128)(2,1)S(1)}, bf16[8,8,16,256]{3,2,1,0:T(8,128)(2,1)S(1)}, u32[]{:S(2)}, u32[]{:S(2)}) collective-permute-start(bf16[8,8,16,256]{3,2,1,0:T(8,128)(2,1)S(1)} %get-tuple-element.16), channel_id=1, source_target_pairs={{0,2},{1,3},{2,0},{3,1},{4,6},{5,7},{6,4},{7,5},{8,10},{9,11},{10,... | collective-permute-start | bytes 1572872 | tf_op jit(solution)/shard_map/ppermute | solution.py:278
  62.6 1.0 collective-permute-done.3.refs_1_
  63.6 1.1 %collective-permute-start.2 = (bf16[8,8,16,256]{3,2,1,0:T(8,128)(2,1)S(1)}, bf16[8,8,16,256]{3,2,1,0:T(8,128)(2,1)S(1)}, u32[]{:S(2)}, u32[]{:S(2)}) collective-permute-start(bf16[8,8,16,256]{3,2,1,0:T(8,128)(2,1)S(1)} %get-tuple-element.17), channel_id=1, source_target_pairs={{0,3},{1,2},{2,1},{3,0},{4,7},{5,6},{6,5},{7,4},{8,11},{9,10},{10,... | collective-permute-start | bytes 1572872 | tf_op jit(solution)/shard_map/ppermute | solution.py:278
  64.7 8.4 %collective-permute-done.4.refs_2_ = bf16[8,8,16,256]{3,2,1,0:T(8,128)(2,1)} collective-permute-done((bf16[8,8,16,256]{3,2,1,0:T(8,128)(2,1)}, bf16[8,8,16,256]{3,2,1,0:T(8,128)(2,1)}, u32[]{:S(2)}, u32[]{:S(2)}) %collective-permute-start.4) | collective-permute-done | bytes 524320 | tf_op jit(solution)/shard_map/ppermute | solution.py:278
  73.1 2.3 %collective-permute-done.5.refs_3_ = bf16[8,8,16,256]{3,2,1,0:T(8,128)(2,1)} collective-permute-done((bf16[8,8,16,256]{3,2,1,0:T(8,128)(2,1)}, bf16[8,8,16,256]{3,2,1,0:T(8,128)(2,1)}, u32[]{:S(2)}, u32[]{:S(2)}) %collective-permute-start.5) | collective-permute-done | bytes 524320 | tf_op jit(solution)/shard_map/ppermute | solution.py:278
  75.5 6.6 %spectra.2 = (f32[8192,128]{1,0:T(8,128)}, f32[8192,128]{1,0:T(8,128)}) custom-call(bf16[8,8,16,256]{3,2,1,0:T(8,128)(2,1)S(1)} %copy-done.4, bf16[8,8,16,256]{3,2,1,0:T(8,128)(2,1)S(1)} %collective-permute-done.3.refs_1_, bf16[8,8,16,256]{3,2,1,0:T(8,128)(2,1)} %collective-permute-done.4.refs_2_, bf16[8,8,16,256]{3,2,1,0:T(8,128)(2,1)} %collective-permute-done.5.refs_3_, ...), custom_call_target="tpu_custom_call" | custom-call | flops 8000000000 | bytes 8388608 | tf_op jit(solution)/shard_map/spectra/pallas_call | solution.py:188
  82.1 4.0 %collective-permute-done.refs_1_ = bf16[8,8,16,256]{3,2,1,0:T(8,128)(2,1)S(1)} collective-permute-done((bf16[8,8,16,256]{3,2,1,0:T(8,128)(2,1)S(1)}, bf16[8,8,16,256]{3,2,1,0:T(8,128)(2,1)S(1)}, u32[]{:S(2)}, u32[]{:S(2)}) %collective-permute-start) | collective-permute-done | bytes 524320 | tf_op jit(solution)/shard_map/ppermute | solution.py:278
  86.2 10.0 %collective-permute-done.2.refs_3_ = bf16[8,8,16,256]{3,2,1,0:T(8,128)(2,1)S(1)} collective-permute-done((bf16[8,8,16,256]{3,2,1,0:T(8,128)(2,1)S(1)}, bf16[8,8,16,256]{3,2,1,0:T(8,128)(2,1)S(1)}, u32[]{:S(2)}, u32[]{:S(2)}) %collective-permute-start.2) | collective-permute-done | bytes 524320 | tf_op jit(solution)/shard_map/ppermute | solution.py:278
  96.2 5.4 %spectra.3 = (f32[8192,128]{1,0:T(8,128)}, f32[8192,128]{1,0:T(8,128)}) custom-call(bf16[8,8,16,256]{3,2,1,0:T(8,128)(2,1)S(1)} %get-tuple-element.14.refs_0_, bf16[8,8,16,256]{3,2,1,0:T(8,128)(2,1)S(1)} %collective-permute-done.refs_1_, bf16[8,8,16,256]{3,2,1,0:T(8,128)(2,1)S(1)} %collective-permute-done.1.refs_2_, ...), custom_call_target="tpu_custom_call", output_to_operand_aliasing={{0}: (10, {}), {1}: (11, {})} | custom-call | flops 8000000000 | bytes 8388608 | tf_op jit(solution)/shard_map/spectra/pallas_call | solution.py:188
  (29 shorter events, 1.3 us)
Async XLA Ops:
  0.6 14.4 %copy-start.5 = (s32[64,64]{1,0:T(8,128)S(1)}, s32[64,64]{1,0:T(8,128)}, u32[]{:S(2)}) copy-start(s32[64,64]{1,0:T(8,128)} %param.8) | copy-start | bytes 49156
  4.3 40.6 %all-to-all-start = ((bf16[32,16,2048]{2,1,0:T(8,128)(2,1)}), bf16[32,16,2048]{2,1,0:T(8,128)(2,1)S(1)}, u32[]{:S(2)}, u32[]{:S(2)}) async-start(bf16[32,16,2048]{2,1,0:T(8,128)(2,1)} %regroup.1), calls=%async_computation | async-start | bytes 4194304 | tf_op jit(solution)/shard_map/all_to_all | solution.py:256
  48.5 6.0 %copy-start.3 = (bf16[8,8,16,256]{3,2,1,0:T(8,128)(2,1)}, bf16[8,8,16,256]{3,2,1,0:T(8,128)(2,1)S(1)}, u32[]{:S(2)}) copy-start(bf16[8,8,16,256]{3,2,1,0:T(8,128)(2,1)S(1)} %get-tuple-element.18.refs_0_) | copy-start | bytes 1572868
  48.5 15.1 %collective-permute-start.3 = (bf16[8,8,16,256]{3,2,1,0:T(8,128)(2,1)}, bf16[8,8,16,256]{3,2,1,0:T(8,128)(2,1)S(1)}, u32[]{:S(2)}, u32[]{:S(2)}) collective-permute-start(bf16[8,8,16,256]{3,2,1,0:T(8,128)(2,1)} %get-tuple-element.19), channel_id=1, source_target_pairs={{0,1},{1,0},{2,3},{3,2},{4,5},{5,4},{6,7},{7,6},{8,9},{9,8},{10,11... | collective-permute-start | bytes 1572872 | tf_op jit(solution)/shard_map/ppermute | solution.py:278
  49.1 24.0 %collective-permute-start.4 = (bf16[8,8,16,256]{3,2,1,0:T(8,128)(2,1)}, bf16[8,8,16,256]{3,2,1,0:T(8,128)(2,1)}, u32[]{:S(2)}, u32[]{:S(2)}) collective-permute-start(bf16[8,8,16,256]{3,2,1,0:T(8,128)(2,1)} %get-tuple-element.20), channel_id=1, source_target_pairs={{0,2},{1,3},{2,0},{3,1},{4,6},{5,7},{6,4},{7,5},{8,10},{9,11},{10,... | collective-permute-start | bytes 1572872 | tf_op jit(solution)/shard_map/ppermute | solution.py:278
  50.2 25.3 %collective-permute-start.5 = (bf16[8,8,16,256]{3,2,1,0:T(8,128)(2,1)}, bf16[8,8,16,256]{3,2,1,0:T(8,128)(2,1)}, u32[]{:S(2)}, u32[]{:S(2)}) collective-permute-start(bf16[8,8,16,256]{3,2,1,0:T(8,128)(2,1)} %get-tuple-element.21), channel_id=1, source_target_pairs={{0,3},{1,2},{2,1},{3,0},{4,7},{5,6},{6,5},{7,4},{8,11},{9,10},{10,... | collective-permute-start | bytes 1572872 | tf_op jit(solution)/shard_map/ppermute | solution.py:278
  57.8 17.7 %copy-start = (bf16[2,256,512]{2,1,0:T(8,128)(2,1)S(1)}, bf16[2,256,512]{2,1,0:T(8,128)(2,1)}, u32[]{:S(2)}) copy-start(bf16[2,256,512]{2,1,0:T(8,128)(2,1)} %constant.77.clone.refs_7_) | copy-start | bytes 1572868
  57.8 17.7 %copy-start.1 = (f32[256,256]{1,0:T(8,128)S(1)}, f32[256,256]{1,0:T(8,128)}, u32[]{:S(2)}) copy-start(f32[256,256]{1,0:T(8,128)} %constant.76.clone.refs_6_) | copy-start | bytes 786436
  57.8 17.7 %copy-start.2 = (f32[256,256]{1,0:T(8,128)S(1)}, f32[256,256]{1,0:T(8,128)}, u32[]{:S(2)}) copy-start(f32[256,256]{1,0:T(8,128)} %constant.75.clone.refs_5_) | copy-start | bytes 786436
  57.8 17.7 %copy-start.4 = (bf16[8,8,16,256]{3,2,1,0:T(8,128)(2,1)S(1)}, bf16[8,8,16,256]{3,2,1,0:T(8,128)(2,1)}, u32[]{:S(2)}) copy-start(bf16[8,8,16,256]{3,2,1,0:T(8,128)(2,1)} %copy-done.3) | copy-start | bytes 1572868
  60.8 25.3 %collective-permute-start = (bf16[8,8,16,256]{3,2,1,0:T(8,128)(2,1)S(1)}, bf16[8,8,16,256]{3,2,1,0:T(8,128)(2,1)S(1)}, u32[]{:S(2)}, u32[]{:S(2)}) collective-permute-start(bf16[8,8,16,256]{3,2,1,0:T(8,128)(2,1)S(1)} %get-tuple-element.15), channel_id=1, source_target_pairs={{0,1},{1,0},{2,3},{3,2},{4,5},{5,4},{6,7},{7,6},{8,9},{9,8},{10,11... | collective-permute-start | bytes 1572872 | tf_op jit(solution)/shard_map/ppermute | solution.py:278
  61.5 24.7 %collective-permute-start.1 = (bf16[8,8,16,256]{3,2,1,0:T(8,128)(2,1)S(1)}, bf16[8,8,16,256]{3,2,1,0:T(8,128)(2,1)S(1)}, u32[]{:S(2)}, u32[]{:S(2)}) collective-permute-start(bf16[8,8,16,256]{3,2,1,0:T(8,128)(2,1)S(1)} %get-tuple-element.16), channel_id=1, source_target_pairs={{0,2},{1,3},{2,0},{3,1},{4,6},{5,7},{6,4},{7,5},{8,10},{9,11},{10,... | collective-permute-start | bytes 1572872 | tf_op jit(solution)/shard_map/ppermute | solution.py:278
  63.6 32.7 %collective-permute-start.2 = (bf16[8,8,16,256]{3,2,1,0:T(8,128)(2,1)S(1)}, bf16[8,8,16,256]{3,2,1,0:T(8,128)(2,1)S(1)}, u32[]{:S(2)}, u32[]{:S(2)}) collective-permute-start(bf16[8,8,16,256]{3,2,1,0:T(8,128)(2,1)S(1)} %get-tuple-element.17), channel_id=1, source_target_pairs={{0,3},{1,2},{2,1},{3,0},{4,7},{5,6},{6,5},{7,4},{8,11},{9,10},{10,... | collective-permute-start | bytes 1572872 | tf_op jit(solution)/shard_map/ppermute | solution.py:278

commit v3 on v2

--- a/solution.py
+++ b/solution.py
@@ -45,17 +45,15 @@
 
 def regroup_kernel(views_ref, out_ref):
     dirs, cols, lanes = views_ref.shape
-    low_half = lax.broadcasted_iota(jnp.int32, (dirs, 128), 1) < 64
     for pair in range(lanes // 128):
-        block = views_ref[:, :, 128 * pair : 128 * (pair + 1)]
-        block = jnp.swapaxes(block, 0, 1).astype(jnp.float32)
+        block = jnp.swapaxes(views_ref[:, :, 128 * pair : 128 * (pair + 1)], 0, 1)
         for col in range(0, cols, 2):
             even, odd = block[col], block[col + 1]
-            first = jnp.where(low_half, even, pltpu.roll(odd, 64, 1))
-            second = jnp.where(low_half, pltpu.roll(even, 64, 1), odd)
             place = slice(64 * col, 64 * col + 128)
-            out_ref[2 * pair, :, place] = first.astype(jnp.bfloat16)
-            out_ref[2 * pair + 1, :, place] = second.astype(jnp.bfloat16)
+            for side in range(2):
+                own = slice(64 * side, 64 * (side + 1))
+                joined = jnp.concatenate([even[:, own], odd[:, own]], axis=1)
+                out_ref[2 * pair + side, :, place] = joined
 
 
 def regroup(views, steps=2):
@@ -110,8 +108,7 @@
             out_refs[partner][group] = block[each * partner : each * (partner + 1)]
 
 
-def fields(rays, phase_cos, phase_sin, inner, outer, step=2):
-    groups = rays.shape[1]
+def fields(rays, phase_cos, phase_sin, inner, outer, start, groups, step=2):
     count = outer.shape[0] // 2
     whole = lambda i: (0, 0)
     out_block = pl.BlockSpec((step, count // 4, 16, 256), lambda i: (i, 0, 0, 0))
@@ -119,7 +116,7 @@
         field_kernel,
         grid=(groups // step,),
         in_specs=[
-            pl.BlockSpec((4, step, 16, 2048), lambda i: (0, i, 0, 0)),
+            pl.BlockSpec((4, step, 16, 2048), lambda i: (0, start // step + i, 0, 0)),
             pl.BlockSpec((DIRS, 128), whole),
             pl.BlockSpec((DIRS, 128), whole),
             pl.BlockSpec((256, 256), whole),
@@ -135,16 +132,16 @@
     )(rays, phase_cos, phase_sin, inner, outer)
 
 
-def spectrum_kernel(filled, *refs):
-    pieces = refs[:4]
-    first_ref, twist_re_ref, twist_im_ref, second_ref, turn_re_ref, turn_im_ref = refs[4:10]
-    re_ref, im_ref, turned_ref = refs[10 + filled :]
+def spectrum_kernel(count, filled, *refs):
+    pieces, tables = refs[:count], refs[count : count + 6]
+    first_ref, twist_re_ref, twist_im_ref, second_ref, turn_re_ref, turn_im_ref = tables
+    re_ref, im_ref, turned_ref = refs[count + 6 + filled :]
     rows = turned_ref.shape[0]
 
     @pl.when(pl.program_id(0) == 0)
     def _():
         for row in range(rows):
-            signal = [p[:, row].reshape(128, SIDE) for p in pieces]
+            signal = [p[:, row].reshape(-1, SIDE) for p in pieces]
             signal = jnp.concatenate(signal, axis=0)
             section = jnp.dot(first_ref[...], signal, preferred_element_type=jnp.float32)
             section_re, section_im = section[:SIDE], section[SIDE:]
@@ -175,20 +172,20 @@
 
 
 def spectra(pieces, tables, half, filled):
-    groups, rows = pieces[0].shape[:2]
+    count, rows = len(pieces), pieces[0].shape[1]
     whole = lambda i: (0, 0)
-    piece = pl.BlockSpec((groups, rows, 16, SIDE), lambda i: (0, 0, 0, 0))
+    piece_specs = [pl.BlockSpec(p.shape, lambda i: (0, 0, 0, 0)) for p in pieces]
     square = pl.BlockSpec((SIDE, SIDE), whole)
     first = pl.BlockSpec((2 * SIDE, 2 * SIDE), whole)
     second = pl.BlockSpec((2, SIDE // 2, 2 * SIDE), lambda i: (0, i, 0))
     turn = pl.BlockSpec((SIDE // 2, SIDE), lambda i: (i, 0))
     out_block = pl.BlockSpec((8 * SIDE, 128), lambda i: (2 * half + i, 0))
     out_shape = jax.ShapeDtypeStruct((2 * 16 * SIDE, 128), jnp.float32)
-    aliases = {10 + i: i for i in range(len(filled))}
+    aliases = {count + 6 + i: i for i in range(len(filled))}
     return pl.pallas_call(
-        functools.partial(spectrum_kernel, len(filled)),
+        functools.partial(spectrum_kernel, count, len(filled)),
         grid=(2,),
-        in_specs=[piece] * 4
+        in_specs=piece_specs
         + [first, square, square, second, turn, turn]
         + [pl.BlockSpec(memory_space=pl.ANY)] * len(filled),
         out_specs=[out_block, out_block],
@@ -269,14 +266,18 @@
     turn = kernel_phase.reshape(SIDE, SIDE)
     tables = (first, twist_re, twist_im, second_table(), jnp.cos(turn), jnp.sin(turn))
     halves = []
-    for half in range(2):
+    for half, starts in enumerate(((0, 4, 8), (0, 8))):
         outer_half = outer[:, :, half].reshape(2 * 4 * 8, 2 * DIRS)
-        sending = fields(rays, phase_cos, phase_sin, inner, outer_half)
-        pieces = [sending[0], None, None, None]
-        for d in (3, 1, 2):
-            swaps = [(i, i ^ d) for i in range(4)]
-            pieces[d] = lax.ppermute(sending[d], SQUARE, swaps)
-        halves.append(pieces)
+        pieces = [[] for _ in range(4)]
+        for start, end in zip(starts[:-1], starts[1:]):
+            sending = fields(
+                rays, phase_cos, phase_sin, inner, outer_half, start, end - start
+            )
+            pieces[0].append(sending[0])
+            for d in (3, 1, 2):
+                swaps = [(i, i ^ d) for i in range(4)]
+                pieces[d].append(lax.ppermute(sending[d], SQUARE, swaps))
+        halves.append([p for partner in pieces for p in partner])
     filled = spectra(halves[0], tables, 0, ())
     flat_re, flat_im = spectra(halves[1], tables, 1, filled)
     return to_rows(flat_re), to_rows(flat_im)

time: 102 us -> 99.3 us (0.974)
  local copies, waits for them, and re-layouts: 6.13 us -> 1.53 us
  starting transfers between devices: 17.1 us -> 21.4 us
  Pallas kernels: 22.3 us -> 20.1 us
    ppermute x6 -> x9, starting transfers between devices: 6.38 us -> 10.6 us  [per_device(): pieces[d].append(lax.ppermute(sending[d], SQUARE, swaps))]
    sin x2, local copies, waits for them, and re-layouts: 3.57 us -> 1.04 us  [per_device(): jnp.sin(turn)]
    all_to_all x1, waiting for transfers between devices: 28.2 us -> 27 us  [per_device(): lax.all_to_all(sent, HOGEL_GROUP, split_axis=0, concat_axis=0, tiled=True)]
    pallas_call x2, Pallas kernels: 12.1 us -> 10.9 us  [spectra(): pl.pallas_call(functools.partial(spectrum_kernel, count, len(filled)), gr...]
    squeeze x1, local copies, waits for them, and re-layouts: 1.14 us -> 0.04 us  [per_device(): lax.dynamic_index_in_dim(table, at, axis, False)]
    ppermute x6 -> x9, waiting for transfers between devices: 25.9 us -> 27 us  [per_device(): pieces[d].append(lax.ppermute(sending[d], SQUARE, swaps))]
    pallas_call x2 -> x3, Pallas kernels: 6.61 us -> 5.92 us  [fields(): pl.pallas_call(field_kernel, grid=(groups // step,), in_specs=[pl.BlockSp...]
  transfers between devices with their start and end apart: 7 -> 10, of which waited for: 7 -> 9; matrix products, arithmetic and copies ran while one was open for 7% -> 3% of each run, Pallas kernels for 9% -> 10%
where the time goes in v3:
time: 99.3 us; the launch traced here: 99.1 us
  waiting for transfers between devices  54 us (54%)
  starting transfers between devices  21.4 us (22%)
  Pallas kernels  20.1 us (20%)
  local copies, waits for them, and re-layouts  1.53 us (2%)
  other arithmetic  1.26 us (1%)
    all_to_all x1, waiting for transfers between devices, per_device(): lax.all_to_all(sent, HOGEL_GROUP, split_axis=0, concat_axis=0, tiled=True)  27 us
    ppermute x9, waiting for transfers between devices, per_device(): pieces[d].append(lax.ppermute(sending[d], SQUARE, swaps))  27 us
    pallas_call x2, Pallas kernels, spectra(): pl.pallas_call(functools.partial(spectrum_kernel, count, len(filled)), gr...  10.9 us
    all_to_all x1, starting transfers between devices, per_device(): lax.all_to_all(sent, HOGEL_GROUP, split_axis=0, concat_axis=0, tiled=True)  10.7 us
    ppermute x9, starting transfers between devices, per_device(): pieces[d].append(lax.ppermute(sending[d], SQUARE, swaps))  10.6 us
    pallas_call x3, Pallas kernels, fields(): pl.pallas_call(field_kernel, grid=(groups // step,), in_specs=[pl.BlockSp...  5.92 us
    pallas_call x1, Pallas kernels, regroup(): pl.pallas_call(regroup_kernel, grid=(steps,), in_specs=[pl.BlockSpec((dir...  3.32 us
  transfers between devices with their start and end apart: 10, of which 9 were waited for; matrix products, arithmetic and copies ran while one was open for 3% of the time, Pallas kernels for 10%

profile of v3, /device:TPU:0, one launch (start us, length us, event | category | flops | bytes accessed | tf_op | source)
XLA Modules:
  0.0 99.1 jit_solution(11886237150952368300)
XLA Ops:
  0.6 3.3 %regroup.1 = bf16[32,16,2048]{2,1,0:T(8,128)(2,1)} custom-call(bf16[16,32,2048]{2,1,0:T(8,128)(2,1)} %views_ref.1), custom_call_target="tpu_custom_call" | custom-call | tf_op jit(solution)/shard_map/regroup/pallas_call | solution.py:62
  4.0 10.7 %all-to-all-start = ((bf16[32,16,2048]{2,1,0:T(8,128)(2,1)}), bf16[32,16,2048]{2,1,0:T(8,128)(2,1)S(1)}, u32[]{:S(2)}, u32[]{:S(2)}) async-start(bf16[32,16,2048]{2,1,0:T(8,128)(2,1)} %regroup.1), calls=%async_computation | async-start | bytes 4194304 | tf_op jit(solution)/shard_map/all_to_all | solution.py:253
  14.7 1.0 fusion.35
  17.5 27.0 %all-to-all-done = bf16[32,16,2048]{2,1,0:T(8,128)(2,1)S(1)} async-done(((bf16[32,16,2048]{2,1,0:T(8,128)(2,1)}), bf16[32,16,2048]{2,1,0:T(8,128)(2,1)S(1)}, u32[]{:S(2)}, u32[]{:S(2)}) %all-to-all-start) | async-done | bytes 2097184 | tf_op jit(solution)/shard_map/all_to_all | solution.py:253
  44.5 1.5 %fields.5 = (bf16[4,8,16,256]{3,2,1,0:T(8,128)(2,1)S(1)}, bf16[4,8,16,256]{3,2,1,0:T(8,128)(2,1)S(1)}, bf16[4,8,16,256]{3,2,1,0:T(8,128)(2,1)S(1)}, bf16[4,8,16,256]{3,2,1,0:T(8,128)(2,1)S(1)}) custom-call(bf16[4,8,16,2048]{3,2,1,0:T(8,128)(2,1)S(1)} %bitcast.21, f32[64,128]{1,0:T(8,128)S(1)} %tile.9.cos_ref, f32[64,128]{1,0:T(8,128)S(1)} %tile.21.sin_ref, ...), custom_call_target="tpu_custom_call" | custom-call | flops 2000000000 | bytes 4194304 | tf_op jit(solution)/shard_map/fields/pallas_call | solution.py:115
  46.0 0.7 collective-permute-start.4
  46.8 1.1 %collective-permute-start.6 = (bf16[4,8,16,256]{3,2,1,0:T(8,128)(2,1)S(1)}, bf16[4,8,16,256]{3,2,1,0:T(8,128)(2,1)S(1)}, u32[]{:S(2)}, u32[]{:S(2)}) collective-permute-start(bf16[4,8,16,256]{3,2,1,0:T(8,128)(2,1)S(1)} %get-tuple-element.27), channel_id=1, source_target_pairs={{0,2},{1,3},{2,0},{3,1},{4,6},{5,7},{6,4},{7,5},{8,10},{9,11},{10,... | collective-permute-start | bytes 786440 | tf_op jit(solution)/shard_map/ppermute | solution.py:279
  47.9 1.8 %collective-permute-start.8 = (bf16[4,8,16,256]{3,2,1,0:T(8,128)(2,1)S(1)}, bf16[4,8,16,256]{3,2,1,0:T(8,128)(2,1)S(1)}, u32[]{:S(2)}, u32[]{:S(2)}) collective-permute-start(bf16[4,8,16,256]{3,2,1,0:T(8,128)(2,1)S(1)} %get-tuple-element.29), channel_id=1, source_target_pairs={{0,3},{1,2},{2,1},{3,0},{4,7},{5,6},{6,5},{7,4},{8,11},{9,10},{10,... | collective-permute-start | bytes 786440 | tf_op jit(solution)/shard_map/ppermute | solution.py:279
  49.7 1.5 %fields.4 = (bf16[4,8,16,256]{3,2,1,0:T(8,128)(2,1)S(1)}, bf16[4,8,16,256]{3,2,1,0:T(8,128)(2,1)S(1)}, bf16[4,8,16,256]{3,2,1,0:T(8,128)(2,1)S(1)}, bf16[4,8,16,256]{3,2,1,0:T(8,128)(2,1)S(1)}) custom-call(bf16[4,8,16,2048]{3,2,1,0:T(8,128)(2,1)S(1)} %bitcast.22, f32[64,128]{1,0:T(8,128)S(1)} %tile.9.cos_ref, f32[64,128]{1,0:T(8,128)S(1)} %tile.21.sin_ref, ...), custom_call_target="tpu_custom_call" | custom-call | flops 2000000000 | bytes 4194304 | tf_op jit(solution)/shard_map/fields/pallas_call | solution.py:115
  51.2 0.7 collective-permute-start.3
  51.9 1.0 %collective-permute-start.5 = (bf16[4,8,16,256]{3,2,1,0:T(8,128)(2,1)S(1)}, bf16[4,8,16,256]{3,2,1,0:T(8,128)(2,1)S(1)}, u32[]{:S(2)}, u32[]{:S(2)}) collective-permute-start(bf16[4,8,16,256]{3,2,1,0:T(8,128)(2,1)S(1)} %get-tuple-element.26), channel_id=1, source_target_pairs={{0,2},{1,3},{2,0},{3,1},{4,6},{5,7},{6,4},{7,5},{8,10},{9,11},{10,... | collective-permute-start | bytes 786440 | tf_op jit(solution)/shard_map/ppermute | solution.py:279
  53.0 2.4 %collective-permute-done.4.refs_3_ = bf16[4,8,16,256]{3,2,1,0:T(8,128)(2,1)S(1)} collective-permute-done((bf16[4,8,16,256]{3,2,1,0:T(8,128)(2,1)S(1)}, bf16[4,8,16,256]{3,2,1,0:T(8,128)(2,1)S(1)}, u32[]{:S(2)}, u32[]{:S(2)}) %collective-permute-start.4) | collective-permute-done | bytes 262176 | tf_op jit(solution)/shard_map/ppermute | solution.py:279
  55.4 1.1 %collective-permute-start.7 = (bf16[4,8,16,256]{3,2,1,0:T(8,128)(2,1)S(1)}, bf16[4,8,16,256]{3,2,1,0:T(8,128)(2,1)S(1)}, u32[]{:S(2)}, u32[]{:S(2)}) collective-permute-start(bf16[4,8,16,256]{3,2,1,0:T(8,128)(2,1)S(1)} %get-tuple-element.28), channel_id=1, source_target_pairs={{0,3},{1,2},{2,1},{3,0},{4,7},{5,6},{6,5},{7,4},{8,11},{9,10},{10,... | collective-permute-start | bytes 786440 | tf_op jit(solution)/shard_map/ppermute | solution.py:279
  56.5 3.0 %fields.3 = (bf16[8,8,16,256]{3,2,1,0:T(8,128)(2,1)S(1)}, bf16[8,8,16,256]{3,2,1,0:T(8,128)(2,1)S(1)}, bf16[8,8,16,256]{3,2,1,0:T(8,128)(2,1)S(1)}, bf16[8,8,16,256]{3,2,1,0:T(8,128)(2,1)S(1)}) custom-call(bf16[4,8,16,2048]{3,2,1,0:T(8,128)(2,1)S(1)} %bitcast.23, f32[64,128]{1,0:T(8,128)S(1)} %tile.9.cos_ref, f32[64,128]{1,0:T(8,128)S(1)} %tile.21.sin_ref, ...), custom_call_target="tpu_custom_call" | custom-call | flops 2000000000 | bytes 4194304 | tf_op jit(solution)/shard_map/fields/pallas_call | solution.py:115
  59.5 1.6 %collective-permute-done.6.refs_5_ = bf16[4,8,16,256]{3,2,1,0:T(8,128)(2,1)S(1)} collective-permute-done((bf16[4,8,16,256]{3,2,1,0:T(8,128)(2,1)S(1)}, bf16[4,8,16,256]{3,2,1,0:T(8,128)(2,1)S(1)}, u32[]{:S(2)}, u32[]{:S(2)}) %collective-permute-start.6) | collective-permute-done | bytes 262176 | tf_op jit(solution)/shard_map/ppermute | solution.py:279
  61.0 2.1 %collective-permute-start = (bf16[8,8,16,256]{3,2,1,0:T(8,128)(2,1)S(1)}, bf16[8,8,16,256]{3,2,1,0:T(8,128)(2,1)S(1)}, u32[]{:S(2)}, u32[]{:S(2)}) collective-permute-start(bf16[8,8,16,256]{3,2,1,0:T(8,128)(2,1)S(1)} %get-tuple-element.19), channel_id=1, source_target_pairs={{0,1},{1,0},{2,3},{3,2},{4,5},{5,4},{6,7},{7,6},{8,9},{9,8},{10,11... | collective-permute-start | bytes 1572872 | tf_op jit(solution)/shard_map/ppermute | solution.py:279
  63.1 1.0 %collective-permute-start.1 = (bf16[8,8,16,256]{3,2,1,0:T(8,128)(2,1)S(1)}, bf16[8,8,16,256]{3,2,1,0:T(8,128)(2,1)S(1)}, u32[]{:S(2)}, u32[]{:S(2)}) collective-permute-start(bf16[8,8,16,256]{3,2,1,0:T(8,128)(2,1)S(1)} %get-tuple-element.20), channel_id=1, source_target_pairs={{0,2},{1,3},{2,0},{3,1},{4,6},{5,7},{6,4},{7,5},{8,10},{9,11},{10,... | collective-permute-start | bytes 1572872 | tf_op jit(solution)/shard_map/ppermute | solution.py:279
  64.1 2.5 %collective-permute-done.3.refs_2_ = bf16[4,8,16,256]{3,2,1,0:T(8,128)(2,1)S(1)} collective-permute-done((bf16[4,8,16,256]{3,2,1,0:T(8,128)(2,1)S(1)}, bf16[4,8,16,256]{3,2,1,0:T(8,128)(2,1)S(1)}, u32[]{:S(2)}, u32[]{:S(2)}) %collective-permute-start.3) | collective-permute-done | bytes 262176 | tf_op jit(solution)/shard_map/ppermute | solution.py:279
  66.6 1.1 %collective-permute-start.2 = (bf16[8,8,16,256]{3,2,1,0:T(8,128)(2,1)S(1)}, bf16[8,8,16,256]{3,2,1,0:T(8,128)(2,1)S(1)}, u32[]{:S(2)}, u32[]{:S(2)}) collective-permute-start(bf16[8,8,16,256]{3,2,1,0:T(8,128)(2,1)S(1)} %get-tuple-element.21), channel_id=1, source_target_pairs={{0,3},{1,2},{2,1},{3,0},{4,7},{5,6},{6,5},{7,4},{8,11},{9,10},{10,... | collective-permute-start | bytes 1572872 | tf_op jit(solution)/shard_map/ppermute | solution.py:279
  67.7 4.5 %collective-permute-done.5.refs_4_ = bf16[4,8,16,256]{3,2,1,0:T(8,128)(2,1)S(1)} collective-permute-done((bf16[4,8,16,256]{3,2,1,0:T(8,128)(2,1)S(1)}, bf16[4,8,16,256]{3,2,1,0:T(8,128)(2,1)S(1)}, u32[]{:S(2)}, u32[]{:S(2)}) %collective-permute-start.5) | collective-permute-done | bytes 262176 | tf_op jit(solution)/shard_map/ppermute | solution.py:279
  72.8 5.5 %spectra.2 = (f32[8192,128]{1,0:T(8,128)}, f32[8192,128]{1,0:T(8,128)}) custom-call(bf16[4,8,16,256]{3,2,1,0:T(8,128)(2,1)S(1)} %get-tuple-element.22.refs_0_, bf16[4,8,16,256]{3,2,1,0:T(8,128)(2,1)S(1)} %get-tuple-element.23.refs_1_, bf16[4,8,16,256]{3,2,1,0:T(8,128)(2,1)S(1)} %collective-permute-done.3.refs_2_, ...), custom_call_target="tpu_custom_call" | custom-call | flops 8000000000 | bytes 8388608 | tf_op jit(solution)/shard_map/spectra/pallas_call | solution.py:185
  78.2 5.3 %collective-permute-done.refs_1_ = bf16[8,8,16,256]{3,2,1,0:T(8,128)(2,1)S(1)} collective-permute-done((bf16[8,8,16,256]{3,2,1,0:T(8,128)(2,1)S(1)}, bf16[8,8,16,256]{3,2,1,0:T(8,128)(2,1)S(1)}, u32[]{:S(2)}, u32[]{:S(2)}) %collective-permute-start) | collective-permute-done | bytes 524320 | tf_op jit(solution)/shard_map/ppermute | solution.py:279
  83.8 9.9 %collective-permute-done.2.refs_3_ = bf16[8,8,16,256]{3,2,1,0:T(8,128)(2,1)S(1)} collective-permute-done((bf16[8,8,16,256]{3,2,1,0:T(8,128)(2,1)S(1)}, bf16[8,8,16,256]{3,2,1,0:T(8,128)(2,1)S(1)}, u32[]{:S(2)}, u32[]{:S(2)}) %collective-permute-start.2) | collective-permute-done | bytes 524320 | tf_op jit(solution)/shard_map/ppermute | solution.py:279
  93.7 5.4 %spectra.3 = (f32[8192,128]{1,0:T(8,128)}, f32[8192,128]{1,0:T(8,128)}) custom-call(bf16[8,8,16,256]{3,2,1,0:T(8,128)(2,1)S(1)} %get-tuple-element.18.refs_0_, bf16[8,8,16,256]{3,2,1,0:T(8,128)(2,1)S(1)} %collective-permute-done.refs_1_, bf16[8,8,16,256]{3,2,1,0:T(8,128)(2,1)S(1)} %collective-permute-done.1.refs_2_, ...), custom_call_target="tpu_custom_call", output_to_operand_aliasing={{0}: (10, {}), {1}: (11, {})} | custom-call | flops 8000000000 | bytes 8388608 | tf_op jit(solution)/shard_map/spectra/pallas_call | solution.py:185
  (36 shorter events, 2.6 us)
Async XLA Ops:
  0.6 14.1 %copy-start.4 = (f32[65536]{0:T(1024)S(1)}, f32[65536]{0:T(1024)}, u32[]{:S(2)}) copy-start(f32[65536]{0:T(1024)} %param.9) | copy-start | bytes 786436
  0.6 15.1 %copy-start.5 = (s32[64,64]{1,0:T(8,128)S(1)}, s32[64,64]{1,0:T(8,128)}, u32[]{:S(2)}) copy-start(s32[64,64]{1,0:T(8,128)} %param.8) | copy-start | bytes 49156
  4.0 40.6 %all-to-all-start = ((bf16[32,16,2048]{2,1,0:T(8,128)(2,1)}), bf16[32,16,2048]{2,1,0:T(8,128)(2,1)S(1)}, u32[]{:S(2)}, u32[]{:S(2)}) async-start(bf16[32,16,2048]{2,1,0:T(8,128)(2,1)} %regroup.1), calls=%async_computation | async-start | bytes 4194304 | tf_op jit(solution)/shard_map/all_to_all | solution.py:253
  16.2 30.6 %copy-start.3 = (bf16[4,512,128]{2,1,0:T(8,128)(2,1)S(1)}, bf16[4,512,128]{2,1,0:T(8,128)(2,1)}, u32[]{:S(2)}) copy-start(bf16[4,512,128]{2,1,0:T(8,128)(2,1)} %constant.74.clone) | copy-start | bytes 1572868
  46.0 9.3 %collective-permute-start.4 = (bf16[4,8,16,256]{3,2,1,0:T(8,128)(2,1)S(1)}, bf16[4,8,16,256]{3,2,1,0:T(8,128)(2,1)S(1)}, u32[]{:S(2)}, u32[]{:S(2)}) collective-permute-start(bf16[4,8,16,256]{3,2,1,0:T(8,128)(2,1)S(1)} %get-tuple-element.25), channel_id=1, source_target_pairs={{0,1},{1,0},{2,3},{3,2},{4,5},{5,4},{6,7},{7,6},{8,9},{9,8},{10,11... | collective-permute-start | bytes 786440 | tf_op jit(solution)/shard_map/ppermute | solution.py:279
  46.8 14.3 %collective-permute-start.6 = (bf16[4,8,16,256]{3,2,1,0:T(8,128)(2,1)S(1)}, bf16[4,8,16,256]{3,2,1,0:T(8,128)(2,1)S(1)}, u32[]{:S(2)}, u32[]{:S(2)}) collective-permute-start(bf16[4,8,16,256]{3,2,1,0:T(8,128)(2,1)S(1)} %get-tuple-element.27), channel_id=1, source_target_pairs={{0,2},{1,3},{2,0},{3,1},{4,6},{5,7},{6,4},{7,5},{8,10},{9,11},{10,... | collective-permute-start | bytes 786440 | tf_op jit(solution)/shard_map/ppermute | solution.py:279
  47.9 15.2 %collective-permute-start.8 = (bf16[4,8,16,256]{3,2,1,0:T(8,128)(2,1)S(1)}, bf16[4,8,16,256]{3,2,1,0:T(8,128)(2,1)S(1)}, u32[]{:S(2)}, u32[]{:S(2)}) collective-permute-start(bf16[4,8,16,256]{3,2,1,0:T(8,128)(2,1)S(1)} %get-tuple-element.29), channel_id=1, source_target_pairs={{0,3},{1,2},{2,1},{3,0},{4,7},{5,6},{6,5},{7,4},{8,11},{9,10},{10,... | collective-permute-start | bytes 786440 | tf_op jit(solution)/shard_map/ppermute | solution.py:279
  51.2 15.4 %collective-permute-start.3 = (bf16[4,8,16,256]{3,2,1,0:T(8,128)(2,1)S(1)}, bf16[4,8,16,256]{3,2,1,0:T(8,128)(2,1)S(1)}, u32[]{:S(2)}, u32[]{:S(2)}) collective-permute-start(bf16[4,8,16,256]{3,2,1,0:T(8,128)(2,1)S(1)} %get-tuple-element.24), channel_id=1, source_target_pairs={{0,1},{1,0},{2,3},{3,2},{4,5},{5,4},{6,7},{7,6},{8,9},{9,8},{10,11... | collective-permute-start | bytes 786440 | tf_op jit(solution)/shard_map/ppermute | solution.py:279
  51.9 20.3 %collective-permute-start.5 = (bf16[4,8,16,256]{3,2,1,0:T(8,128)(2,1)S(1)}, bf16[4,8,16,256]{3,2,1,0:T(8,128)(2,1)S(1)}, u32[]{:S(2)}, u32[]{:S(2)}) collective-permute-start(bf16[4,8,16,256]{3,2,1,0:T(8,128)(2,1)S(1)} %get-tuple-element.26), channel_id=1, source_target_pairs={{0,2},{1,3},{2,0},{3,1},{4,6},{5,7},{6,4},{7,5},{8,10},{9,11},{10,... | collective-permute-start | bytes 786440 | tf_op jit(solution)/shard_map/ppermute | solution.py:279
  55.4 17.4 %collective-permute-start.7 = (bf16[4,8,16,256]{3,2,1,0:T(8,128)(2,1)S(1)}, bf16[4,8,16,256]{3,2,1,0:T(8,128)(2,1)S(1)}, u32[]{:S(2)}, u32[]{:S(2)}) collective-permute-start(bf16[4,8,16,256]{3,2,1,0:T(8,128)(2,1)S(1)} %get-tuple-element.28), channel_id=1, source_target_pairs={{0,3},{1,2},{2,1},{3,0},{4,7},{5,6},{6,5},{7,4},{8,11},{9,10},{10,... | collective-permute-start | bytes 786440 | tf_op jit(solution)/shard_map/ppermute | solution.py:279
  56.4 16.3 %copy-start = (bf16[2,256,512]{2,1,0:T(8,128)(2,1)S(1)}, bf16[2,256,512]{2,1,0:T(8,128)(2,1)}, u32[]{:S(2)}) copy-start(bf16[2,256,512]{2,1,0:T(8,128)(2,1)} %constant.77.clone.refs_11_.refs_7_) | copy-start | bytes 1572868
  56.4 16.3 %copy-start.1 = (f32[256,256]{1,0:T(8,128)S(1)}, f32[256,256]{1,0:T(8,128)}, u32[]{:S(2)}) copy-start(f32[256,256]{1,0:T(8,128)} %constant.76.clone.refs_10_.refs_6_) | copy-start | bytes 786436
  56.4 16.3 %copy-start.2 = (f32[256,256]{1,0:T(8,128)S(1)}, f32[256,256]{1,0:T(8,128)}, u32[]{:S(2)}) copy-start(f32[256,256]{1,0:T(8,128)} %constant.75.clone.refs_9_.refs_5_) | copy-start | bytes 786436
  61.0 22.5 %collective-permute-start = (bf16[8,8,16,256]{3,2,1,0:T(8,128)(2,1)S(1)}, bf16[8,8,16,256]{3,2,1,0:T(8,128)(2,1)S(1)}, u32[]{:S(2)}, u32[]{:S(2)}) collective-permute-start(bf16[8,8,16,256]{3,2,1,0:T(8,128)(2,1)S(1)} %get-tuple-element.19), channel_id=1, source_target_pairs={{0,1},{1,0},{2,3},{3,2},{4,5},{5,4},{6,7},{7,6},{8,9},{9,8},{10,11... | collective-permute-start | bytes 1572872 | tf_op jit(solution)/shard_map/ppermute | solution.py:279
  63.1 20.6 %collective-permute-start.1 = (bf16[8,8,16,256]{3,2,1,0:T(8,128)(2,1)S(1)}, bf16[8,8,16,256]{3,2,1,0:T(8,128)(2,1)S(1)}, u32[]{:S(2)}, u32[]{:S(2)}) collective-permute-start(bf16[8,8,16,256]{3,2,1,0:T(8,128)(2,1)S(1)} %get-tuple-element.20), channel_id=1, source_target_pairs={{0,2},{1,3},{2,0},{3,1},{4,6},{5,7},{6,4},{7,5},{8,10},{9,11},{10,... | collective-permute-start | bytes 1572872 | tf_op jit(solution)/shard_map/ppermute | solution.py:279
  66.6 27.0 %collective-permute-start.2 = (bf16[8,8,16,256]{3,2,1,0:T(8,128)(2,1)S(1)}, bf16[8,8,16,256]{3,2,1,0:T(8,128)(2,1)S(1)}, u32[]{:S(2)}, u32[]{:S(2)}) collective-permute-start(bf16[8,8,16,256]{3,2,1,0:T(8,128)(2,1)S(1)} %get-tuple-element.21), channel_id=1, source_target_pairs={{0,3},{1,2},{2,1},{3,0},{4,7},{5,6},{6,5},{7,4},{8,11},{9,10},{10,... | collective-permute-start | bytes 1572872 | tf_op jit(solution)/shard_map/ppermute | solution.py:279

commit v4 on v3

--- a/solution.py
+++ b/solution.py
@@ -15,7 +15,11 @@
 SIDE = 256
 VIEW = ("xh", "co")
 COL = ("y", "zh", "zl", "xl")
-HOGEL_GROUP = ("xh", "co", "y", "zh")
+HOGEL_ORDER = (
+    29, 5, 15, 12, 24, 14, 31, 11, 16, 30, 13, 8, 4, 1, 6, 23,
+    0, 21, 26, 2, 22, 28, 19, 17, 3, 10, 7, 9, 18, 27, 25, 20,
+)
+RANK_OF = tuple(HOGEL_ORDER.index(row) for row in range(len(HOGEL_ORDER)))
 SQUARE = ("zl", "xl")
 VMEM_BYTES = 40 * 1024 * 1024
 
@@ -53,34 +57,37 @@
             for side in range(2):
                 own = slice(64 * side, 64 * (side + 1))
                 joined = jnp.concatenate([even[:, own], odd[:, own]], axis=1)
-                out_ref[2 * pair + side, :, place] = joined
+                out_ref[RANK_OF[2 * pair + side], :, place] = joined
 
 
 def regroup(views, steps=2):
     dirs, cols, merged = views.shape
-    lanes = merged // steps
+    each = cols // steps
     return pl.pallas_call(
         regroup_kernel,
         grid=(steps,),
-        in_specs=[pl.BlockSpec((dirs, cols, lanes), lambda i: (0, 0, i))],
-        out_specs=pl.BlockSpec((lanes // 64, dirs, cols * 64), lambda i: (i, 0, 0)),
+        in_specs=[pl.BlockSpec((dirs, each, merged), lambda i: (0, i, 0))],
+        out_specs=pl.BlockSpec((merged // 64, dirs, each * 64), lambda i: (0, 0, i)),
         out_shape=jax.ShapeDtypeStruct((merged // 64, dirs, cols * 64), jnp.bfloat16),
         compiler_params=params(60 * 1024 * 1024),
         name="regroup",
     )(views)
 
 
-def field_kernel(rays_ref, cos_ref, sin_ref, inner_ref, outer_ref, *out_refs):
+def field_kernel(place_ref, *refs):
+    rays_refs, out_refs = refs[:-8], refs[-4:]
+    cos_ref, sin_ref, inner_ref, outer_ref = refs[-8:-4]
     phase_cos = cos_ref[...]
     phase_sin = sin_ref[...]
     inner = inner_ref[...]
     outer = outer_ref[...]
     count = outer.shape[0] // 2
     each = count // 4
-    groups = rays_ref.shape[1]
+    groups = len(rays_refs) // 4
     stacked = []
     for group in range(groups):
-        rays = rays_ref[:, group].reshape(DIRS, 32 * DIRS)
+        own = rays_refs[4 * group : 4 * (group + 1)]
+        rays = jnp.concatenate([r[0] for r in own], axis=0)
 
         def wave(tile):
             amplitude = rays[:, 128 * tile : 128 * (tile + 1)].astype(jnp.float32)
@@ -110,26 +117,45 @@
 
 def fields(rays, phase_cos, phase_sin, inner, outer, start, groups, step=2):
     count = outer.shape[0] // 2
-    whole = lambda i: (0, 0)
-    out_block = pl.BlockSpec((step, count // 4, 16, 256), lambda i: (i, 0, 0, 0))
+    whole = lambda i, place: (0, 0)
+    out_block = pl.BlockSpec(
+        (step, count // 4, 16, 256), lambda i, place: (i, 0, 0, 0)
+    )
+    out_shape = jax.ShapeDtypeStruct((groups, count // 4, 16, 256), jnp.bfloat16)
+
+    def source(group, view):
+        at = lambda i, place: (place[8 * view + start + step * i + group], 0, 0)
+        return pl.BlockSpec((1, 16, 2048), at)
+
+    sources = [source(group, view) for group in range(step) for view in range(4)]
     return pl.pallas_call(
         field_kernel,
-        grid=(groups // step,),
-        in_specs=[
-            pl.BlockSpec((4, step, 16, 2048), lambda i: (0, start // step + i, 0, 0)),
-            pl.BlockSpec((DIRS, 128), whole),
-            pl.BlockSpec((DIRS, 128), whole),
-            pl.BlockSpec((256, 256), whole),
-            pl.BlockSpec((2 * count, 128), whole),
-        ],
-        out_specs=[out_block] * 4,
-        out_shape=[jax.ShapeDtypeStruct((groups, count // 4, 16, 256), jnp.bfloat16)] * 4,
+        grid_spec=pltpu.PrefetchScalarGridSpec(
+            num_scalar_prefetch=1,
+            grid=(groups // step,),
+            in_specs=sources
+            + [
+                pl.BlockSpec((DIRS, 128), whole),
+                pl.BlockSpec((DIRS, 128), whole),
+                pl.BlockSpec((256, 256), whole),
+                pl.BlockSpec((2 * count, 128), whole),
+            ],
+            out_specs=[out_block] * 4,
+        ),
+        out_shape=[out_shape] * 4,
         compiler_params=params(),
         cost_estimate=pl.CostEstimate(
             flops=2 * 10**9, bytes_accessed=4 * 2**20, transcendentals=0
         ),
         name="fields",
-    )(rays, phase_cos, phase_sin, inner, outer)
+    )(
+        jnp.asarray(RANK_OF, jnp.int32),
+        *[rays] * len(sources),
+        phase_cos,
+        phase_sin,
+        inner,
+        outer,
+    )
 
 
 def spectrum_kernel(count, filled, *refs):
@@ -248,10 +274,15 @@
     return tiles.transpose(0, 3, 1, 2, 4).reshape(rows, SIDE * SIDE)
 
 
+def hogel_groups():
+    return [[4 * row + at for row in HOGEL_ORDER] for at in range(4)]
+
+
 def per_device(views, phases, kernel_phase):
     sent = regroup(views)
-    rays = lax.all_to_all(sent, HOGEL_GROUP, split_axis=0, concat_axis=0, tiled=True)
-    rays = rays.reshape(4, 8, 16, 2048)
+    rays = lax.all_to_all(
+        sent, VIEW + COL, 0, 0, axis_index_groups=hogel_groups(), tiled=True
+    )
     angles = phases.astype(jnp.float32) * (2.0 * math.pi / PHASES)
     phase_cos = jnp.tile(jnp.cos(angles), (1, 2))
     phase_sin = jnp.tile(jnp.sin(angles), (1, 2))

time: 99.3 us -> 97.3 us (0.980)
  waiting for transfers between devices: 54 us -> 49.3 us
  Pallas kernels: 20.1 us -> 21.9 us
    all_to_all x1, waiting for transfers between devices: 27 us -> 22.6 us  [per_device(): lax.all_to_all(sent, VIEW + COL, 0, 0, axis_index_groups=hogel_groups(),...]
    all_to_all x1, starting transfers between devices: 10.7 us -> 12.4 us  [per_device(): lax.all_to_all(sent, VIEW + COL, 0, 0, axis_index_groups=hogel_groups(),...]
    pallas_call x3, Pallas kernels: 5.92 us -> 7.23 us  [fields(): pl.pallas_call(field_kernel, grid_spec=pltpu.PrefetchScalarGridSpec(num_s...]
  transfers between devices with their start and end apart: 10 -> 10, of which waited for: 9 -> 8; matrix products, arithmetic and copies ran while one was open for 3% -> 3% of each run, Pallas kernels for 10% -> 11%
where the time goes in v4:
time: 97.3 us; the launch traced here: 97.1 us
  waiting for transfers between devices  49.3 us (51%)
  starting transfers between devices  22.2 us (23%)
  Pallas kernels  21.9 us (23%)
  local copies, waits for them, and re-layouts  1.55 us (2%)
  other arithmetic  1.26 us (1%)
    ppermute x9, waiting for transfers between devices, per_device(): pieces[d].append(lax.ppermute(sending[d], SQUARE, swaps))  26.7 us
    all_to_all x1, waiting for transfers between devices, per_device(): lax.all_to_all(sent, VIEW + COL, 0, 0, axis_index_groups=hogel_groups(),...  22.6 us
    all_to_all x1, starting transfers between devices, per_device(): lax.all_to_all(sent, VIEW + COL, 0, 0, axis_index_groups=hogel_groups(),...  12.4 us
    pallas_call x2, Pallas kernels, spectra(): pl.pallas_call(functools.partial(spectrum_kernel, count, len(filled)), gr...  11.3 us
    ppermute x9, starting transfers between devices, per_device(): pieces[d].append(lax.ppermute(sending[d], SQUARE, swaps))  9.83 us
    pallas_call x3, Pallas kernels, fields(): pl.pallas_call(field_kernel, grid_spec=pltpu.PrefetchScalarGridSpec(num_s...  7.23 us
    pallas_call x1, Pallas kernels, regroup(): pl.pallas_call(regroup_kernel, grid=(steps,), in_specs=[pl.BlockSpec((dir...  3.33 us
  transfers between devices with their start and end apart: 10, of which 8 were waited for; matrix products, arithmetic and copies ran while one was open for 3% of the time, Pallas kernels for 11%

profile of v4, /device:TPU:0, one launch (start us, length us, event | category | flops | bytes accessed | tf_op | source)
XLA Modules:
  0.0 97.1 jit_solution(5208964422372632308)
XLA Ops:
  0.6 3.3 %regroup.1 = bf16[32,16,2048]{2,1,0:T(8,128)(2,1)} custom-call(bf16[16,32,2048]{2,1,0:T(8,128)(2,1)} %views_ref.1), custom_call_target="tpu_custom_call" | custom-call | tf_op jit(solution)/shard_map/regroup/pallas_call | solution.py:66
  4.0 12.4 %all-to-all-start = ((bf16[32,16,2048]{2,1,0:T(8,128)(2,1)}), bf16[32,16,2048]{2,1,0:T(8,128)(2,1)S(1)}, u32[]{:S(2)}, u32[]{:S(2)}) async-start(bf16[32,16,2048]{2,1,0:T(8,128)(2,1)} %regroup.1), calls=%async_computation | async-start | bytes 4194304 | tf_op jit(solution)/shard_map/all_to_all | solution.py:283
  16.4 1.0 fusion.35
  18.7 0.2 multiply_convert_fusion
  19.2 22.6 %all-to-all-done.refs_0_.refs_1_.refs_2_.refs_3_.refs_4_.refs_5_.refs_6_.refs_7_ = bf16[32,16,2048]{2,1,0:T(8,128)(2,1)S(1)} async-done(((bf16[32,16,2048]{2,1,0:T(8,128)(2,1)}), bf16[32,16,2048]{2,1,0:T(8,128)(2,1)S(1)}, u32[]{:S(2)}, u32[]{:S(2)}) %all-to-all-start) | async-done | bytes 2097184 | tf_op jit(solution)/shard_map/all_to_all | solution.py:283
  41.8 1.9 %fields.5 = (bf16[4,8,16,256]{3,2,1,0:T(8,128)(2,1)S(1)}, bf16[4,8,16,256]{3,2,1,0:T(8,128)(2,1)S(1)}, bf16[4,8,16,256]{3,2,1,0:T(8,128)(2,1)S(1)}, bf16[4,8,16,256]{3,2,1,0:T(8,128)(2,1)S(1)}) custom-call(s32[32]{0:T(128)S(1)} %copy-done, bf16[32,16,2048]{2,1,0:T(8,128)(2,1)S(1)} %all-to-all-done.refs_0_.refs_1_.refs_2_.refs_3_.refs_4_.refs_5_.refs_6_.refs_7_, ...), custom_call_target="tpu_custom_call" | custom-call | flops 2000000000 | bytes 4194304 | tf_op jit(solution)/shard_map/fields/pallas_call | solution.py:131
  43.9 1.1 %collective-permute-start.6 = (bf16[4,8,16,256]{3,2,1,0:T(8,128)(2,1)S(1)}, bf16[4,8,16,256]{3,2,1,0:T(8,128)(2,1)S(1)}, u32[]{:S(2)}, u32[]{:S(2)}) collective-permute-start(bf16[4,8,16,256]{3,2,1,0:T(8,128)(2,1)S(1)} %get-tuple-element.27), channel_id=1, source_target_pairs={{0,2},{1,3},{2,0},{3,1},{4,6},{5,7},{6,4},{7,5},{8,10},{9,11},{10,... | collective-permute-start | bytes 786440 | tf_op jit(solution)/shard_map/ppermute | solution.py:310
  45.0 2.4 %collective-permute-start.8 = (bf16[4,8,16,256]{3,2,1,0:T(8,128)(2,1)S(1)}, bf16[4,8,16,256]{3,2,1,0:T(8,128)(2,1)S(1)}, u32[]{:S(2)}, u32[]{:S(2)}) collective-permute-start(bf16[4,8,16,256]{3,2,1,0:T(8,128)(2,1)S(1)} %get-tuple-element.29), channel_id=1, source_target_pairs={{0,3},{1,2},{2,1},{3,0},{4,7},{5,6},{6,5},{7,4},{8,11},{9,10},{10,... | collective-permute-start | bytes 786440 | tf_op jit(solution)/shard_map/ppermute | solution.py:310
  47.4 1.9 %fields.4 = (bf16[4,8,16,256]{3,2,1,0:T(8,128)(2,1)S(1)}, bf16[4,8,16,256]{3,2,1,0:T(8,128)(2,1)S(1)}, bf16[4,8,16,256]{3,2,1,0:T(8,128)(2,1)S(1)}, bf16[4,8,16,256]{3,2,1,0:T(8,128)(2,1)S(1)}) custom-call(s32[32]{0:T(128)S(1)} %copy-done, bf16[32,16,2048]{2,1,0:T(8,128)(2,1)S(1)} %all-to-all-done.refs_0_.refs_1_.refs_2_.refs_3_.refs_4_.refs_5_.refs_6_.refs_7_, ...), custom_call_target="tpu_custom_call" | custom-call | flops 2000000000 | bytes 4194304 | tf_op jit(solution)/shard_map/fields/pallas_call | solution.py:131
  49.5 1.1 %collective-permute-start.5 = (bf16[4,8,16,256]{3,2,1,0:T(8,128)(2,1)S(1)}, bf16[4,8,16,256]{3,2,1,0:T(8,128)(2,1)S(1)}, u32[]{:S(2)}, u32[]{:S(2)}) collective-permute-start(bf16[4,8,16,256]{3,2,1,0:T(8,128)(2,1)S(1)} %get-tuple-element.26), channel_id=1, source_target_pairs={{0,2},{1,3},{2,0},{3,1},{4,6},{5,7},{6,4},{7,5},{8,10},{9,11},{10,... | collective-permute-start | bytes 786440 | tf_op jit(solution)/shard_map/ppermute | solution.py:310
  50.6 2.5 %collective-permute-done.4.refs_3_ = bf16[4,8,16,256]{3,2,1,0:T(8,128)(2,1)S(1)} collective-permute-done((bf16[4,8,16,256]{3,2,1,0:T(8,128)(2,1)S(1)}, bf16[4,8,16,256]{3,2,1,0:T(8,128)(2,1)S(1)}, u32[]{:S(2)}, u32[]{:S(2)}) %collective-permute-start.4) | collective-permute-done | bytes 262176 | tf_op jit(solution)/shard_map/ppermute | solution.py:310
  53.1 0.4 collective-permute-start.7
  53.6 3.3 %fields.3 = (bf16[8,8,16,256]{3,2,1,0:T(8,128)(2,1)S(1)}, bf16[8,8,16,256]{3,2,1,0:T(8,128)(2,1)S(1)}, bf16[8,8,16,256]{3,2,1,0:T(8,128)(2,1)S(1)}, bf16[8,8,16,256]{3,2,1,0:T(8,128)(2,1)S(1)}) custom-call(s32[32]{0:T(128)S(1)} %copy-done, bf16[32,16,2048]{2,1,0:T(8,128)(2,1)S(1)} %all-to-all-done.refs_0_.refs_1_.refs_2_.refs_3_.refs_4_.refs_5_.refs_6_.refs_7_, ...), custom_call_target="tpu_custom_call" | custom-call | flops 2000000000 | bytes 4194304 | tf_op jit(solution)/shard_map/fields/pallas_call | solution.py:131
  56.9 0.5 collective-permute-done.6.refs_5_
  57.4 3.2 %collective-permute-start = (bf16[8,8,16,256]{3,2,1,0:T(8,128)(2,1)S(1)}, bf16[8,8,16,256]{3,2,1,0:T(8,128)(2,1)S(1)}, u32[]{:S(2)}, u32[]{:S(2)}) collective-permute-start(bf16[8,8,16,256]{3,2,1,0:T(8,128)(2,1)S(1)} %get-tuple-element.19), channel_id=1, source_target_pairs={{0,1},{1,0},{2,3},{3,2},{4,5},{5,4},{6,7},{7,6},{8,9},{9,8},{10,11... | collective-permute-start | bytes 1572872 | tf_op jit(solution)/shard_map/ppermute | solution.py:310
  60.6 1.0 %collective-permute-start.1 = (bf16[8,8,16,256]{3,2,1,0:T(8,128)(2,1)S(1)}, bf16[8,8,16,256]{3,2,1,0:T(8,128)(2,1)S(1)}, u32[]{:S(2)}, u32[]{:S(2)}) collective-permute-start(bf16[8,8,16,256]{3,2,1,0:T(8,128)(2,1)S(1)} %get-tuple-element.20), channel_id=1, source_target_pairs={{0,2},{1,3},{2,0},{3,1},{4,6},{5,7},{6,4},{7,5},{8,10},{9,11},{10,... | collective-permute-start | bytes 1572872 | tf_op jit(solution)/shard_map/ppermute | solution.py:310
  61.6 2.7 %collective-permute-done.3.refs_2_ = bf16[4,8,16,256]{3,2,1,0:T(8,128)(2,1)S(1)} collective-permute-done((bf16[4,8,16,256]{3,2,1,0:T(8,128)(2,1)S(1)}, bf16[4,8,16,256]{3,2,1,0:T(8,128)(2,1)S(1)}, u32[]{:S(2)}, u32[]{:S(2)}) %collective-permute-start.3) | collective-permute-done | bytes 262176 | tf_op jit(solution)/shard_map/ppermute | solution.py:310
  64.3 0.4 collective-permute-start.2
  64.8 3.9 %collective-permute-done.5.refs_4_ = bf16[4,8,16,256]{3,2,1,0:T(8,128)(2,1)S(1)} collective-permute-done((bf16[4,8,16,256]{3,2,1,0:T(8,128)(2,1)S(1)}, bf16[4,8,16,256]{3,2,1,0:T(8,128)(2,1)S(1)}, u32[]{:S(2)}, u32[]{:S(2)}) %collective-permute-start.5) | collective-permute-done | bytes 262176 | tf_op jit(solution)/shard_map/ppermute | solution.py:310
  68.6 1.8 %collective-permute-done.7.refs_6_ = bf16[4,8,16,256]{3,2,1,0:T(8,128)(2,1)S(1)} collective-permute-done((bf16[4,8,16,256]{3,2,1,0:T(8,128)(2,1)S(1)}, bf16[4,8,16,256]{3,2,1,0:T(8,128)(2,1)S(1)}, u32[]{:S(2)}, u32[]{:S(2)}) %collective-permute-start.7) | collective-permute-done | bytes 262176 | tf_op jit(solution)/shard_map/ppermute | solution.py:310
  70.5 5.7 %spectra.2 = (f32[8192,128]{1,0:T(8,128)}, f32[8192,128]{1,0:T(8,128)}) custom-call(bf16[4,8,16,256]{3,2,1,0:T(8,128)(2,1)S(1)} %get-tuple-element.22.refs_0_, bf16[4,8,16,256]{3,2,1,0:T(8,128)(2,1)S(1)} %get-tuple-element.23.refs_1_, bf16[4,8,16,256]{3,2,1,0:T(8,128)(2,1)S(1)} %collective-permute-done.3.refs_2_, ...), custom_call_target="tpu_custom_call" | custom-call | flops 8000000000 | bytes 8388608 | tf_op jit(solution)/shard_map/spectra/pallas_call | solution.py:211
  76.1 5.1 %collective-permute-done.refs_1_ = bf16[8,8,16,256]{3,2,1,0:T(8,128)(2,1)S(1)} collective-permute-done((bf16[8,8,16,256]{3,2,1,0:T(8,128)(2,1)S(1)}, bf16[8,8,16,256]{3,2,1,0:T(8,128)(2,1)S(1)}, u32[]{:S(2)}, u32[]{:S(2)}) %collective-permute-start) | collective-permute-done | bytes 524320 | tf_op jit(solution)/shard_map/ppermute | solution.py:310
  81.2 10.2 %collective-permute-done.2.refs_3_ = bf16[8,8,16,256]{3,2,1,0:T(8,128)(2,1)S(1)} collective-permute-done((bf16[8,8,16,256]{3,2,1,0:T(8,128)(2,1)S(1)}, bf16[8,8,16,256]{3,2,1,0:T(8,128)(2,1)S(1)}, u32[]{:S(2)}, u32[]{:S(2)}) %collective-permute-start.2) | collective-permute-done | bytes 524320 | tf_op jit(solution)/shard_map/ppermute | solution.py:310
  91.5 5.6 %spectra.3 = (f32[8192,128]{1,0:T(8,128)}, f32[8192,128]{1,0:T(8,128)}) custom-call(bf16[8,8,16,256]{3,2,1,0:T(8,128)(2,1)S(1)} %get-tuple-element.18.refs_0_, bf16[8,8,16,256]{3,2,1,0:T(8,128)(2,1)S(1)} %collective-permute-done.refs_1_, bf16[8,8,16,256]{3,2,1,0:T(8,128)(2,1)S(1)} %collective-permute-done.1.refs_2_, ...), custom_call_target="tpu_custom_call", output_to_operand_aliasing={{0}: (10, {}), {1}: (11, {})} | custom-call | flops 8000000000 | bytes 8388608 | tf_op jit(solution)/shard_map/spectra/pallas_call | solution.py:211
  (38 shorter events, 1.8 us)
Async XLA Ops:
  0.6 15.8 %copy-start.5 = (f32[65536]{0:T(1024)S(1)}, f32[65536]{0:T(1024)}, u32[]{:S(2)}) copy-start(f32[65536]{0:T(1024)} %param.12) | copy-start | bytes 786436
  0.6 16.8 %copy-start.6 = (s32[64,64]{1,0:T(8,128)S(1)}, s32[64,64]{1,0:T(8,128)}, u32[]{:S(2)}) copy-start(s32[64,64]{1,0:T(8,128)} %param.11) | copy-start | bytes 49156
  4.0 37.8 %copy-start = (s32[32]{0:T(128)S(1)}, s32[32]{0:T(128)}, u32[]{:S(2)}) copy-start(s32[32]{0:T(128)} %constant.80.clone.place_ref) | copy-start | bytes 388
  4.0 37.8 %all-to-all-start = ((bf16[32,16,2048]{2,1,0:T(8,128)(2,1)}), bf16[32,16,2048]{2,1,0:T(8,128)(2,1)S(1)}, u32[]{:S(2)}, u32[]{:S(2)}) async-start(bf16[32,16,2048]{2,1,0:T(8,128)(2,1)} %regroup.1), calls=%async_computation | async-start | bytes 4194304 | tf_op jit(solution)/shard_map/all_to_all | solution.py:283
  41.8 2.1 %copy-start.4 = (bf16[4,512,128]{2,1,0:T(8,128)(2,1)S(1)}, bf16[4,512,128]{2,1,0:T(8,128)(2,1)}, u32[]{:S(2)}) copy-start(bf16[4,512,128]{2,1,0:T(8,128)(2,1)} %constant.76.clone) | copy-start | bytes 1572868
  43.7 9.3 %collective-permute-start.4 = (bf16[4,8,16,256]{3,2,1,0:T(8,128)(2,1)S(1)}, bf16[4,8,16,256]{3,2,1,0:T(8,128)(2,1)S(1)}, u32[]{:S(2)}, u32[]{:S(2)}) collective-permute-start(bf16[4,8,16,256]{3,2,1,0:T(8,128)(2,1)S(1)} %get-tuple-element.25), channel_id=1, source_target_pairs={{0,1},{1,0},{2,3},{3,2},{4,5},{5,4},{6,7},{7,6},{8,9},{9,8},{10,11... | collective-permute-start | bytes 786440 | tf_op jit(solution)/shard_map/ppermute | solution.py:310
  43.9 13.5 %collective-permute-start.6 = (bf16[4,8,16,256]{3,2,1,0:T(8,128)(2,1)S(1)}, bf16[4,8,16,256]{3,2,1,0:T(8,128)(2,1)S(1)}, u32[]{:S(2)}, u32[]{:S(2)}) collective-permute-start(bf16[4,8,16,256]{3,2,1,0:T(8,128)(2,1)S(1)} %get-tuple-element.27), channel_id=1, source_target_pairs={{0,2},{1,3},{2,0},{3,1},{4,6},{5,7},{6,4},{7,5},{8,10},{9,11},{10,... | collective-permute-start | bytes 786440 | tf_op jit(solution)/shard_map/ppermute | solution.py:310
  45.0 15.6 %collective-permute-start.8 = (bf16[4,8,16,256]{3,2,1,0:T(8,128)(2,1)S(1)}, bf16[4,8,16,256]{3,2,1,0:T(8,128)(2,1)S(1)}, u32[]{:S(2)}, u32[]{:S(2)}) collective-permute-start(bf16[4,8,16,256]{3,2,1,0:T(8,128)(2,1)S(1)} %get-tuple-element.29), channel_id=1, source_target_pairs={{0,3},{1,2},{2,1},{3,0},{4,7},{5,6},{6,5},{7,4},{8,11},{9,10},{10,... | collective-permute-start | bytes 786440 | tf_op jit(solution)/shard_map/ppermute | solution.py:310
  49.4 15.0 %collective-permute-start.3 = (bf16[4,8,16,256]{3,2,1,0:T(8,128)(2,1)S(1)}, bf16[4,8,16,256]{3,2,1,0:T(8,128)(2,1)S(1)}, u32[]{:S(2)}, u32[]{:S(2)}) collective-permute-start(bf16[4,8,16,256]{3,2,1,0:T(8,128)(2,1)S(1)} %get-tuple-element.24), channel_id=1, source_target_pairs={{0,1},{1,0},{2,3},{3,2},{4,5},{5,4},{6,7},{7,6},{8,9},{9,8},{10,11... | collective-permute-start | bytes 786440 | tf_op jit(solution)/shard_map/ppermute | solution.py:310
  49.5 19.1 %collective-permute-start.5 = (bf16[4,8,16,256]{3,2,1,0:T(8,128)(2,1)S(1)}, bf16[4,8,16,256]{3,2,1,0:T(8,128)(2,1)S(1)}, u32[]{:S(2)}, u32[]{:S(2)}) collective-permute-start(bf16[4,8,16,256]{3,2,1,0:T(8,128)(2,1)S(1)} %get-tuple-element.26), channel_id=1, source_target_pairs={{0,2},{1,3},{2,0},{3,1},{4,6},{5,7},{6,4},{7,5},{8,10},{9,11},{10,... | collective-permute-start | bytes 786440 | tf_op jit(solution)/shard_map/ppermute | solution.py:310
  53.1 17.4 %collective-permute-start.7 = (bf16[4,8,16,256]{3,2,1,0:T(8,128)(2,1)S(1)}, bf16[4,8,16,256]{3,2,1,0:T(8,128)(2,1)S(1)}, u32[]{:S(2)}, u32[]{:S(2)}) collective-permute-start(bf16[4,8,16,256]{3,2,1,0:T(8,128)(2,1)S(1)} %get-tuple-element.28), channel_id=1, source_target_pairs={{0,3},{1,2},{2,1},{3,0},{4,7},{5,6},{6,5},{7,4},{8,11},{9,10},{10,... | collective-permute-start | bytes 786440 | tf_op jit(solution)/shard_map/ppermute | solution.py:310
  53.5 16.9 %copy-start.1 = (bf16[2,256,512]{2,1,0:T(8,128)(2,1)S(1)}, bf16[2,256,512]{2,1,0:T(8,128)(2,1)}, u32[]{:S(2)}) copy-start(bf16[2,256,512]{2,1,0:T(8,128)(2,1)} %constant.79.clone.refs_11_.refs_7_) | copy-start | bytes 1572868
  53.6 16.9 %copy-start.2 = (f32[256,256]{1,0:T(8,128)S(1)}, f32[256,256]{1,0:T(8,128)}, u32[]{:S(2)}) copy-start(f32[256,256]{1,0:T(8,128)} %constant.78.clone.refs_10_.refs_6_) | copy-start | bytes 786436
  53.6 16.9 %copy-start.3 = (f32[256,256]{1,0:T(8,128)S(1)}, f32[256,256]{1,0:T(8,128)}, u32[]{:S(2)}) copy-start(f32[256,256]{1,0:T(8,128)} %constant.77.clone.refs_9_.refs_5_) | copy-start | bytes 786436
  57.4 23.8 %collective-permute-start = (bf16[8,8,16,256]{3,2,1,0:T(8,128)(2,1)S(1)}, bf16[8,8,16,256]{3,2,1,0:T(8,128)(2,1)S(1)}, u32[]{:S(2)}, u32[]{:S(2)}) collective-permute-start(bf16[8,8,16,256]{3,2,1,0:T(8,128)(2,1)S(1)} %get-tuple-element.19), channel_id=1, source_target_pairs={{0,1},{1,0},{2,3},{3,2},{4,5},{5,4},{6,7},{7,6},{8,9},{9,8},{10,11... | collective-permute-start | bytes 1572872 | tf_op jit(solution)/shard_map/ppermute | solution.py:310
  60.6 20.6 %collective-permute-start.1 = (bf16[8,8,16,256]{3,2,1,0:T(8,128)(2,1)S(1)}, bf16[8,8,16,256]{3,2,1,0:T(8,128)(2,1)S(1)}, u32[]{:S(2)}, u32[]{:S(2)}) collective-permute-start(bf16[8,8,16,256]{3,2,1,0:T(8,128)(2,1)S(1)} %get-tuple-element.20), channel_id=1, source_target_pairs={{0,2},{1,3},{2,0},{3,1},{4,6},{5,7},{6,4},{7,5},{8,10},{9,11},{10,... | collective-permute-start | bytes 1572872 | tf_op jit(solution)/shard_map/ppermute | solution.py:310
  64.3 27.1 %collective-permute-start.2 = (bf16[8,8,16,256]{3,2,1,0:T(8,128)(2,1)S(1)}, bf16[8,8,16,256]{3,2,1,0:T(8,128)(2,1)S(1)}, u32[]{:S(2)}, u32[]{:S(2)}) collective-permute-start(bf16[8,8,16,256]{3,2,1,0:T(8,128)(2,1)S(1)} %get-tuple-element.21), channel_id=1, source_target_pairs={{0,3},{1,2},{2,1},{3,0},{4,7},{5,6},{6,5},{7,4},{8,11},{9,10},{10,... | collective-permute-start | bytes 1572872 | tf_op jit(solution)/shard_map/ppermute | solution.py:310

commit v5 on v3

--- a/solution.py
+++ b/solution.py
@@ -15,7 +15,11 @@
 SIDE = 256
 VIEW = ("xh", "co")
 COL = ("y", "zh", "zl", "xl")
-HOGEL_GROUP = ("xh", "co", "y", "zh")
+HOGEL_ORDER = (
+    29, 5, 15, 12, 24, 14, 31, 11, 16, 30, 13, 8, 4, 1, 6, 23,
+    0, 21, 26, 2, 22, 28, 19, 17, 3, 10, 7, 9, 18, 27, 25, 20,
+)
+RANK_OF = tuple(HOGEL_ORDER.index(row) for row in range(len(HOGEL_ORDER)))
 SQUARE = ("zl", "xl")
 VMEM_BYTES = 40 * 1024 * 1024
 
@@ -53,34 +57,37 @@
             for side in range(2):
                 own = slice(64 * side, 64 * (side + 1))
                 joined = jnp.concatenate([even[:, own], odd[:, own]], axis=1)
-                out_ref[2 * pair + side, :, place] = joined
+                out_ref[RANK_OF[2 * pair + side], :, place] = joined
 
 
 def regroup(views, steps=2):
     dirs, cols, merged = views.shape
-    lanes = merged // steps
+    each = cols // steps
     return pl.pallas_call(
         regroup_kernel,
         grid=(steps,),
-        in_specs=[pl.BlockSpec((dirs, cols, lanes), lambda i: (0, 0, i))],
-        out_specs=pl.BlockSpec((lanes // 64, dirs, cols * 64), lambda i: (i, 0, 0)),
+        in_specs=[pl.BlockSpec((dirs, each, merged), lambda i: (0, i, 0))],
+        out_specs=pl.BlockSpec((merged // 64, dirs, each * 64), lambda i: (0, 0, i)),
         out_shape=jax.ShapeDtypeStruct((merged // 64, dirs, cols * 64), jnp.bfloat16),
         compiler_params=params(60 * 1024 * 1024),
         name="regroup",
     )(views)
 
 
-def field_kernel(rays_ref, cos_ref, sin_ref, inner_ref, outer_ref, *out_refs):
+def field_kernel(
+    start, groups, place_ref, rays_ref, cos_ref, sin_ref, inner_ref, outer_ref, *out_refs
+):
+    begin = start + groups * pl.program_id(0)
     phase_cos = cos_ref[...]
     phase_sin = sin_ref[...]
     inner = inner_ref[...]
     outer = outer_ref[...]
     count = outer.shape[0] // 2
     each = count // 4
-    groups = rays_ref.shape[1]
     stacked = []
     for group in range(groups):
-        rays = rays_ref[:, group].reshape(DIRS, 32 * DIRS)
+        own = [rays_ref[place_ref[8 * view + begin + group]] for view in range(4)]
+        rays = jnp.concatenate(own, axis=0)
 
         def wave(tile):
             amplitude = rays[:, 128 * tile : 128 * (tile + 1)].astype(jnp.float32)
@@ -109,34 +116,31 @@
 
 
 def fields(rays, phase_cos, phase_sin, inner, outer, start, groups, step=2):
-    count = outer.shape[0] // 2
-    whole = lambda i: (0, 0)
-    out_block = pl.BlockSpec((step, count // 4, 16, 256), lambda i: (i, 0, 0, 0))
+    each = outer.shape[0] // 8
+    in_vmem = pl.BlockSpec(memory_space=pltpu.VMEM)
+    out_block = pl.BlockSpec((step, each, 16, 256), lambda i: (i, 0, 0, 0))
+    out_shape = jax.ShapeDtypeStruct((groups, each, 16, 256), jnp.bfloat16)
     return pl.pallas_call(
-        field_kernel,
+        functools.partial(field_kernel, start, step),
         grid=(groups // step,),
-        in_specs=[
-            pl.BlockSpec((4, step, 16, 2048), lambda i: (0, start // step + i, 0, 0)),
-            pl.BlockSpec((DIRS, 128), whole),
-            pl.BlockSpec((DIRS, 128), whole),
-            pl.BlockSpec((256, 256), whole),
-            pl.BlockSpec((2 * count, 128), whole),
-        ],
+        in_specs=[pl.BlockSpec(memory_space=pltpu.SMEM)] + [in_vmem] * 5,
         out_specs=[out_block] * 4,
-        out_shape=[jax.ShapeDtypeStruct((groups, count // 4, 16, 256), jnp.bfloat16)] * 4,
+        out_shape=[out_shape] * 4,
         compiler_params=params(),
         cost_estimate=pl.CostEstimate(
             flops=2 * 10**9, bytes_accessed=4 * 2**20, transcendentals=0
         ),
         name="fields",
-    )(rays, phase_cos, phase_sin, inner, outer)
-
-
-def spectrum_kernel(count, filled, *refs):
+    )(jnp.asarray(RANK_OF, jnp.int32), rays, phase_cos, phase_sin, inner, outer)
+
+
+def spectrum_kernel(count, early, filled, keep, *refs):
     pieces, tables = refs[:count], refs[count : count + 6]
     first_ref, twist_re_ref, twist_im_ref, second_ref, turn_re_ref, turn_im_ref = tables
-    re_ref, im_ref, turned_ref = refs[count + 6 + filled :]
+    early_refs = refs[count + 6 : count + 6 + early]
+    re_ref, im_ref, turned_ref = refs[count + 6 + early + filled :]
     rows = turned_ref.shape[0]
+    half = SIDE // 2
 
     @pl.when(pl.program_id(0) == 0)
     def _():
@@ -151,7 +155,13 @@
             turned_ref[row, :, :SIDE] = turned_re.astype(jnp.bfloat16)
             turned_ref[row, :, SIDE:] = turned_im.astype(jnp.bfloat16)
 
-    half = SIDE // 2
+    def place_row(row, out_re, out_im):
+        for side in range(2):
+            lanes = slice(128 * side, 128 * (side + 1))
+            place = pl.ds(8 * side + row, half, stride=16)
+            re_ref[place, :] = out_re[:, lanes]
+            im_ref[place, :] = out_im[:, lanes]
+
     second = second_ref[...].reshape(2 * half, 2 * SIDE)
     for row in range(rows):
         final = lax.dot_general(
@@ -164,29 +174,39 @@
         turn_re, turn_im = turn_re_ref[...], turn_im_ref[...]
         out_re = final_re * turn_re - final_im * turn_im
         out_im = final_re * turn_im + final_im * turn_re
-        for side in range(2):
-            lanes = slice(128 * side, 128 * (side + 1))
-            place = pl.ds(8 * side + row, half, stride=16)
-            re_ref[place, :] = out_re[:, lanes]
-            im_ref[place, :] = out_im[:, lanes]
-
-
-def spectra(pieces, tables, half, filled):
+        if keep:
+            re_ref[row] = out_re
+            im_ref[row] = out_im
+        else:
+            place_row(8 - rows + row, out_re, out_im)
+    if early:
+        for row in range(8 - rows):
+            place_row(row, early_refs[0][row], early_refs[1][row])
+
+
+def spectra(pieces, tables, half, early=(), filled=()):
     count, rows = len(pieces), pieces[0].shape[1]
+    keep = half is None
     whole = lambda i: (0, 0)
     piece_specs = [pl.BlockSpec(p.shape, lambda i: (0, 0, 0, 0)) for p in pieces]
     square = pl.BlockSpec((SIDE, SIDE), whole)
     first = pl.BlockSpec((2 * SIDE, 2 * SIDE), whole)
     second = pl.BlockSpec((2, SIDE // 2, 2 * SIDE), lambda i: (0, i, 0))
     turn = pl.BlockSpec((SIDE // 2, SIDE), lambda i: (i, 0))
-    out_block = pl.BlockSpec((8 * SIDE, 128), lambda i: (2 * half + i, 0))
-    out_shape = jax.ShapeDtypeStruct((2 * 16 * SIDE, 128), jnp.float32)
-    aliases = {count + 6 + i: i for i in range(len(filled))}
+    kept_spec = lambda n: pl.BlockSpec((n, SIDE // 2, SIDE), lambda i: (0, i, 0))
+    if keep:
+        out_block = kept_spec(rows)
+        out_shape = jax.ShapeDtypeStruct((rows, SIDE, SIDE), jnp.float32)
+    else:
+        out_block = pl.BlockSpec((8 * SIDE, 128), lambda i: (2 * half + i, 0))
+        out_shape = jax.ShapeDtypeStruct((2 * 16 * SIDE, 128), jnp.float32)
+    aliases = {count + 6 + len(early) + i: i for i in range(len(filled))}
     return pl.pallas_call(
-        functools.partial(spectrum_kernel, count, len(filled)),
+        functools.partial(spectrum_kernel, count, len(early), len(filled), keep),
         grid=(2,),
         in_specs=piece_specs
         + [first, square, square, second, turn, turn]
+        + [kept_spec(8 - rows)] * len(early)
         + [pl.BlockSpec(memory_space=pl.ANY)] * len(filled),
         out_specs=[out_block, out_block],
         out_shape=[out_shape, out_shape],
@@ -194,10 +214,10 @@
         input_output_aliases=aliases,
         compiler_params=params(),
         cost_estimate=pl.CostEstimate(
-            flops=8 * 10**9, bytes_accessed=8 * 2**20, transcendentals=0
+            flops=10**9 * rows, bytes_accessed=2**20 * rows, transcendentals=0
         ),
         name="spectra",
-    )(*pieces, *tables, *filled)
+    )(*pieces, *tables, *early, *filled)
 
 
 def inner_outer_tables():
@@ -213,7 +233,7 @@
             jnp.concatenate([table_im, table_re], axis=1),
         ]
     )
-    return inner, outer.reshape(2, 4, 2, 8, 2 * DIRS)
+    return inner, outer.reshape(2, 4, 16, 2 * DIRS)
 
 
 def first_tables():
@@ -248,10 +268,15 @@
     return tiles.transpose(0, 3, 1, 2, 4).reshape(rows, SIDE * SIDE)
 
 
+def hogel_groups():
+    return [[4 * row + at for row in HOGEL_ORDER] for at in range(4)]
+
+
 def per_device(views, phases, kernel_phase):
     sent = regroup(views)
-    rays = lax.all_to_all(sent, HOGEL_GROUP, split_axis=0, concat_axis=0, tiled=True)
-    rays = rays.reshape(4, 8, 16, 2048)
+    rays = lax.all_to_all(
+        sent, VIEW + COL, 0, 0, axis_index_groups=hogel_groups(), tiled=True
+    )
     angles = phases.astype(jnp.float32) * (2.0 * math.pi / PHASES)
     phase_cos = jnp.tile(jnp.cos(angles), (1, 2))
     phase_sin = jnp.tile(jnp.sin(angles), (1, 2))
@@ -265,21 +290,22 @@
     twist_re, twist_im = twist_tables()
     turn = kernel_phase.reshape(SIDE, SIDE)
     tables = (first, twist_re, twist_im, second_table(), jnp.cos(turn), jnp.sin(turn))
-    halves = []
-    for half, starts in enumerate(((0, 4, 8), (0, 8))):
-        outer_half = outer[:, :, half].reshape(2 * 4 * 8, 2 * DIRS)
+    parts = []
+    for rows, starts in (((0, 8), (0, 4, 8)), ((8, 12), (0, 8)), ((12, 16), (0, 8))):
+        outer_part = outer[:, :, rows[0] : rows[1]].reshape(-1, 2 * DIRS)
         pieces = [[] for _ in range(4)]
         for start, end in zip(starts[:-1], starts[1:]):
             sending = fields(
-                rays, phase_cos, phase_sin, inner, outer_half, start, end - start
+                rays, phase_cos, phase_sin, inner, outer_part, start, end - start
             )
             pieces[0].append(sending[0])
             for d in (3, 1, 2):
                 swaps = [(i, i ^ d) for i in range(4)]
                 pieces[d].append(lax.ppermute(sending[d], SQUARE, swaps))
-        halves.append([p for partner in pieces for p in partner])
-    filled = spectra(halves[0], tables, 0, ())
-    flat_re, flat_im = spectra(halves[1], tables, 1, filled)
+        parts.append([p for partner in pieces for p in partner])
+    filled = spectra(parts[0], tables, 0)
+    early = spectra(parts[1], tables, None)
+    flat_re, flat_im = spectra(parts[2], tables, 1, early, filled)
     return to_rows(flat_re), to_rows(flat_im)
 
 

time: 99.3 us -> 96.2 us (0.969)
  waiting for transfers between devices: 54 us -> 39.7 us
  Pallas kernels: 20.1 us -> 25.5 us
  starting transfers between devices: 21.4 us -> 26 us
  local copies, waits for them, and re-layouts: 1.53 us -> 2.63 us
    ppermute x9 -> x12, waiting for transfers between devices: 27 us -> 18.3 us  [per_device(): pieces[d].append(lax.ppermute(sending[d], SQUARE, swaps))]
    all_to_all x1, waiting for transfers between devices: 27 us -> 21.4 us  [per_device(): lax.all_to_all(sent, VIEW + COL, 0, 0, axis_index_groups=hogel_groups(),...]
    pallas_call x5 -> x7, Pallas kernels: 16.8 us -> 22.2 us  [the longest x3 12.1 us: spectra(): pl.pallas_call(functools.partial(spectrum_kernel, count, len(early), len(...]
    ppermute x9 -> x12, starting transfers between devices: 10.6 us -> 13.6 us  [per_device(): pieces[d].append(lax.ppermute(sending[d], SQUARE, swaps))]
    all_to_all x1, starting transfers between devices: 10.7 us -> 12.4 us  [per_device(): lax.all_to_all(sent, VIEW + COL, 0, 0, axis_index_groups=hogel_groups(),...]
    squeeze x1, local copies, waits for them, and re-layouts: 0.04 us -> 1.14 us  [per_device(): lax.dynamic_index_in_dim(table, at, axis, False)]
  transfers between devices with their start and end apart: 10 -> 13, of which waited for: 9 -> 8; matrix products, arithmetic and copies ran while one was open for 3% -> 4% of each run, Pallas kernels for 10% -> 16%
where the time goes in v5:
time: 96.2 us; the launch traced here: 96 us
  waiting for transfers between devices  39.7 us (41%)
  starting transfers between devices  26 us (27%)
  Pallas kernels  25.5 us (27%)
  local copies, waits for them, and re-layouts  2.63 us (3%)
  other arithmetic  1.26 us (1%)
    all_to_all x1, waiting for transfers between devices, per_device(): lax.all_to_all(sent, VIEW + COL, 0, 0, axis_index_groups=hogel_groups(),...  21.4 us
    ppermute x12, waiting for transfers between devices, per_device(): pieces[d].append(lax.ppermute(sending[d], SQUARE, swaps))  18.3 us
    ppermute x12, starting transfers between devices, per_device(): pieces[d].append(lax.ppermute(sending[d], SQUARE, swaps))  13.6 us
    all_to_all x1, starting transfers between devices, per_device(): lax.all_to_all(sent, VIEW + COL, 0, 0, axis_index_groups=hogel_groups(),...  12.4 us
    pallas_call x3, Pallas kernels, spectra(): pl.pallas_call(functools.partial(spectrum_kernel, count, len(early), len(...  12.1 us
    pallas_call x4, Pallas kernels, fields(): pl.pallas_call(functools.partial(field_kernel, start, step), grid=(groups...  10.1 us
    pallas_call x1, Pallas kernels, regroup(): pl.pallas_call(regroup_kernel, grid=(steps,), in_specs=[pl.BlockSpec((dir...  3.33 us
  transfers between devices with their start and end apart: 13, of which 8 were waited for; matrix products, arithmetic and copies ran while one was open for 4% of the time, Pallas kernels for 16%

profile of v5, /device:TPU:0, one launch (start us, length us, event | category | flops | bytes accessed | tf_op | source)
XLA Modules:
  0.0 96.0 jit_solution(4932823791574589918)
XLA Ops:
  0.6 3.3 %regroup.1 = bf16[32,16,2048]{2,1,0:T(8,128)(2,1)} custom-call(bf16[16,32,2048]{2,1,0:T(8,128)(2,1)} %views_ref.1), custom_call_target="tpu_custom_call" | custom-call | tf_op jit(solution)/shard_map/regroup/pallas_call | solution.py:66
  4.0 12.4 %all-to-all-start = ((bf16[32,16,2048]{2,1,0:T(8,128)(2,1)}), bf16[32,16,2048]{2,1,0:T(8,128)(2,1)S(1)}, u32[]{:S(2)}, u32[]{:S(2)}) async-start(bf16[32,16,2048]{2,1,0:T(8,128)(2,1)} %regroup.1), calls=%async_computation | async-start | bytes 4194304 | tf_op jit(solution)/shard_map/all_to_all | solution.py:277
  19.2 1.1 %dynamic-slice_bitcast_fusion.3 = (bf16[512,128]{1,0:T(8,128)(2,1)S(1)}, bf16[512,128]{1,0:T(8,128)(2,1)S(1)}, bf16[512,128]{1,0:T(8,128)(2,1)S(1)}, bf16[512,128]{1,0:T(8,128)(2,1)S(1)}) fusion(bf16[4,512,128]{2,1,0:T(8,128)(2,1)} %constant.71.clone, s32[]{:T(128)S(6)} %select_n.57, s32[]{:T(128)S(6)} %select_n.58, s32[]{:T(128)S(6)} %select_n.60, ...), kind=kLoop, calls=%fused_computation.31 | loop fusion | bytes 1048592 | tf_op jit(solution)/shard_map/jit(dynamic_index_in_dim)/squeeze | solution.py:286
  20.4 21.4 %all-to-all-done.rays_ref = bf16[32,16,2048]{2,1,0:T(8,128)(2,1)S(1)} async-done(((bf16[32,16,2048]{2,1,0:T(8,128)(2,1)}), bf16[32,16,2048]{2,1,0:T(8,128)(2,1)S(1)}, u32[]{:S(2)}, u32[]{:S(2)}) %all-to-all-start) | async-done | bytes 2097184 | tf_op jit(solution)/shard_map/all_to_all | solution.py:277
  41.8 1.9 %fields.7 = (bf16[4,8,16,256]{3,2,1,0:T(8,128)(2,1)S(1)}, bf16[4,8,16,256]{3,2,1,0:T(8,128)(2,1)S(1)}, bf16[4,8,16,256]{3,2,1,0:T(8,128)(2,1)S(1)}, bf16[4,8,16,256]{3,2,1,0:T(8,128)(2,1)S(1)}) custom-call(s32[32]{0:T(128)S(1)} %copy-done.3, bf16[32,16,2048]{2,1,0:T(8,128)(2,1)S(1)} %all-to-all-done.rays_ref, f32[64,128]{1,0:T(8,128)S(1)} %tile.9.cos_ref, ...), custom_call_target="tpu_custom_call" | custom-call | flops 2000000000 | bytes 4194304 | tf_op jit(solution)/shard_map/fields/pallas_call | solution.py:123
  43.9 1.1 %collective-permute-start.9 = (bf16[4,8,16,256]{3,2,1,0:T(8,128)(2,1)S(1)}, bf16[4,8,16,256]{3,2,1,0:T(8,128)(2,1)S(1)}, u32[]{:S(2)}, u32[]{:S(2)}) collective-permute-start(bf16[4,8,16,256]{3,2,1,0:T(8,128)(2,1)S(1)} %get-tuple-element.39), channel_id=1, source_target_pairs={{0,2},{1,3},{2,0},{3,1},{4,6},{5,7},{6,4},{7,5},{8,10},{9,11},{10,... | collective-permute-start | bytes 786440 | tf_op jit(solution)/shard_map/ppermute | solution.py:304
  45.0 2.5 %collective-permute-start.11 = (bf16[4,8,16,256]{3,2,1,0:T(8,128)(2,1)S(1)}, bf16[4,8,16,256]{3,2,1,0:T(8,128)(2,1)S(1)}, u32[]{:S(2)}, u32[]{:S(2)}) collective-permute-start(bf16[4,8,16,256]{3,2,1,0:T(8,128)(2,1)S(1)} %get-tuple-element.41), channel_id=1, source_target_pairs={{0,3},{1,2},{2,1},{3,0},{4,7},{5,6},{6,5},{7,4},{8,11},{9,10},{10,... | collective-permute-start | bytes 786440 | tf_op jit(solution)/shard_map/ppermute | solution.py:304
  47.4 1.9 %fields.6 = (bf16[4,8,16,256]{3,2,1,0:T(8,128)(2,1)S(1)}, bf16[4,8,16,256]{3,2,1,0:T(8,128)(2,1)S(1)}, bf16[4,8,16,256]{3,2,1,0:T(8,128)(2,1)S(1)}, bf16[4,8,16,256]{3,2,1,0:T(8,128)(2,1)S(1)}) custom-call(s32[32]{0:T(128)S(1)} %copy-done.3, bf16[32,16,2048]{2,1,0:T(8,128)(2,1)S(1)} %all-to-all-done.rays_ref, f32[64,128]{1,0:T(8,128)S(1)} %tile.9.cos_ref, ...), custom_call_target="tpu_custom_call" | custom-call | flops 2000000000 | bytes 4194304 | tf_op jit(solution)/shard_map/fields/pallas_call | solution.py:123
  49.5 1.1 %collective-permute-start.8 = (bf16[4,8,16,256]{3,2,1,0:T(8,128)(2,1)S(1)}, bf16[4,8,16,256]{3,2,1,0:T(8,128)(2,1)S(1)}, u32[]{:S(2)}, u32[]{:S(2)}) collective-permute-start(bf16[4,8,16,256]{3,2,1,0:T(8,128)(2,1)S(1)} %get-tuple-element.38), channel_id=1, source_target_pairs={{0,2},{1,3},{2,0},{3,1},{4,6},{5,7},{6,4},{7,5},{8,10},{9,11},{10,... | collective-permute-start | bytes 786440 | tf_op jit(solution)/shard_map/ppermute | solution.py:304
  50.5 2.5 %collective-permute-done.7.refs_3_ = bf16[4,8,16,256]{3,2,1,0:T(8,128)(2,1)S(1)} collective-permute-done((bf16[4,8,16,256]{3,2,1,0:T(8,128)(2,1)S(1)}, bf16[4,8,16,256]{3,2,1,0:T(8,128)(2,1)S(1)}, u32[]{:S(2)}, u32[]{:S(2)}) %collective-permute-start.7) | collective-permute-done | bytes 262176 | tf_op jit(solution)/shard_map/ppermute | solution.py:304
  53.5 3.1 %fields.5 = (bf16[8,4,16,256]{3,2,1,0:T(8,128)(2,1)S(1)}, bf16[8,4,16,256]{3,2,1,0:T(8,128)(2,1)S(1)}, bf16[8,4,16,256]{3,2,1,0:T(8,128)(2,1)S(1)}, bf16[8,4,16,256]{3,2,1,0:T(8,128)(2,1)S(1)}) custom-call(s32[32]{0:T(128)S(1)} %copy-done.3, bf16[32,16,2048]{2,1,0:T(8,128)(2,1)S(1)} %all-to-all-done.rays_ref, f32[64,128]{1,0:T(8,128)S(1)} %tile.9.cos_ref, ...), custom_call_target="tpu_custom_call" | custom-call | flops 2000000000 | bytes 4194304 | tf_op jit(solution)/shard_map/fields/pallas_call | solution.py:123
  56.6 3.1 %fields.4 = (bf16[8,4,16,256]{3,2,1,0:T(8,128)(2,1)S(1)}, bf16[8,4,16,256]{3,2,1,0:T(8,128)(2,1)S(1)}, bf16[8,4,16,256]{3,2,1,0:T(8,128)(2,1)S(1)}, bf16[8,4,16,256]{3,2,1,0:T(8,128)(2,1)S(1)}) custom-call(s32[32]{0:T(128)S(1)} %copy-done.3, bf16[32,16,2048]{2,1,0:T(8,128)(2,1)S(1)} %all-to-all-done.rays_ref, f32[64,128]{1,0:T(8,128)S(1)} %tile.9.cos_ref, ...), custom_call_target="tpu_custom_call" | custom-call | flops 2000000000 | bytes 4194304 | tf_op jit(solution)/shard_map/fields/pallas_call | solution.py:123
  59.7 2.1 %collective-permute-start.3 = (bf16[8,4,16,256]{3,2,1,0:T(8,128)(2,1)S(1)}, bf16[8,4,16,256]{3,2,1,0:T(8,128)(2,1)S(1)}, u32[]{:S(2)}, u32[]{:S(2)}) collective-permute-start(bf16[8,4,16,256]{3,2,1,0:T(8,128)(2,1)S(1)} %get-tuple-element.29), channel_id=1, source_target_pairs={{0,1},{1,0},{2,3},{3,2},{4,5},{5,4},{6,7},{7,6},{8,9},{9,8},{10,11... | collective-permute-start | bytes 786440 | tf_op jit(solution)/shard_map/ppermute | solution.py:304
  61.9 1.0 %collective-permute-start.4 = (bf16[8,4,16,256]{3,2,1,0:T(8,128)(2,1)S(1)}, bf16[8,4,16,256]{3,2,1,0:T(8,128)(2,1)S(1)}, u32[]{:S(2)}, u32[]{:S(2)}) collective-permute-start(bf16[8,4,16,256]{3,2,1,0:T(8,128)(2,1)S(1)} %get-tuple-element.30), channel_id=1, source_target_pairs={{0,2},{1,3},{2,0},{3,1},{4,6},{5,7},{6,4},{7,5},{8,10},{9,11},{10,... | collective-permute-start | bytes 786440 | tf_op jit(solution)/shard_map/ppermute | solution.py:304
  62.9 1.4 %collective-permute-done.6.refs_2_ = bf16[4,8,16,256]{3,2,1,0:T(8,128)(2,1)S(1)} collective-permute-done((bf16[4,8,16,256]{3,2,1,0:T(8,128)(2,1)S(1)}, bf16[4,8,16,256]{3,2,1,0:T(8,128)(2,1)S(1)}, u32[]{:S(2)}, u32[]{:S(2)}) %collective-permute-start.6) | collective-permute-done | bytes 262176 | tf_op jit(solution)/shard_map/ppermute | solution.py:304
  64.8 3.7 %collective-permute-done.8.refs_4_ = bf16[4,8,16,256]{3,2,1,0:T(8,128)(2,1)S(1)} collective-permute-done((bf16[4,8,16,256]{3,2,1,0:T(8,128)(2,1)S(1)}, bf16[4,8,16,256]{3,2,1,0:T(8,128)(2,1)S(1)}, u32[]{:S(2)}, u32[]{:S(2)}) %collective-permute-start.8) | collective-permute-done | bytes 262176 | tf_op jit(solution)/shard_map/ppermute | solution.py:304
  68.5 3.3 %collective-permute-start = (bf16[8,4,16,256]{3,2,1,0:T(8,128)(2,1)S(1)}, bf16[8,4,16,256]{3,2,1,0:T(8,128)(2,1)S(1)}, u32[]{:S(2)}, u32[]{:S(2)}) collective-permute-start(bf16[8,4,16,256]{3,2,1,0:T(8,128)(2,1)S(1)} %get-tuple-element.25), channel_id=1, source_target_pairs={{0,1},{1,0},{2,3},{3,2},{4,5},{5,4},{6,7},{7,6},{8,9},{9,8},{10,11... | collective-permute-start | bytes 786440 | tf_op jit(solution)/shard_map/ppermute | solution.py:304
  71.8 1.0 %collective-permute-start.1 = (bf16[8,4,16,256]{3,2,1,0:T(8,128)(2,1)S(1)}, bf16[8,4,16,256]{3,2,1,0:T(8,128)(2,1)S(1)}, u32[]{:S(2)}, u32[]{:S(2)}) collective-permute-start(bf16[8,4,16,256]{3,2,1,0:T(8,128)(2,1)S(1)} %get-tuple-element.26), channel_id=1, source_target_pairs={{0,2},{1,3},{2,0},{3,1},{4,6},{5,7},{6,4},{7,5},{8,10},{9,11},{10,... | collective-permute-start | bytes 786440 | tf_op jit(solution)/shard_map/ppermute | solution.py:304
  72.8 5.5 %spectra.4 = (f32[8192,128]{1,0:T(8,128)}, f32[8192,128]{1,0:T(8,128)}) custom-call(bf16[4,8,16,256]{3,2,1,0:T(8,128)(2,1)S(1)} %get-tuple-element.34.refs_0_, bf16[4,8,16,256]{3,2,1,0:T(8,128)(2,1)S(1)} %get-tuple-element.35.refs_1_, bf16[4,8,16,256]{3,2,1,0:T(8,128)(2,1)S(1)} %collective-permute-done.6.refs_2_, ...), custom_call_target="tpu_custom_call" | custom-call | flops 8000000000 | bytes 8388608 | tf_op jit(solution)/shard_map/spectra/pallas_call | solution.py:204
  79.7 2.0 %collective-permute-done.5.refs_3_ = bf16[8,4,16,256]{3,2,1,0:T(8,128)(2,1)S(1)} collective-permute-done((bf16[8,4,16,256]{3,2,1,0:T(8,128)(2,1)S(1)}, bf16[8,4,16,256]{3,2,1,0:T(8,128)(2,1)S(1)}, u32[]{:S(2)}, u32[]{:S(2)}) %collective-permute-start.5) | collective-permute-done | bytes 262176 | tf_op jit(solution)/shard_map/ppermute | solution.py:304
  81.7 2.1 %spectra.3 = (f32[4,256,256]{2,1,0:T(8,128)S(1)}, f32[4,256,256]{2,1,0:T(8,128)S(1)}) custom-call(bf16[8,4,16,256]{3,2,1,0:T(8,128)(2,1)S(1)} %get-tuple-element.28.refs_0_, bf16[8,4,16,256]{3,2,1,0:T(8,128)(2,1)S(1)} %collective-permute-done.3.refs_1_, bf16[8,4,16,256]{3,2,1,0:T(8,128)(2,1)S(1)} %collective-permute-done.4.refs_2_, ...), custom_call_target="tpu_custom_call" | custom-call | flops 4000000000 | bytes 4194304 | tf_op jit(solution)/shard_map/spectra/pallas_call | solution.py:204
  83.8 3.1 %collective-permute-done.refs_1_ = bf16[8,4,16,256]{3,2,1,0:T(8,128)(2,1)S(1)} collective-permute-done((bf16[8,4,16,256]{3,2,1,0:T(8,128)(2,1)S(1)}, bf16[8,4,16,256]{3,2,1,0:T(8,128)(2,1)S(1)}, u32[]{:S(2)}, u32[]{:S(2)}) %collective-permute-start) | collective-permute-done | bytes 262176 | tf_op jit(solution)/shard_map/ppermute | solution.py:304
  86.9 4.6 %collective-permute-done.2.refs_3_ = bf16[8,4,16,256]{3,2,1,0:T(8,128)(2,1)S(1)} collective-permute-done((bf16[8,4,16,256]{3,2,1,0:T(8,128)(2,1)S(1)}, bf16[8,4,16,256]{3,2,1,0:T(8,128)(2,1)S(1)}, u32[]{:S(2)}, u32[]{:S(2)}) %collective-permute-start.2) | collective-permute-done | bytes 262176 | tf_op jit(solution)/shard_map/ppermute | solution.py:304
  91.5 4.5 %spectra.5 = (f32[8192,128]{1,0:T(8,128)}, f32[8192,128]{1,0:T(8,128)}) custom-call(bf16[8,4,16,256]{3,2,1,0:T(8,128)(2,1)S(1)} %get-tuple-element.24.refs_0_, bf16[8,4,16,256]{3,2,1,0:T(8,128)(2,1)S(1)} %collective-permute-done.refs_1_, bf16[8,4,16,256]{3,2,1,0:T(8,128)(2,1)S(1)} %collective-permute-done.1.refs_2_, ...), custom_call_target="tpu_custom_call", output_to_operand_aliasing={{0}: (12, {}), {1}: (13, {})} | custom-call | flops 4000000000 | bytes 4194304 | tf_op jit(solution)/shard_map/spectra/pallas_call | solution.py:204
  (44 shorter events, 5.1 us)
Async XLA Ops:
  0.6 15.8 %copy-start.4 = (f32[65536]{0:T(1024)S(1)}, f32[65536]{0:T(1024)}, u32[]{:S(2)}) copy-start(f32[65536]{0:T(1024)} %param.13) | copy-start | bytes 786436
  0.6 16.8 %copy-start.5 = (s32[64,64]{1,0:T(8,128)S(1)}, s32[64,64]{1,0:T(8,128)}, u32[]{:S(2)}) copy-start(s32[64,64]{1,0:T(8,128)} %param.12) | copy-start | bytes 49156
  4.0 37.8 %copy-start.3 = (s32[32]{0:T(128)S(1)}, s32[32]{0:T(128)}, u32[]{:S(2)}) copy-start(s32[32]{0:T(128)} %constant.75.clone.place_ref) | copy-start | bytes 388
  4.0 37.8 %all-to-all-start = ((bf16[32,16,2048]{2,1,0:T(8,128)(2,1)}), bf16[32,16,2048]{2,1,0:T(8,128)(2,1)S(1)}, u32[]{:S(2)}, u32[]{:S(2)}) async-start(bf16[32,16,2048]{2,1,0:T(8,128)(2,1)} %regroup.1), calls=%async_computation | async-start | bytes 4194304 | tf_op jit(solution)/shard_map/all_to_all | solution.py:277
  43.7 9.3 %collective-permute-start.7 = (bf16[4,8,16,256]{3,2,1,0:T(8,128)(2,1)S(1)}, bf16[4,8,16,256]{3,2,1,0:T(8,128)(2,1)S(1)}, u32[]{:S(2)}, u32[]{:S(2)}) collective-permute-start(bf16[4,8,16,256]{3,2,1,0:T(8,128)(2,1)S(1)} %get-tuple-element.37), channel_id=1, source_target_pairs={{0,1},{1,0},{2,3},{3,2},{4,5},{5,4},{6,7},{7,6},{8,9},{9,8},{10,11... | collective-permute-start | bytes 786440 | tf_op jit(solution)/shard_map/ppermute | solution.py:304
  43.9 15.9 %collective-permute-start.9 = (bf16[4,8,16,256]{3,2,1,0:T(8,128)(2,1)S(1)}, bf16[4,8,16,256]{3,2,1,0:T(8,128)(2,1)S(1)}, u32[]{:S(2)}, u32[]{:S(2)}) collective-permute-start(bf16[4,8,16,256]{3,2,1,0:T(8,128)(2,1)S(1)} %get-tuple-element.39), channel_id=1, source_target_pairs={{0,2},{1,3},{2,0},{3,1},{4,6},{5,7},{6,4},{7,5},{8,10},{9,11},{10,... | collective-permute-start | bytes 786440 | tf_op jit(solution)/shard_map/ppermute | solution.py:304
  45.0 16.9 %collective-permute-start.11 = (bf16[4,8,16,256]{3,2,1,0:T(8,128)(2,1)S(1)}, bf16[4,8,16,256]{3,2,1,0:T(8,128)(2,1)S(1)}, u32[]{:S(2)}, u32[]{:S(2)}) collective-permute-start(bf16[4,8,16,256]{3,2,1,0:T(8,128)(2,1)S(1)} %get-tuple-element.41), channel_id=1, source_target_pairs={{0,3},{1,2},{2,1},{3,0},{4,7},{5,6},{6,5},{7,4},{8,11},{9,10},{10,... | collective-permute-start | bytes 786440 | tf_op jit(solution)/shard_map/ppermute | solution.py:304
  49.4 15.0 %collective-permute-start.6 = (bf16[4,8,16,256]{3,2,1,0:T(8,128)(2,1)S(1)}, bf16[4,8,16,256]{3,2,1,0:T(8,128)(2,1)S(1)}, u32[]{:S(2)}, u32[]{:S(2)}) collective-permute-start(bf16[4,8,16,256]{3,2,1,0:T(8,128)(2,1)S(1)} %get-tuple-element.36), channel_id=1, source_target_pairs={{0,1},{1,0},{2,3},{3,2},{4,5},{5,4},{6,7},{7,6},{8,9},{9,8},{10,11... | collective-permute-start | bytes 786440 | tf_op jit(solution)/shard_map/ppermute | solution.py:304
  49.5 19.0 %collective-permute-start.8 = (bf16[4,8,16,256]{3,2,1,0:T(8,128)(2,1)S(1)}, bf16[4,8,16,256]{3,2,1,0:T(8,128)(2,1)S(1)}, u32[]{:S(2)}, u32[]{:S(2)}) collective-permute-start(bf16[4,8,16,256]{3,2,1,0:T(8,128)(2,1)S(1)} %get-tuple-element.38), channel_id=1, source_target_pairs={{0,2},{1,3},{2,0},{3,1},{4,6},{5,7},{6,4},{7,5},{8,10},{9,11},{10,... | collective-permute-start | bytes 786440 | tf_op jit(solution)/shard_map/ppermute | solution.py:304
  53.1 18.8 %collective-permute-start.10 = (bf16[4,8,16,256]{3,2,1,0:T(8,128)(2,1)S(1)}, bf16[4,8,16,256]{3,2,1,0:T(8,128)(2,1)S(1)}, u32[]{:S(2)}, u32[]{:S(2)}) collective-permute-start(bf16[4,8,16,256]{3,2,1,0:T(8,128)(2,1)S(1)} %get-tuple-element.40), channel_id=1, source_target_pairs={{0,3},{1,2},{2,1},{3,0},{4,7},{5,6},{6,5},{7,4},{8,11},{9,10},{10,... | collective-permute-start | bytes 786440 | tf_op jit(solution)/shard_map/ppermute | solution.py:304
  56.6 16.3 %copy-start = (bf16[2,256,512]{2,1,0:T(8,128)(2,1)S(1)}, bf16[2,256,512]{2,1,0:T(8,128)(2,1)}, u32[]{:S(2)}) copy-start(bf16[2,256,512]{2,1,0:T(8,128)(2,1)} %constant.74.clone.refs_7_.refs_11_) | copy-start | bytes 1572868
  56.6 16.3 %copy-start.1 = (f32[256,256]{1,0:T(8,128)S(1)}, f32[256,256]{1,0:T(8,128)}, u32[]{:S(2)}) copy-start(f32[256,256]{1,0:T(8,128)} %constant.73.clone.refs_6_.refs_10_) | copy-start | bytes 786436
  56.6 16.2 %copy-start.2 = (f32[256,256]{1,0:T(8,128)S(1)}, f32[256,256]{1,0:T(8,128)}, u32[]{:S(2)}) copy-start(f32[256,256]{1,0:T(8,128)} %constant.72.clone.refs_5_.refs_9_) | copy-start | bytes 786436
  59.7 18.6 %collective-permute-start.3 = (bf16[8,4,16,256]{3,2,1,0:T(8,128)(2,1)S(1)}, bf16[8,4,16,256]{3,2,1,0:T(8,128)(2,1)S(1)}, u32[]{:S(2)}, u32[]{:S(2)}) collective-permute-start(bf16[8,4,16,256]{3,2,1,0:T(8,128)(2,1)S(1)} %get-tuple-element.29), channel_id=1, source_target_pairs={{0,1},{1,0},{2,3},{3,2},{4,5},{5,4},{6,7},{7,6},{8,9},{9,8},{10,11... | collective-permute-start | bytes 786440 | tf_op jit(solution)/shard_map/ppermute | solution.py:304
  61.9 17.8 %collective-permute-start.4 = (bf16[8,4,16,256]{3,2,1,0:T(8,128)(2,1)S(1)}, bf16[8,4,16,256]{3,2,1,0:T(8,128)(2,1)S(1)}, u32[]{:S(2)}, u32[]{:S(2)}) collective-permute-start(bf16[8,4,16,256]{3,2,1,0:T(8,128)(2,1)S(1)} %get-tuple-element.30), channel_id=1, source_target_pairs={{0,2},{1,3},{2,0},{3,1},{4,6},{5,7},{6,4},{7,5},{8,10},{9,11},{10,... | collective-permute-start | bytes 786440 | tf_op jit(solution)/shard_map/ppermute | solution.py:304
  64.3 17.4 %collective-permute-start.5 = (bf16[8,4,16,256]{3,2,1,0:T(8,128)(2,1)S(1)}, bf16[8,4,16,256]{3,2,1,0:T(8,128)(2,1)S(1)}, u32[]{:S(2)}, u32[]{:S(2)}) collective-permute-start(bf16[8,4,16,256]{3,2,1,0:T(8,128)(2,1)S(1)} %get-tuple-element.31), channel_id=1, source_target_pairs={{0,3},{1,2},{2,1},{3,0},{4,7},{5,6},{6,5},{7,4},{8,11},{9,10},{10,... | collective-permute-start | bytes 786440 | tf_op jit(solution)/shard_map/ppermute | solution.py:304
  68.5 18.4 %collective-permute-start = (bf16[8,4,16,256]{3,2,1,0:T(8,128)(2,1)S(1)}, bf16[8,4,16,256]{3,2,1,0:T(8,128)(2,1)S(1)}, u32[]{:S(2)}, u32[]{:S(2)}) collective-permute-start(bf16[8,4,16,256]{3,2,1,0:T(8,128)(2,1)S(1)} %get-tuple-element.25), channel_id=1, source_target_pairs={{0,1},{1,0},{2,3},{3,2},{4,5},{5,4},{6,7},{7,6},{8,9},{9,8},{10,11... | collective-permute-start | bytes 786440 | tf_op jit(solution)/shard_map/ppermute | solution.py:304
  71.8 15.1 %collective-permute-start.1 = (bf16[8,4,16,256]{3,2,1,0:T(8,128)(2,1)S(1)}, bf16[8,4,16,256]{3,2,1,0:T(8,128)(2,1)S(1)}, u32[]{:S(2)}, u32[]{:S(2)}) collective-permute-start(bf16[8,4,16,256]{3,2,1,0:T(8,128)(2,1)S(1)} %get-tuple-element.26), channel_id=1, source_target_pairs={{0,2},{1,3},{2,0},{3,1},{4,6},{5,7},{6,4},{7,5},{8,10},{9,11},{10,... | collective-permute-start | bytes 786440 | tf_op jit(solution)/shard_map/ppermute | solution.py:304
  78.4 13.1 %collective-permute-start.2 = (bf16[8,4,16,256]{3,2,1,0:T(8,128)(2,1)S(1)}, bf16[8,4,16,256]{3,2,1,0:T(8,128)(2,1)S(1)}, u32[]{:S(2)}, u32[]{:S(2)}) collective-permute-start(bf16[8,4,16,256]{3,2,1,0:T(8,128)(2,1)S(1)} %get-tuple-element.27), channel_id=1, source_target_pairs={{0,3},{1,2},{2,1},{3,0},{4,7},{5,6},{6,5},{7,4},{8,11},{9,10},{10,... | collective-permute-start | bytes 786440 | tf_op jit(solution)/shard_map/ppermute | solution.py:304

commit v6 on v5

--- a/solution.py
+++ b/solution.py
@@ -75,18 +75,17 @@
 
 
 def field_kernel(
-    start, groups, place_ref, rays_ref, cos_ref, sin_ref, inner_ref, outer_ref, *out_refs
+    start, groups, step, rays_ref, cos_ref, sin_ref, inner_ref, outer_ref, *out_refs
 ):
-    begin = start + groups * pl.program_id(0)
     phase_cos = cos_ref[...]
     phase_sin = sin_ref[...]
     inner = inner_ref[...]
     outer = outer_ref[...]
     count = outer.shape[0] // 2
     each = count // 4
-    stacked = []
-    for group in range(groups):
-        own = [rays_ref[place_ref[8 * view + begin + group]] for view in range(4)]
+
+    def partials(group):
+        own = [rays_ref[RANK_OF[8 * view + start + group]] for view in range(4)]
         rays = jnp.concatenate(own, axis=0)
 
         def wave(tile):
@@ -100,38 +99,41 @@
             waves = jnp.concatenate([wave(2 * low), wave(2 * low + 1)], axis=0)
             part = jnp.dot(waves, inner, preferred_element_type=jnp.float32)
             parts.append(part.astype(jnp.bfloat16))
-        for part in parts:
-            left = jnp.concatenate([part[:DIRS, :128], part[:DIRS, 128:]], axis=0)
-            right = jnp.concatenate([part[DIRS:, :128], part[DIRS:, 128:]], axis=0)
-            stacked.append(jnp.concatenate([left, right], axis=1))
-    field = [jnp.dot(outer, s, preferred_element_type=jnp.float32) for s in stacked]
-    for group in range(groups):
-        own = field[8 * group : 8 * (group + 1)]
-        sides = []
-        for rows in (slice(0, count), slice(count, 2 * count)):
-            sides.append(jnp.swapaxes(jnp.stack([f[rows] for f in own]), 0, 1))
-        block = jnp.concatenate(sides, axis=1).astype(jnp.bfloat16)
-        for partner in range(4):
-            out_refs[partner][group] = block[each * partner : each * (partner + 1)]
-
-
-def fields(rays, phase_cos, phase_sin, inner, outer, start, groups, step=2):
+        return parts
+
+    for begin in range(0, groups, step):
+        stacked = []
+        for group in range(begin, begin + step):
+            for part in partials(group):
+                left = jnp.concatenate([part[:DIRS, :128], part[:DIRS, 128:]], axis=0)
+                right = jnp.concatenate([part[DIRS:, :128], part[DIRS:, 128:]], axis=0)
+                stacked.append(jnp.concatenate([left, right], axis=1))
+        field = [jnp.dot(outer, s, preferred_element_type=jnp.float32) for s in stacked]
+        for at in range(step):
+            own = field[8 * at : 8 * (at + 1)]
+            sides = []
+            for rows in (slice(0, count), slice(count, 2 * count)):
+                sides.append(jnp.swapaxes(jnp.stack([f[rows] for f in own]), 0, 1))
+            block = jnp.concatenate(sides, axis=1).astype(jnp.bfloat16)
+            for partner in range(4):
+                out_refs[partner][begin + at] = block[each * partner : each * (partner + 1)]
+
+
+def fields(rays, phase_cos, phase_sin, inner, outer, start, groups, step=4):
     each = outer.shape[0] // 8
     in_vmem = pl.BlockSpec(memory_space=pltpu.VMEM)
-    out_block = pl.BlockSpec((step, each, 16, 256), lambda i: (i, 0, 0, 0))
     out_shape = jax.ShapeDtypeStruct((groups, each, 16, 256), jnp.bfloat16)
     return pl.pallas_call(
-        functools.partial(field_kernel, start, step),
-        grid=(groups // step,),
-        in_specs=[pl.BlockSpec(memory_space=pltpu.SMEM)] + [in_vmem] * 5,
-        out_specs=[out_block] * 4,
+        functools.partial(field_kernel, start, groups, step),
+        in_specs=[in_vmem] * 5,
+        out_specs=[in_vmem] * 4,
         out_shape=[out_shape] * 4,
-        compiler_params=params(),
+        compiler_params=pltpu.CompilerParams(vmem_limit_bytes=VMEM_BYTES),
         cost_estimate=pl.CostEstimate(
             flops=2 * 10**9, bytes_accessed=4 * 2**20, transcendentals=0
         ),
         name="fields",
-    )(jnp.asarray(RANK_OF, jnp.int32), rays, phase_cos, phase_sin, inner, outer)
+    )(rays, phase_cos, phase_sin, inner, outer)
 
 
 def spectrum_kernel(count, early, filled, keep, *refs):

time: 96.2 us -> 95.4 us (level)
  Pallas kernels: 25.5 us -> 21.8 us
  waiting for transfers between devices: 39.7 us -> 43.1 us
    pallas_call x4, Pallas kernels: 10.1 us -> 6.54 us  [fields(): pl.pallas_call(functools.partial(field_kernel, start, groups, step), in_s...]
    ppermute x12, waiting for transfers between devices: 18.3 us -> 21.7 us  [per_device(): pieces[d].append(lax.ppermute(sending[d], SQUARE, swaps))]
  transfers between devices with their start and end apart: 13 -> 13, of which waited for: 8 -> 9; matrix products, arithmetic and copies ran while one was open for 4% -> 4% of each run, Pallas kernels for 16% -> 13%
where the time goes in v6:
time: 95.4 us; the launch traced here: 95.1 us
  waiting for transfers between devices  43.1 us (45%)
  starting transfers between devices  25.4 us (27%)
  Pallas kernels  21.8 us (23%)
  local copies, waits for them, and re-layouts  2.63 us (3%)
  other arithmetic  1.26 us (1%)
    ppermute x12, waiting for transfers between devices, per_device(): pieces[d].append(lax.ppermute(sending[d], SQUARE, swaps))  21.7 us
    all_to_all x1, waiting for transfers between devices, per_device(): lax.all_to_all(sent, VIEW + COL, 0, 0, axis_index_groups=hogel_groups(),...  21.4 us
    ppermute x12, starting transfers between devices, per_device(): pieces[d].append(lax.ppermute(sending[d], SQUARE, swaps))  13.1 us
    all_to_all x1, starting transfers between devices, per_device(): lax.all_to_all(sent, VIEW + COL, 0, 0, axis_index_groups=hogel_groups(),...  12.3 us
    pallas_call x3, Pallas kernels, spectra(): pl.pallas_call(functools.partial(spectrum_kernel, count, len(early), len(...  12 us
    pallas_call x4, Pallas kernels, fields(): pl.pallas_call(functools.partial(field_kernel, start, groups, step), in_s...  6.54 us
    pallas_call x1, Pallas kernels, regroup(): pl.pallas_call(regroup_kernel, grid=(steps,), in_specs=[pl.BlockSpec((dir...  3.33 us
  transfers between devices with their start and end apart: 13, of which 9 were waited for; matrix products, arithmetic and copies ran while one was open for 4% of the time, Pallas kernels for 13%

profile of v6, /device:TPU:0, one launch (start us, length us, event | category | flops | bytes accessed | tf_op | source)
XLA Modules:
  0.0 95.1 jit_solution(7490093584797196183)
XLA Ops:
  0.6 3.3 %regroup.1 = bf16[32,16,2048]{2,1,0:T(8,128)(2,1)} custom-call(bf16[16,32,2048]{2,1,0:T(8,128)(2,1)} %views_ref.1), custom_call_target="tpu_custom_call" | custom-call | tf_op jit(solution)/shard_map/regroup/pallas_call | solution.py:66
  4.0 12.3 %all-to-all-start = ((bf16[32,16,2048]{2,1,0:T(8,128)(2,1)}), bf16[32,16,2048]{2,1,0:T(8,128)(2,1)S(1)}, u32[]{:S(2)}, u32[]{:S(2)}) async-start(bf16[32,16,2048]{2,1,0:T(8,128)(2,1)} %regroup.1), calls=%async_computation | async-start | bytes 4194304 | tf_op jit(solution)/shard_map/all_to_all | solution.py:279
  19.1 1.1 %dynamic-slice_bitcast_fusion.3 = (bf16[512,128]{1,0:T(8,128)(2,1)S(1)}, bf16[512,128]{1,0:T(8,128)(2,1)S(1)}, bf16[512,128]{1,0:T(8,128)(2,1)S(1)}, bf16[512,128]{1,0:T(8,128)(2,1)S(1)}) fusion(bf16[4,512,128]{2,1,0:T(8,128)(2,1)} %constant.69.clone, s32[]{:T(128)S(6)} %select_n.57, s32[]{:T(128)S(6)} %select_n.58, s32[]{:T(128)S(6)} %select_n.60, ...), kind=kLoop, calls=%fused_computation.31 | loop fusion | bytes 1048592 | tf_op jit(solution)/shard_map/jit(dynamic_index_in_dim)/squeeze | solution.py:288
  20.3 21.4 %all-to-all-done.rays_ref = bf16[32,16,2048]{2,1,0:T(8,128)(2,1)S(1)} async-done(((bf16[32,16,2048]{2,1,0:T(8,128)(2,1)}), bf16[32,16,2048]{2,1,0:T(8,128)(2,1)S(1)}, u32[]{:S(2)}, u32[]{:S(2)}) %all-to-all-start) | async-done | bytes 2097184 | tf_op jit(solution)/shard_map/all_to_all | solution.py:279
  41.7 1.2 %fields.7 = (bf16[4,8,16,256]{3,2,1,0:T(8,128)(2,1)S(1)}, bf16[4,8,16,256]{3,2,1,0:T(8,128)(2,1)S(1)}, bf16[4,8,16,256]{3,2,1,0:T(8,128)(2,1)S(1)}, bf16[4,8,16,256]{3,2,1,0:T(8,128)(2,1)S(1)}) custom-call(bf16[32,16,2048]{2,1,0:T(8,128)(2,1)S(1)} %all-to-all-done.rays_ref, f32[64,128]{1,0:T(8,128)S(1)} %tile.9.cos_ref, f32[64,128]{1,0:T(8,128)S(1)} %tile.21.sin_ref, ...), custom_call_target="tpu_custom_call" | custom-call | flops 2000000000 | bytes 4194304 | tf_op jit(solution)/shard_map/fields/pallas_call | solution.py:126
  43.0 1.1 %collective-permute-start.9 = (bf16[4,8,16,256]{3,2,1,0:T(8,128)(2,1)S(1)}, bf16[4,8,16,256]{3,2,1,0:T(8,128)(2,1)S(1)}, u32[]{:S(2)}, u32[]{:S(2)}) collective-permute-start(bf16[4,8,16,256]{3,2,1,0:T(8,128)(2,1)S(1)} %get-tuple-element.39), channel_id=1, source_target_pairs={{0,2},{1,3},{2,0},{3,1},{4,6},{5,7},{6,4},{7,5},{8,10},{9,11},{10,... | collective-permute-start | bytes 786440 | tf_op jit(solution)/shard_map/ppermute | solution.py:306
  44.1 2.4 %collective-permute-start.11 = (bf16[4,8,16,256]{3,2,1,0:T(8,128)(2,1)S(1)}, bf16[4,8,16,256]{3,2,1,0:T(8,128)(2,1)S(1)}, u32[]{:S(2)}, u32[]{:S(2)}) collective-permute-start(bf16[4,8,16,256]{3,2,1,0:T(8,128)(2,1)S(1)} %get-tuple-element.41), channel_id=1, source_target_pairs={{0,3},{1,2},{2,1},{3,0},{4,7},{5,6},{6,5},{7,4},{8,11},{9,10},{10,... | collective-permute-start | bytes 786440 | tf_op jit(solution)/shard_map/ppermute | solution.py:306
  46.6 1.2 %fields.6 = (bf16[4,8,16,256]{3,2,1,0:T(8,128)(2,1)S(1)}, bf16[4,8,16,256]{3,2,1,0:T(8,128)(2,1)S(1)}, bf16[4,8,16,256]{3,2,1,0:T(8,128)(2,1)S(1)}, bf16[4,8,16,256]{3,2,1,0:T(8,128)(2,1)S(1)}) custom-call(bf16[32,16,2048]{2,1,0:T(8,128)(2,1)S(1)} %all-to-all-done.rays_ref, f32[64,128]{1,0:T(8,128)S(1)} %tile.9.cos_ref, f32[64,128]{1,0:T(8,128)S(1)} %tile.21.sin_ref, ...), custom_call_target="tpu_custom_call" | custom-call | flops 2000000000 | bytes 4194304 | tf_op jit(solution)/shard_map/fields/pallas_call | solution.py:126
  47.9 1.1 %collective-permute-start.8 = (bf16[4,8,16,256]{3,2,1,0:T(8,128)(2,1)S(1)}, bf16[4,8,16,256]{3,2,1,0:T(8,128)(2,1)S(1)}, u32[]{:S(2)}, u32[]{:S(2)}) collective-permute-start(bf16[4,8,16,256]{3,2,1,0:T(8,128)(2,1)S(1)} %get-tuple-element.38), channel_id=1, source_target_pairs={{0,2},{1,3},{2,0},{3,1},{4,6},{5,7},{6,4},{7,5},{8,10},{9,11},{10,... | collective-permute-start | bytes 786440 | tf_op jit(solution)/shard_map/ppermute | solution.py:306
  49.0 3.2 %collective-permute-done.7.refs_3_ = bf16[4,8,16,256]{3,2,1,0:T(8,128)(2,1)S(1)} collective-permute-done((bf16[4,8,16,256]{3,2,1,0:T(8,128)(2,1)S(1)}, bf16[4,8,16,256]{3,2,1,0:T(8,128)(2,1)S(1)}, u32[]{:S(2)}, u32[]{:S(2)}) %collective-permute-start.7) | collective-permute-done | bytes 262176 | tf_op jit(solution)/shard_map/ppermute | solution.py:306
  52.6 2.0 %fields.5 = (bf16[8,4,16,256]{3,2,1,0:T(8,128)(2,1)S(1)}, bf16[8,4,16,256]{3,2,1,0:T(8,128)(2,1)S(1)}, bf16[8,4,16,256]{3,2,1,0:T(8,128)(2,1)S(1)}, bf16[8,4,16,256]{3,2,1,0:T(8,128)(2,1)S(1)}) custom-call(bf16[32,16,2048]{2,1,0:T(8,128)(2,1)S(1)} %all-to-all-done.rays_ref, f32[64,128]{1,0:T(8,128)S(1)} %tile.9.cos_ref, f32[64,128]{1,0:T(8,128)S(1)} %tile.21.sin_ref, ...), custom_call_target="tpu_custom_call" | custom-call | flops 2000000000 | bytes 4194304 | tf_op jit(solution)/shard_map/fields/pallas_call | solution.py:126
  54.7 2.0 %fields.4 = (bf16[8,4,16,256]{3,2,1,0:T(8,128)(2,1)S(1)}, bf16[8,4,16,256]{3,2,1,0:T(8,128)(2,1)S(1)}, bf16[8,4,16,256]{3,2,1,0:T(8,128)(2,1)S(1)}, bf16[8,4,16,256]{3,2,1,0:T(8,128)(2,1)S(1)}) custom-call(bf16[32,16,2048]{2,1,0:T(8,128)(2,1)S(1)} %all-to-all-done.rays_ref, f32[64,128]{1,0:T(8,128)S(1)} %tile.9.cos_ref, f32[64,128]{1,0:T(8,128)S(1)} %tile.21.sin_ref, ...), custom_call_target="tpu_custom_call" | custom-call | flops 2000000000 | bytes 4194304 | tf_op jit(solution)/shard_map/fields/pallas_call | solution.py:126
  57.5 2.4 %collective-permute-start.3 = (bf16[8,4,16,256]{3,2,1,0:T(8,128)(2,1)S(1)}, bf16[8,4,16,256]{3,2,1,0:T(8,128)(2,1)S(1)}, u32[]{:S(2)}, u32[]{:S(2)}) collective-permute-start(bf16[8,4,16,256]{3,2,1,0:T(8,128)(2,1)S(1)} %get-tuple-element.29), channel_id=1, source_target_pairs={{0,1},{1,0},{2,3},{3,2},{4,5},{5,4},{6,7},{7,6},{8,9},{9,8},{10,11... | collective-permute-start | bytes 786440 | tf_op jit(solution)/shard_map/ppermute | solution.py:306
  60.0 1.0 %collective-permute-start.4 = (bf16[8,4,16,256]{3,2,1,0:T(8,128)(2,1)S(1)}, bf16[8,4,16,256]{3,2,1,0:T(8,128)(2,1)S(1)}, u32[]{:S(2)}, u32[]{:S(2)}) collective-permute-start(bf16[8,4,16,256]{3,2,1,0:T(8,128)(2,1)S(1)} %get-tuple-element.30), channel_id=1, source_target_pairs={{0,2},{1,3},{2,0},{3,1},{4,6},{5,7},{6,4},{7,5},{8,10},{9,11},{10,... | collective-permute-start | bytes 786440 | tf_op jit(solution)/shard_map/ppermute | solution.py:306
  61.0 2.5 %collective-permute-done.6.refs_2_ = bf16[4,8,16,256]{3,2,1,0:T(8,128)(2,1)S(1)} collective-permute-done((bf16[4,8,16,256]{3,2,1,0:T(8,128)(2,1)S(1)}, bf16[4,8,16,256]{3,2,1,0:T(8,128)(2,1)S(1)}, u32[]{:S(2)}, u32[]{:S(2)}) %collective-permute-start.6) | collective-permute-done | bytes 262176 | tf_op jit(solution)/shard_map/ppermute | solution.py:306
  63.9 4.8 %collective-permute-done.8.refs_4_ = bf16[4,8,16,256]{3,2,1,0:T(8,128)(2,1)S(1)} collective-permute-done((bf16[4,8,16,256]{3,2,1,0:T(8,128)(2,1)S(1)}, bf16[4,8,16,256]{3,2,1,0:T(8,128)(2,1)S(1)}, u32[]{:S(2)}, u32[]{:S(2)}) %collective-permute-start.8) | collective-permute-done | bytes 262176 | tf_op jit(solution)/shard_map/ppermute | solution.py:306
  68.7 2.5 %collective-permute-start = (bf16[8,4,16,256]{3,2,1,0:T(8,128)(2,1)S(1)}, bf16[8,4,16,256]{3,2,1,0:T(8,128)(2,1)S(1)}, u32[]{:S(2)}, u32[]{:S(2)}) collective-permute-start(bf16[8,4,16,256]{3,2,1,0:T(8,128)(2,1)S(1)} %get-tuple-element.25), channel_id=1, source_target_pairs={{0,1},{1,0},{2,3},{3,2},{4,5},{5,4},{6,7},{7,6},{8,9},{9,8},{10,11... | collective-permute-start | bytes 786440 | tf_op jit(solution)/shard_map/ppermute | solution.py:306
  71.2 1.0 %collective-permute-start.1 = (bf16[8,4,16,256]{3,2,1,0:T(8,128)(2,1)S(1)}, bf16[8,4,16,256]{3,2,1,0:T(8,128)(2,1)S(1)}, u32[]{:S(2)}, u32[]{:S(2)}) collective-permute-start(bf16[8,4,16,256]{3,2,1,0:T(8,128)(2,1)S(1)} %get-tuple-element.26), channel_id=1, source_target_pairs={{0,2},{1,3},{2,0},{3,1},{4,6},{5,7},{6,4},{7,5},{8,10},{9,11},{10,... | collective-permute-start | bytes 786440 | tf_op jit(solution)/shard_map/ppermute | solution.py:306
  72.2 5.5 %spectra.4 = (f32[8192,128]{1,0:T(8,128)}, f32[8192,128]{1,0:T(8,128)}) custom-call(bf16[4,8,16,256]{3,2,1,0:T(8,128)(2,1)S(1)} %get-tuple-element.34.refs_0_, bf16[4,8,16,256]{3,2,1,0:T(8,128)(2,1)S(1)} %get-tuple-element.35.refs_1_, bf16[4,8,16,256]{3,2,1,0:T(8,128)(2,1)S(1)} %collective-permute-done.6.refs_2_, ...), custom_call_target="tpu_custom_call" | custom-call | flops 8000000000 | bytes 8388608 | tf_op jit(solution)/shard_map/spectra/pallas_call | solution.py:206
  78.1 1.8 %collective-permute-done.4.refs_2_ = bf16[8,4,16,256]{3,2,1,0:T(8,128)(2,1)S(1)} collective-permute-done((bf16[8,4,16,256]{3,2,1,0:T(8,128)(2,1)S(1)}, bf16[8,4,16,256]{3,2,1,0:T(8,128)(2,1)S(1)}, u32[]{:S(2)}, u32[]{:S(2)}) %collective-permute-start.4) | collective-permute-done | bytes 262176 | tf_op jit(solution)/shard_map/ppermute | solution.py:306
  80.9 2.0 %spectra.3 = (f32[4,256,256]{2,1,0:T(8,128)S(1)}, f32[4,256,256]{2,1,0:T(8,128)S(1)}) custom-call(bf16[8,4,16,256]{3,2,1,0:T(8,128)(2,1)S(1)} %get-tuple-element.28.refs_0_, bf16[8,4,16,256]{3,2,1,0:T(8,128)(2,1)S(1)} %collective-permute-done.3.refs_1_, bf16[8,4,16,256]{3,2,1,0:T(8,128)(2,1)S(1)} %collective-permute-done.4.refs_2_, ...), custom_call_target="tpu_custom_call" | custom-call | flops 4000000000 | bytes 4194304 | tf_op jit(solution)/shard_map/spectra/pallas_call | solution.py:206
  83.0 3.1 %collective-permute-done.refs_1_ = bf16[8,4,16,256]{3,2,1,0:T(8,128)(2,1)S(1)} collective-permute-done((bf16[8,4,16,256]{3,2,1,0:T(8,128)(2,1)S(1)}, bf16[8,4,16,256]{3,2,1,0:T(8,128)(2,1)S(1)}, u32[]{:S(2)}, u32[]{:S(2)}) %collective-permute-start) | collective-permute-done | bytes 262176 | tf_op jit(solution)/shard_map/ppermute | solution.py:306
  86.1 4.6 %collective-permute-done.2.refs_3_ = bf16[8,4,16,256]{3,2,1,0:T(8,128)(2,1)S(1)} collective-permute-done((bf16[8,4,16,256]{3,2,1,0:T(8,128)(2,1)S(1)}, bf16[8,4,16,256]{3,2,1,0:T(8,128)(2,1)S(1)}, u32[]{:S(2)}, u32[]{:S(2)}) %collective-permute-start.2) | collective-permute-done | bytes 262176 | tf_op jit(solution)/shard_map/ppermute | solution.py:306
  90.6 4.5 %spectra.5 = (f32[8192,128]{1,0:T(8,128)}, f32[8192,128]{1,0:T(8,128)}) custom-call(bf16[8,4,16,256]{3,2,1,0:T(8,128)(2,1)S(1)} %get-tuple-element.24.refs_0_, bf16[8,4,16,256]{3,2,1,0:T(8,128)(2,1)S(1)} %collective-permute-done.refs_1_, bf16[8,4,16,256]{3,2,1,0:T(8,128)(2,1)S(1)} %collective-permute-done.1.refs_2_, ...), custom_call_target="tpu_custom_call", output_to_operand_aliasing={{0}: (12, {}), {1}: (13, {})} | custom-call | flops 4000000000 | bytes 4194304 | tf_op jit(solution)/shard_map/spectra/pallas_call | solution.py:206
  (42 shorter events, 6.0 us)
Async XLA Ops:
  0.6 15.6 %copy-start.3 = (f32[65536]{0:T(1024)S(1)}, f32[65536]{0:T(1024)}, u32[]{:S(2)}) copy-start(f32[65536]{0:T(1024)} %param.9) | copy-start | bytes 786436
  0.6 16.6 %copy-start.4 = (s32[64,64]{1,0:T(8,128)S(1)}, s32[64,64]{1,0:T(8,128)}, u32[]{:S(2)}) copy-start(s32[64,64]{1,0:T(8,128)} %param.8) | copy-start | bytes 49156
  4.0 37.7 %all-to-all-start = ((bf16[32,16,2048]{2,1,0:T(8,128)(2,1)}), bf16[32,16,2048]{2,1,0:T(8,128)(2,1)S(1)}, u32[]{:S(2)}, u32[]{:S(2)}) async-start(bf16[32,16,2048]{2,1,0:T(8,128)(2,1)} %regroup.1), calls=%async_computation | async-start | bytes 4194304 | tf_op jit(solution)/shard_map/all_to_all | solution.py:279
  42.9 9.3 %collective-permute-start.7 = (bf16[4,8,16,256]{3,2,1,0:T(8,128)(2,1)S(1)}, bf16[4,8,16,256]{3,2,1,0:T(8,128)(2,1)S(1)}, u32[]{:S(2)}, u32[]{:S(2)}) collective-permute-start(bf16[4,8,16,256]{3,2,1,0:T(8,128)(2,1)S(1)} %get-tuple-element.37), channel_id=1, source_target_pairs={{0,1},{1,0},{2,3},{3,2},{4,5},{5,4},{6,7},{7,6},{8,9},{9,8},{10,11... | collective-permute-start | bytes 786440 | tf_op jit(solution)/shard_map/ppermute | solution.py:306
  43.0 14.5 %collective-permute-start.9 = (bf16[4,8,16,256]{3,2,1,0:T(8,128)(2,1)S(1)}, bf16[4,8,16,256]{3,2,1,0:T(8,128)(2,1)S(1)}, u32[]{:S(2)}, u32[]{:S(2)}) collective-permute-start(bf16[4,8,16,256]{3,2,1,0:T(8,128)(2,1)S(1)} %get-tuple-element.39), channel_id=1, source_target_pairs={{0,2},{1,3},{2,0},{3,1},{4,6},{5,7},{6,4},{7,5},{8,10},{9,11},{10,... | collective-permute-start | bytes 786440 | tf_op jit(solution)/shard_map/ppermute | solution.py:306
  44.1 15.8 %collective-permute-start.11 = (bf16[4,8,16,256]{3,2,1,0:T(8,128)(2,1)S(1)}, bf16[4,8,16,256]{3,2,1,0:T(8,128)(2,1)S(1)}, u32[]{:S(2)}, u32[]{:S(2)}) collective-permute-start(bf16[4,8,16,256]{3,2,1,0:T(8,128)(2,1)S(1)} %get-tuple-element.41), channel_id=1, source_target_pairs={{0,3},{1,2},{2,1},{3,0},{4,7},{5,6},{6,5},{7,4},{8,11},{9,10},{10,... | collective-permute-start | bytes 786440 | tf_op jit(solution)/shard_map/ppermute | solution.py:306
  47.8 15.7 %collective-permute-start.6 = (bf16[4,8,16,256]{3,2,1,0:T(8,128)(2,1)S(1)}, bf16[4,8,16,256]{3,2,1,0:T(8,128)(2,1)S(1)}, u32[]{:S(2)}, u32[]{:S(2)}) collective-permute-start(bf16[4,8,16,256]{3,2,1,0:T(8,128)(2,1)S(1)} %get-tuple-element.36), channel_id=1, source_target_pairs={{0,1},{1,0},{2,3},{3,2},{4,5},{5,4},{6,7},{7,6},{8,9},{9,8},{10,11... | collective-permute-start | bytes 786440 | tf_op jit(solution)/shard_map/ppermute | solution.py:306
  47.9 20.8 %collective-permute-start.8 = (bf16[4,8,16,256]{3,2,1,0:T(8,128)(2,1)S(1)}, bf16[4,8,16,256]{3,2,1,0:T(8,128)(2,1)S(1)}, u32[]{:S(2)}, u32[]{:S(2)}) collective-permute-start(bf16[4,8,16,256]{3,2,1,0:T(8,128)(2,1)S(1)} %get-tuple-element.38), channel_id=1, source_target_pairs={{0,2},{1,3},{2,0},{3,1},{4,6},{5,7},{6,4},{7,5},{8,10},{9,11},{10,... | collective-permute-start | bytes 786440 | tf_op jit(solution)/shard_map/ppermute | solution.py:306
  52.2 19.0 %collective-permute-start.10 = (bf16[4,8,16,256]{3,2,1,0:T(8,128)(2,1)S(1)}, bf16[4,8,16,256]{3,2,1,0:T(8,128)(2,1)S(1)}, u32[]{:S(2)}, u32[]{:S(2)}) collective-permute-start(bf16[4,8,16,256]{3,2,1,0:T(8,128)(2,1)S(1)} %get-tuple-element.40), channel_id=1, source_target_pairs={{0,3},{1,2},{2,1},{3,0},{4,7},{5,6},{6,5},{7,4},{8,11},{9,10},{10,... | collective-permute-start | bytes 786440 | tf_op jit(solution)/shard_map/ppermute | solution.py:306
  54.7 17.5 %copy-start = (bf16[2,256,512]{2,1,0:T(8,128)(2,1)S(1)}, bf16[2,256,512]{2,1,0:T(8,128)(2,1)}, u32[]{:S(2)}) copy-start(bf16[2,256,512]{2,1,0:T(8,128)(2,1)} %constant.72.clone.refs_7_.refs_11_) | copy-start | bytes 1572868
  54.7 17.5 %copy-start.1 = (f32[256,256]{1,0:T(8,128)S(1)}, f32[256,256]{1,0:T(8,128)}, u32[]{:S(2)}) copy-start(f32[256,256]{1,0:T(8,128)} %constant.71.clone.refs_6_.refs_10_) | copy-start | bytes 786436
  54.7 17.5 %copy-start.2 = (f32[256,256]{1,0:T(8,128)S(1)}, f32[256,256]{1,0:T(8,128)}, u32[]{:S(2)}) copy-start(f32[256,256]{1,0:T(8,128)} %constant.70.clone.refs_5_.refs_9_) | copy-start | bytes 786436
  57.5 20.2 %collective-permute-start.3 = (bf16[8,4,16,256]{3,2,1,0:T(8,128)(2,1)S(1)}, bf16[8,4,16,256]{3,2,1,0:T(8,128)(2,1)S(1)}, u32[]{:S(2)}, u32[]{:S(2)}) collective-permute-start(bf16[8,4,16,256]{3,2,1,0:T(8,128)(2,1)S(1)} %get-tuple-element.29), channel_id=1, source_target_pairs={{0,1},{1,0},{2,3},{3,2},{4,5},{5,4},{6,7},{7,6},{8,9},{9,8},{10,11... | collective-permute-start | bytes 786440 | tf_op jit(solution)/shard_map/ppermute | solution.py:306
  60.0 19.9 %collective-permute-start.4 = (bf16[8,4,16,256]{3,2,1,0:T(8,128)(2,1)S(1)}, bf16[8,4,16,256]{3,2,1,0:T(8,128)(2,1)S(1)}, u32[]{:S(2)}, u32[]{:S(2)}) collective-permute-start(bf16[8,4,16,256]{3,2,1,0:T(8,128)(2,1)S(1)} %get-tuple-element.30), channel_id=1, source_target_pairs={{0,2},{1,3},{2,0},{3,1},{4,6},{5,7},{6,4},{7,5},{8,10},{9,11},{10,... | collective-permute-start | bytes 786440 | tf_op jit(solution)/shard_map/ppermute | solution.py:306
  63.5 17.4 %collective-permute-start.5 = (bf16[8,4,16,256]{3,2,1,0:T(8,128)(2,1)S(1)}, bf16[8,4,16,256]{3,2,1,0:T(8,128)(2,1)S(1)}, u32[]{:S(2)}, u32[]{:S(2)}) collective-permute-start(bf16[8,4,16,256]{3,2,1,0:T(8,128)(2,1)S(1)} %get-tuple-element.31), channel_id=1, source_target_pairs={{0,3},{1,2},{2,1},{3,0},{4,7},{5,6},{6,5},{7,4},{8,11},{9,10},{10,... | collective-permute-start | bytes 786440 | tf_op jit(solution)/shard_map/ppermute | solution.py:306
  68.7 17.3 %collective-permute-start = (bf16[8,4,16,256]{3,2,1,0:T(8,128)(2,1)S(1)}, bf16[8,4,16,256]{3,2,1,0:T(8,128)(2,1)S(1)}, u32[]{:S(2)}, u32[]{:S(2)}) collective-permute-start(bf16[8,4,16,256]{3,2,1,0:T(8,128)(2,1)S(1)} %get-tuple-element.25), channel_id=1, source_target_pairs={{0,1},{1,0},{2,3},{3,2},{4,5},{5,4},{6,7},{7,6},{8,9},{9,8},{10,11... | collective-permute-start | bytes 786440 | tf_op jit(solution)/shard_map/ppermute | solution.py:306
  71.2 14.9 %collective-permute-start.1 = (bf16[8,4,16,256]{3,2,1,0:T(8,128)(2,1)S(1)}, bf16[8,4,16,256]{3,2,1,0:T(8,128)(2,1)S(1)}, u32[]{:S(2)}, u32[]{:S(2)}) collective-permute-start(bf16[8,4,16,256]{3,2,1,0:T(8,128)(2,1)S(1)} %get-tuple-element.26), channel_id=1, source_target_pairs={{0,2},{1,3},{2,0},{3,1},{4,6},{5,7},{6,4},{7,5},{8,10},{9,11},{10,... | collective-permute-start | bytes 786440 | tf_op jit(solution)/shard_map/ppermute | solution.py:306
  77.7 13.0 %collective-permute-start.2 = (bf16[8,4,16,256]{3,2,1,0:T(8,128)(2,1)S(1)}, bf16[8,4,16,256]{3,2,1,0:T(8,128)(2,1)S(1)}, u32[]{:S(2)}, u32[]{:S(2)}) collective-permute-start(bf16[8,4,16,256]{3,2,1,0:T(8,128)(2,1)S(1)} %get-tuple-element.27), channel_id=1, source_target_pairs={{0,3},{1,2},{2,1},{3,0},{4,7},{5,6},{6,5},{7,4},{8,11},{9,10},{10,... | collective-permute-start | bytes 786440 | tf_op jit(solution)/shard_map/ppermute | solution.py:306

commit v7 on v6

--- a/solution.py
+++ b/solution.py
@@ -16,8 +16,8 @@
 VIEW = ("xh", "co")
 COL = ("y", "zh", "zl", "xl")
 HOGEL_ORDER = (
-    29, 5, 15, 12, 24, 14, 31, 11, 16, 30, 13, 8, 4, 1, 6, 23,
-    0, 21, 26, 2, 22, 28, 19, 17, 3, 10, 7, 9, 18, 27, 25, 20,
+    29, 20, 7, 6, 26, 28, 24, 11, 19, 14, 3, 9, 21, 30, 12, 27,
+    0, 31, 23, 13, 5, 1, 8, 2, 10, 22, 15, 18, 16, 17, 4, 25,
 )
 RANK_OF = tuple(HOGEL_ORDER.index(row) for row in range(len(HOGEL_ORDER)))
 SQUARE = ("zl", "xl")

time: 95.4 us -> 95.8 us (level)
    all_to_all x1, waiting for transfers between devices: 21.4 us -> 20.1 us  [per_device(): lax.all_to_all(sent, VIEW + COL, 0, 0, axis_index_groups=hogel_groups(),...]
  transfers between devices with their start and end apart: 13 -> 13, of which waited for: 9 -> 8; matrix products, arithmetic and copies ran while one was open for 4% -> 4% of each run, Pallas kernels for 13% -> 13%
where the time goes in v7:
time: 95.8 us; the launch traced here: 95 us
  waiting for transfers between devices  42.3 us (44%)
  starting transfers between devices  26.1 us (27%)
  Pallas kernels  21.8 us (23%)
  local copies, waits for them, and re-layouts  2.63 us (3%)
  other arithmetic  1.26 us (1%)
    ppermute x12, waiting for transfers between devices, per_device(): pieces[d].append(lax.ppermute(sending[d], SQUARE, swaps))  22.2 us
    all_to_all x1, waiting for transfers between devices, per_device(): lax.all_to_all(sent, VIEW + COL, 0, 0, axis_index_groups=hogel_groups(),...  20.1 us
    ppermute x12, starting transfers between devices, per_device(): pieces[d].append(lax.ppermute(sending[d], SQUARE, swaps))  13.8 us
    all_to_all x1, starting transfers between devices, per_device(): lax.all_to_all(sent, VIEW + COL, 0, 0, axis_index_groups=hogel_groups(),...  12.3 us
    pallas_call x3, Pallas kernels, spectra(): pl.pallas_call(functools.partial(spectrum_kernel, count, len(early), len(...  12 us
    pallas_call x4, Pallas kernels, fields(): pl.pallas_call(functools.partial(field_kernel, start, groups, step), in_s...  6.54 us
    pallas_call x1, Pallas kernels, regroup(): pl.pallas_call(regroup_kernel, grid=(steps,), in_specs=[pl.BlockSpec((dir...  3.33 us
  transfers between devices with their start and end apart: 13, of which 8 were waited for; matrix products, arithmetic and copies ran while one was open for 4% of the time, Pallas kernels for 13%

profile of v7, /device:TPU:0, one launch (start us, length us, event | category | flops | bytes accessed | tf_op | source)
XLA Modules:
  0.0 95.0 jit_solution(6214793085964957092)
XLA Ops:
  0.6 3.3 %regroup.1 = bf16[32,16,2048]{2,1,0:T(8,128)(2,1)} custom-call(bf16[16,32,2048]{2,1,0:T(8,128)(2,1)} %views_ref.1), custom_call_target="tpu_custom_call" | custom-call | tf_op jit(solution)/shard_map/regroup/pallas_call | solution.py:66
  4.0 12.3 %all-to-all-start = ((bf16[32,16,2048]{2,1,0:T(8,128)(2,1)}), bf16[32,16,2048]{2,1,0:T(8,128)(2,1)S(1)}, u32[]{:S(2)}, u32[]{:S(2)}) async-start(bf16[32,16,2048]{2,1,0:T(8,128)(2,1)} %regroup.1), calls=%async_computation | async-start | bytes 4194304 | tf_op jit(solution)/shard_map/all_to_all | solution.py:279
  19.0 1.1 %dynamic-slice_bitcast_fusion.3 = (bf16[512,128]{1,0:T(8,128)(2,1)S(1)}, bf16[512,128]{1,0:T(8,128)(2,1)S(1)}, bf16[512,128]{1,0:T(8,128)(2,1)S(1)}, bf16[512,128]{1,0:T(8,128)(2,1)S(1)}) fusion(bf16[4,512,128]{2,1,0:T(8,128)(2,1)} %constant.69.clone, s32[]{:T(128)S(6)} %select_n.57, s32[]{:T(128)S(6)} %select_n.58, s32[]{:T(128)S(6)} %select_n.60, ...), kind=kLoop, calls=%fused_computation.31 | loop fusion | bytes 1048592 | tf_op jit(solution)/shard_map/jit(dynamic_index_in_dim)/squeeze | solution.py:288
  20.3 20.1 %all-to-all-done.rays_ref = bf16[32,16,2048]{2,1,0:T(8,128)(2,1)S(1)} async-done(((bf16[32,16,2048]{2,1,0:T(8,128)(2,1)}), bf16[32,16,2048]{2,1,0:T(8,128)(2,1)S(1)}, u32[]{:S(2)}, u32[]{:S(2)}) %all-to-all-start) | async-done | bytes 2097184 | tf_op jit(solution)/shard_map/all_to_all | solution.py:279
  40.4 1.2 %fields.7 = (bf16[4,8,16,256]{3,2,1,0:T(8,128)(2,1)S(1)}, bf16[4,8,16,256]{3,2,1,0:T(8,128)(2,1)S(1)}, bf16[4,8,16,256]{3,2,1,0:T(8,128)(2,1)S(1)}, bf16[4,8,16,256]{3,2,1,0:T(8,128)(2,1)S(1)}) custom-call(bf16[32,16,2048]{2,1,0:T(8,128)(2,1)S(1)} %all-to-all-done.rays_ref, f32[64,128]{1,0:T(8,128)S(1)} %tile.9.cos_ref, f32[64,128]{1,0:T(8,128)S(1)} %tile.21.sin_ref, ...), custom_call_target="tpu_custom_call" | custom-call | flops 2000000000 | bytes 4194304 | tf_op jit(solution)/shard_map/fields/pallas_call | solution.py:126
  42.5 1.1 %collective-permute-start.9 = (bf16[4,8,16,256]{3,2,1,0:T(8,128)(2,1)S(1)}, bf16[4,8,16,256]{3,2,1,0:T(8,128)(2,1)S(1)}, u32[]{:S(2)}, u32[]{:S(2)}) collective-permute-start(bf16[4,8,16,256]{3,2,1,0:T(8,128)(2,1)S(1)} %get-tuple-element.39), channel_id=1, source_target_pairs={{0,2},{1,3},{2,0},{3,1},{4,6},{5,7},{6,4},{7,5},{8,10},{9,11},{10,... | collective-permute-start | bytes 786440 | tf_op jit(solution)/shard_map/ppermute | solution.py:306
  43.6 1.7 %collective-permute-start.11 = (bf16[4,8,16,256]{3,2,1,0:T(8,128)(2,1)S(1)}, bf16[4,8,16,256]{3,2,1,0:T(8,128)(2,1)S(1)}, u32[]{:S(2)}, u32[]{:S(2)}) collective-permute-start(bf16[4,8,16,256]{3,2,1,0:T(8,128)(2,1)S(1)} %get-tuple-element.41), channel_id=1, source_target_pairs={{0,3},{1,2},{2,1},{3,0},{4,7},{5,6},{6,5},{7,4},{8,11},{9,10},{10,... | collective-permute-start | bytes 786440 | tf_op jit(solution)/shard_map/ppermute | solution.py:306
  45.3 1.2 %fields.6 = (bf16[4,8,16,256]{3,2,1,0:T(8,128)(2,1)S(1)}, bf16[4,8,16,256]{3,2,1,0:T(8,128)(2,1)S(1)}, bf16[4,8,16,256]{3,2,1,0:T(8,128)(2,1)S(1)}, bf16[4,8,16,256]{3,2,1,0:T(8,128)(2,1)S(1)}) custom-call(bf16[32,16,2048]{2,1,0:T(8,128)(2,1)S(1)} %all-to-all-done.rays_ref, f32[64,128]{1,0:T(8,128)S(1)} %tile.9.cos_ref, f32[64,128]{1,0:T(8,128)S(1)} %tile.21.sin_ref, ...), custom_call_target="tpu_custom_call" | custom-call | flops 2000000000 | bytes 4194304 | tf_op jit(solution)/shard_map/fields/pallas_call | solution.py:126
  48.4 2.5 %collective-permute-done.7.refs_3_ = bf16[4,8,16,256]{3,2,1,0:T(8,128)(2,1)S(1)} collective-permute-done((bf16[4,8,16,256]{3,2,1,0:T(8,128)(2,1)S(1)}, bf16[4,8,16,256]{3,2,1,0:T(8,128)(2,1)S(1)}, u32[]{:S(2)}, u32[]{:S(2)}) %collective-permute-start.7) | collective-permute-done | bytes 262176 | tf_op jit(solution)/shard_map/ppermute | solution.py:306
  50.9 1.2 %collective-permute-start.10 = (bf16[4,8,16,256]{3,2,1,0:T(8,128)(2,1)S(1)}, bf16[4,8,16,256]{3,2,1,0:T(8,128)(2,1)S(1)}, u32[]{:S(2)}, u32[]{:S(2)}) collective-permute-start(bf16[4,8,16,256]{3,2,1,0:T(8,128)(2,1)S(1)} %get-tuple-element.40), channel_id=1, source_target_pairs={{0,3},{1,2},{2,1},{3,0},{4,7},{5,6},{6,5},{7,4},{8,11},{9,10},{10,... | collective-permute-start | bytes 786440 | tf_op jit(solution)/shard_map/ppermute | solution.py:306
  52.1 2.0 %fields.5 = (bf16[8,4,16,256]{3,2,1,0:T(8,128)(2,1)S(1)}, bf16[8,4,16,256]{3,2,1,0:T(8,128)(2,1)S(1)}, bf16[8,4,16,256]{3,2,1,0:T(8,128)(2,1)S(1)}, bf16[8,4,16,256]{3,2,1,0:T(8,128)(2,1)S(1)}) custom-call(bf16[32,16,2048]{2,1,0:T(8,128)(2,1)S(1)} %all-to-all-done.rays_ref, f32[64,128]{1,0:T(8,128)S(1)} %tile.9.cos_ref, f32[64,128]{1,0:T(8,128)S(1)} %tile.21.sin_ref, ...), custom_call_target="tpu_custom_call" | custom-call | flops 2000000000 | bytes 4194304 | tf_op jit(solution)/shard_map/fields/pallas_call | solution.py:126
  54.2 2.0 %fields.4 = (bf16[8,4,16,256]{3,2,1,0:T(8,128)(2,1)S(1)}, bf16[8,4,16,256]{3,2,1,0:T(8,128)(2,1)S(1)}, bf16[8,4,16,256]{3,2,1,0:T(8,128)(2,1)S(1)}, bf16[8,4,16,256]{3,2,1,0:T(8,128)(2,1)S(1)}) custom-call(bf16[32,16,2048]{2,1,0:T(8,128)(2,1)S(1)} %all-to-all-done.rays_ref, f32[64,128]{1,0:T(8,128)S(1)} %tile.9.cos_ref, f32[64,128]{1,0:T(8,128)S(1)} %tile.21.sin_ref, ...), custom_call_target="tpu_custom_call" | custom-call | flops 2000000000 | bytes 4194304 | tf_op jit(solution)/shard_map/fields/pallas_call | solution.py:126
  57.3 1.4 %collective-permute-start.3 = (bf16[8,4,16,256]{3,2,1,0:T(8,128)(2,1)S(1)}, bf16[8,4,16,256]{3,2,1,0:T(8,128)(2,1)S(1)}, u32[]{:S(2)}, u32[]{:S(2)}) collective-permute-start(bf16[8,4,16,256]{3,2,1,0:T(8,128)(2,1)S(1)} %get-tuple-element.29), channel_id=1, source_target_pairs={{0,1},{1,0},{2,3},{3,2},{4,5},{5,4},{6,7},{7,6},{8,9},{9,8},{10,11... | collective-permute-start | bytes 786440 | tf_op jit(solution)/shard_map/ppermute | solution.py:306
  59.7 2.5 %collective-permute-done.6.refs_2_ = bf16[4,8,16,256]{3,2,1,0:T(8,128)(2,1)S(1)} collective-permute-done((bf16[4,8,16,256]{3,2,1,0:T(8,128)(2,1)S(1)}, bf16[4,8,16,256]{3,2,1,0:T(8,128)(2,1)S(1)}, u32[]{:S(2)}, u32[]{:S(2)}) %collective-permute-start.6) | collective-permute-done | bytes 262176 | tf_op jit(solution)/shard_map/ppermute | solution.py:306
  62.2 1.2 %collective-permute-start.5 = (bf16[8,4,16,256]{3,2,1,0:T(8,128)(2,1)S(1)}, bf16[8,4,16,256]{3,2,1,0:T(8,128)(2,1)S(1)}, u32[]{:S(2)}, u32[]{:S(2)}) collective-permute-start(bf16[8,4,16,256]{3,2,1,0:T(8,128)(2,1)S(1)} %get-tuple-element.31), channel_id=1, source_target_pairs={{0,3},{1,2},{2,1},{3,0},{4,7},{5,6},{6,5},{7,4},{8,11},{9,10},{10,... | collective-permute-start | bytes 786440 | tf_op jit(solution)/shard_map/ppermute | solution.py:306
  63.4 5.1 %collective-permute-done.8.refs_4_ = bf16[4,8,16,256]{3,2,1,0:T(8,128)(2,1)S(1)} collective-permute-done((bf16[4,8,16,256]{3,2,1,0:T(8,128)(2,1)S(1)}, bf16[4,8,16,256]{3,2,1,0:T(8,128)(2,1)S(1)}, u32[]{:S(2)}, u32[]{:S(2)}) %collective-permute-start.8) | collective-permute-done | bytes 262176 | tf_op jit(solution)/shard_map/ppermute | solution.py:306
  68.5 1.4 %collective-permute-start = (bf16[8,4,16,256]{3,2,1,0:T(8,128)(2,1)S(1)}, bf16[8,4,16,256]{3,2,1,0:T(8,128)(2,1)S(1)}, u32[]{:S(2)}, u32[]{:S(2)}) collective-permute-start(bf16[8,4,16,256]{3,2,1,0:T(8,128)(2,1)S(1)} %get-tuple-element.25), channel_id=1, source_target_pairs={{0,1},{1,0},{2,3},{3,2},{4,5},{5,4},{6,7},{7,6},{8,9},{9,8},{10,11... | collective-permute-start | bytes 786440 | tf_op jit(solution)/shard_map/ppermute | solution.py:306
  70.9 5.5 %spectra.4 = (f32[8192,128]{1,0:T(8,128)}, f32[8192,128]{1,0:T(8,128)}) custom-call(bf16[4,8,16,256]{3,2,1,0:T(8,128)(2,1)S(1)} %get-tuple-element.34.refs_0_, bf16[4,8,16,256]{3,2,1,0:T(8,128)(2,1)S(1)} %get-tuple-element.35.refs_1_, bf16[4,8,16,256]{3,2,1,0:T(8,128)(2,1)S(1)} %collective-permute-done.6.refs_2_, ...), custom_call_target="tpu_custom_call" | custom-call | flops 8000000000 | bytes 8388608 | tf_op jit(solution)/shard_map/spectra/pallas_call | solution.py:206
  76.4 1.1 %collective-permute-start.2 = (bf16[8,4,16,256]{3,2,1,0:T(8,128)(2,1)S(1)}, bf16[8,4,16,256]{3,2,1,0:T(8,128)(2,1)S(1)}, u32[]{:S(2)}, u32[]{:S(2)}) collective-permute-start(bf16[8,4,16,256]{3,2,1,0:T(8,128)(2,1)S(1)} %get-tuple-element.27), channel_id=1, source_target_pairs={{0,3},{1,2},{2,1},{3,0},{4,7},{5,6},{6,5},{7,4},{8,11},{9,10},{10,... | collective-permute-start | bytes 786440 | tf_op jit(solution)/shard_map/ppermute | solution.py:306
  77.5 2.3 %collective-permute-done.4.refs_2_ = bf16[8,4,16,256]{3,2,1,0:T(8,128)(2,1)S(1)} collective-permute-done((bf16[8,4,16,256]{3,2,1,0:T(8,128)(2,1)S(1)}, bf16[8,4,16,256]{3,2,1,0:T(8,128)(2,1)S(1)}, u32[]{:S(2)}, u32[]{:S(2)}) %collective-permute-start.4) | collective-permute-done | bytes 262176 | tf_op jit(solution)/shard_map/ppermute | solution.py:306
  79.7 2.0 %spectra.3 = (f32[4,256,256]{2,1,0:T(8,128)S(1)}, f32[4,256,256]{2,1,0:T(8,128)S(1)}) custom-call(bf16[8,4,16,256]{3,2,1,0:T(8,128)(2,1)S(1)} %get-tuple-element.28.refs_0_, bf16[8,4,16,256]{3,2,1,0:T(8,128)(2,1)S(1)} %collective-permute-done.3.refs_1_, bf16[8,4,16,256]{3,2,1,0:T(8,128)(2,1)S(1)} %collective-permute-done.4.refs_2_, ...), custom_call_target="tpu_custom_call" | custom-call | flops 4000000000 | bytes 4194304 | tf_op jit(solution)/shard_map/spectra/pallas_call | solution.py:206
  81.8 2.9 %collective-permute-done.refs_1_ = bf16[8,4,16,256]{3,2,1,0:T(8,128)(2,1)S(1)} collective-permute-done((bf16[8,4,16,256]{3,2,1,0:T(8,128)(2,1)S(1)}, bf16[8,4,16,256]{3,2,1,0:T(8,128)(2,1)S(1)}, u32[]{:S(2)}, u32[]{:S(2)}) %collective-permute-start) | collective-permute-done | bytes 262176 | tf_op jit(solution)/shard_map/ppermute | solution.py:306
  84.7 5.8 %collective-permute-done.1.refs_2_ = bf16[8,4,16,256]{3,2,1,0:T(8,128)(2,1)S(1)} collective-permute-done((bf16[8,4,16,256]{3,2,1,0:T(8,128)(2,1)S(1)}, bf16[8,4,16,256]{3,2,1,0:T(8,128)(2,1)S(1)}, u32[]{:S(2)}, u32[]{:S(2)}) %collective-permute-start.1) | collective-permute-done | bytes 262176 | tf_op jit(solution)/shard_map/ppermute | solution.py:306
  90.5 4.5 %spectra.5 = (f32[8192,128]{1,0:T(8,128)}, f32[8192,128]{1,0:T(8,128)}) custom-call(bf16[8,4,16,256]{3,2,1,0:T(8,128)(2,1)S(1)} %get-tuple-element.24.refs_0_, bf16[8,4,16,256]{3,2,1,0:T(8,128)(2,1)S(1)} %collective-permute-done.refs_1_, bf16[8,4,16,256]{3,2,1,0:T(8,128)(2,1)S(1)} %collective-permute-done.1.refs_2_, ...), custom_call_target="tpu_custom_call", output_to_operand_aliasing={{0}: (12, {}), {1}: (13, {})} | custom-call | flops 4000000000 | bytes 4194304 | tf_op jit(solution)/shard_map/spectra/pallas_call | solution.py:206
  (42 shorter events, 8.5 us)
Async XLA Ops:
  0.6 15.6 %copy-start.3 = (f32[65536]{0:T(1024)S(1)}, f32[65536]{0:T(1024)}, u32[]{:S(2)}) copy-start(f32[65536]{0:T(1024)} %param.9) | copy-start | bytes 786436
  0.6 16.6 %copy-start.4 = (s32[64,64]{1,0:T(8,128)S(1)}, s32[64,64]{1,0:T(8,128)}, u32[]{:S(2)}) copy-start(s32[64,64]{1,0:T(8,128)} %param.8) | copy-start | bytes 49156
  4.0 36.4 %all-to-all-start = ((bf16[32,16,2048]{2,1,0:T(8,128)(2,1)}), bf16[32,16,2048]{2,1,0:T(8,128)(2,1)S(1)}, u32[]{:S(2)}, u32[]{:S(2)}) async-start(bf16[32,16,2048]{2,1,0:T(8,128)(2,1)} %regroup.1), calls=%async_computation | async-start | bytes 4194304 | tf_op jit(solution)/shard_map/all_to_all | solution.py:279
  41.6 9.2 %collective-permute-start.7 = (bf16[4,8,16,256]{3,2,1,0:T(8,128)(2,1)S(1)}, bf16[4,8,16,256]{3,2,1,0:T(8,128)(2,1)S(1)}, u32[]{:S(2)}, u32[]{:S(2)}) collective-permute-start(bf16[4,8,16,256]{3,2,1,0:T(8,128)(2,1)S(1)} %get-tuple-element.37), channel_id=1, source_target_pairs={{0,1},{1,0},{2,3},{3,2},{4,5},{5,4},{6,7},{7,6},{8,9},{9,8},{10,11... | collective-permute-start | bytes 786440 | tf_op jit(solution)/shard_map/ppermute | solution.py:306
  42.5 14.8 %collective-permute-start.9 = (bf16[4,8,16,256]{3,2,1,0:T(8,128)(2,1)S(1)}, bf16[4,8,16,256]{3,2,1,0:T(8,128)(2,1)S(1)}, u32[]{:S(2)}, u32[]{:S(2)}) collective-permute-start(bf16[4,8,16,256]{3,2,1,0:T(8,128)(2,1)S(1)} %get-tuple-element.39), channel_id=1, source_target_pairs={{0,2},{1,3},{2,0},{3,1},{4,6},{5,7},{6,4},{7,5},{8,10},{9,11},{10,... | collective-permute-start | bytes 786440 | tf_op jit(solution)/shard_map/ppermute | solution.py:306
  43.6 15.1 %collective-permute-start.11 = (bf16[4,8,16,256]{3,2,1,0:T(8,128)(2,1)S(1)}, bf16[4,8,16,256]{3,2,1,0:T(8,128)(2,1)S(1)}, u32[]{:S(2)}, u32[]{:S(2)}) collective-permute-start(bf16[4,8,16,256]{3,2,1,0:T(8,128)(2,1)S(1)} %get-tuple-element.41), channel_id=1, source_target_pairs={{0,3},{1,2},{2,1},{3,0},{4,7},{5,6},{6,5},{7,4},{8,11},{9,10},{10,... | collective-permute-start | bytes 786440 | tf_op jit(solution)/shard_map/ppermute | solution.py:306
  46.5 15.6 %collective-permute-start.6 = (bf16[4,8,16,256]{3,2,1,0:T(8,128)(2,1)S(1)}, bf16[4,8,16,256]{3,2,1,0:T(8,128)(2,1)S(1)}, u32[]{:S(2)}, u32[]{:S(2)}) collective-permute-start(bf16[4,8,16,256]{3,2,1,0:T(8,128)(2,1)S(1)} %get-tuple-element.36), channel_id=1, source_target_pairs={{0,1},{1,0},{2,3},{3,2},{4,5},{5,4},{6,7},{7,6},{8,9},{9,8},{10,11... | collective-permute-start | bytes 786440 | tf_op jit(solution)/shard_map/ppermute | solution.py:306
  47.4 21.1 %collective-permute-start.8 = (bf16[4,8,16,256]{3,2,1,0:T(8,128)(2,1)S(1)}, bf16[4,8,16,256]{3,2,1,0:T(8,128)(2,1)S(1)}, u32[]{:S(2)}, u32[]{:S(2)}) collective-permute-start(bf16[4,8,16,256]{3,2,1,0:T(8,128)(2,1)S(1)} %get-tuple-element.38), channel_id=1, source_target_pairs={{0,2},{1,3},{2,0},{3,1},{4,6},{5,7},{6,4},{7,5},{8,10},{9,11},{10,... | collective-permute-start | bytes 786440 | tf_op jit(solution)/shard_map/ppermute | solution.py:306
  50.9 19.0 %collective-permute-start.10 = (bf16[4,8,16,256]{3,2,1,0:T(8,128)(2,1)S(1)}, bf16[4,8,16,256]{3,2,1,0:T(8,128)(2,1)S(1)}, u32[]{:S(2)}, u32[]{:S(2)}) collective-permute-start(bf16[4,8,16,256]{3,2,1,0:T(8,128)(2,1)S(1)} %get-tuple-element.40), channel_id=1, source_target_pairs={{0,3},{1,2},{2,1},{3,0},{4,7},{5,6},{6,5},{7,4},{8,11},{9,10},{10,... | collective-permute-start | bytes 786440 | tf_op jit(solution)/shard_map/ppermute | solution.py:306
  54.1 16.8 %copy-start = (bf16[2,256,512]{2,1,0:T(8,128)(2,1)S(1)}, bf16[2,256,512]{2,1,0:T(8,128)(2,1)}, u32[]{:S(2)}) copy-start(bf16[2,256,512]{2,1,0:T(8,128)(2,1)} %constant.72.clone.refs_7_.refs_11_) | copy-start | bytes 1572868
  54.1 16.8 %copy-start.1 = (f32[256,256]{1,0:T(8,128)S(1)}, f32[256,256]{1,0:T(8,128)}, u32[]{:S(2)}) copy-start(f32[256,256]{1,0:T(8,128)} %constant.71.clone.refs_6_.refs_10_) | copy-start | bytes 786436
  54.2 16.8 %copy-start.2 = (f32[256,256]{1,0:T(8,128)S(1)}, f32[256,256]{1,0:T(8,128)}, u32[]{:S(2)}) copy-start(f32[256,256]{1,0:T(8,128)} %constant.70.clone.refs_5_.refs_9_) | copy-start | bytes 786436
  57.3 19.1 %collective-permute-start.3 = (bf16[8,4,16,256]{3,2,1,0:T(8,128)(2,1)S(1)}, bf16[8,4,16,256]{3,2,1,0:T(8,128)(2,1)S(1)}, u32[]{:S(2)}, u32[]{:S(2)}) collective-permute-start(bf16[8,4,16,256]{3,2,1,0:T(8,128)(2,1)S(1)} %get-tuple-element.29), channel_id=1, source_target_pairs={{0,1},{1,0},{2,3},{3,2},{4,5},{5,4},{6,7},{7,6},{8,9},{9,8},{10,11... | collective-permute-start | bytes 786440 | tf_op jit(solution)/shard_map/ppermute | solution.py:306
  58.7 21.1 %collective-permute-start.4 = (bf16[8,4,16,256]{3,2,1,0:T(8,128)(2,1)S(1)}, bf16[8,4,16,256]{3,2,1,0:T(8,128)(2,1)S(1)}, u32[]{:S(2)}, u32[]{:S(2)}) collective-permute-start(bf16[8,4,16,256]{3,2,1,0:T(8,128)(2,1)S(1)} %get-tuple-element.30), channel_id=1, source_target_pairs={{0,2},{1,3},{2,0},{3,1},{4,6},{5,7},{6,4},{7,5},{8,10},{9,11},{10,... | collective-permute-start | bytes 786440 | tf_op jit(solution)/shard_map/ppermute | solution.py:306
  62.2 17.6 %collective-permute-start.5 = (bf16[8,4,16,256]{3,2,1,0:T(8,128)(2,1)S(1)}, bf16[8,4,16,256]{3,2,1,0:T(8,128)(2,1)S(1)}, u32[]{:S(2)}, u32[]{:S(2)}) collective-permute-start(bf16[8,4,16,256]{3,2,1,0:T(8,128)(2,1)S(1)} %get-tuple-element.31), channel_id=1, source_target_pairs={{0,3},{1,2},{2,1},{3,0},{4,7},{5,6},{6,5},{7,4},{8,11},{9,10},{10,... | collective-permute-start | bytes 786440 | tf_op jit(solution)/shard_map/ppermute | solution.py:306
  68.5 16.2 %collective-permute-start = (bf16[8,4,16,256]{3,2,1,0:T(8,128)(2,1)S(1)}, bf16[8,4,16,256]{3,2,1,0:T(8,128)(2,1)S(1)}, u32[]{:S(2)}, u32[]{:S(2)}) collective-permute-start(bf16[8,4,16,256]{3,2,1,0:T(8,128)(2,1)S(1)} %get-tuple-element.25), channel_id=1, source_target_pairs={{0,1},{1,0},{2,3},{3,2},{4,5},{5,4},{6,7},{7,6},{8,9},{9,8},{10,11... | collective-permute-start | bytes 786440 | tf_op jit(solution)/shard_map/ppermute | solution.py:306
  69.9 20.6 %collective-permute-start.1 = (bf16[8,4,16,256]{3,2,1,0:T(8,128)(2,1)S(1)}, bf16[8,4,16,256]{3,2,1,0:T(8,128)(2,1)S(1)}, u32[]{:S(2)}, u32[]{:S(2)}) collective-permute-start(bf16[8,4,16,256]{3,2,1,0:T(8,128)(2,1)S(1)} %get-tuple-element.26), channel_id=1, source_target_pairs={{0,2},{1,3},{2,0},{3,1},{4,6},{5,7},{6,4},{7,5},{8,10},{9,11},{10,... | collective-permute-start | bytes 786440 | tf_op jit(solution)/shard_map/ppermute | solution.py:306
  76.4 14.2 %collective-permute-start.2 = (bf16[8,4,16,256]{3,2,1,0:T(8,128)(2,1)S(1)}, bf16[8,4,16,256]{3,2,1,0:T(8,128)(2,1)S(1)}, u32[]{:S(2)}, u32[]{:S(2)}) collective-permute-start(bf16[8,4,16,256]{3,2,1,0:T(8,128)(2,1)S(1)} %get-tuple-element.27), channel_id=1, source_target_pairs={{0,3},{1,2},{2,1},{3,0},{4,7},{5,6},{6,5},{7,4},{8,11},{9,10},{10,... | collective-permute-start | bytes 786440 | tf_op jit(solution)/shard_map/ppermute | solution.py:306
